TPU v7x, 128 devices: a whole 4x4x4 slice. The times are simulated.
128 devices in a mesh: gx: 8 (over z_hi, y), gy: 4 (over z_lo, core), gz: 4 (over x).
Axes of the slice: x: 4, y: 4, z: 4 (z_hi: 2, z_lo: 2; z = z_hi * 2 + z_lo), core: 2. Of those that a mesh axis runs over, the one named last changes fastest.
Arguments:
- positions: float32 [16, 8, 8, 3, 64], P('gx', 'gy', 'gz'), may hold values from 0 to 8
- velocity: float32 [16, 8, 8, 3, 64], P('gx', 'gy', 'gz'), may hold values from -6 to 6
- atom_embed: bfloat16 [16, 8, 8, 64, 256], P('gx', 'gy', 'gz'), may hold values from -6 to 6
- embed_proj: bfloat16 [256, 256], replicated, may hold values from -0.375 to 0.375
- radial_weight: bfloat16 [8, 256], replicated, may hold values from -2 to 2
- latent_bias: float32 [256], replicated, may hold values from -3 to 3
- energy_weight: bfloat16 [256], replicated, may hold values from -0.375 to 0.375
- block_list: int32 [128, 2, 32], P(('gx', 'gy', 'gz')), may hold values from 0 to 13, as said below
- block_count: int32 [128], P(('gx', 'gy', 'gz')), may hold values from 8 to 32, as said below
- move_slot: int32 [128, 128], P(('gx', 'gy', 'gz')), may hold values from 0 to 511, as said below
- move_dest: int32 [16384, 1], P(('gx', 'gy', 'gz')), may hold values from 0 to 127; in each aligned block of 128 rows (0 to 127, 128 to 255, ...) at most 2 rows name the same one
Outputs:
- forces: float32 [16, 8, 8, 3, 64], P('gx', 'gy', 'gz')
- arrived_motion: float32 [16384, 2, 6], P(('gx', 'gy', 'gz'))
- arrived_embed: bfloat16 [16384, 2, 256], P(('gx', 'gy', 'gz'))
Inputs may be any that keep to these rules, and one draw needn't show every extreme that they name: `block_list`: row 0 names a local cell below 8, row 1 an offset code below 14; no (cell, code) pair repeats within one device's list. `block_count`: some device has all 32 blocks live. `move_slot`: the slots of one device are distinct. `move_dest`: among the rows of one device at most 2 name the same owner.
All inputs are finite; a program needn't handle non-finite values.
Results may differ from a plain program's by a relative error of at most 0.0095.
Values may be sent and summed in bfloat16 or wider, within the bound.
A program may use at most 64 MiB of HBM per device.

v0:
```python
import jax
import jax.numpy as jnp
import numpy as np
from jax import lax
from jax.sharding import PartitionSpec as P

MOVE_CAP = 2


CELL_EDGE = 8.0
CUTOFF = 6.0
SOFTEN = 0.25
STEP = 0.5
OFFSET_TABLE = np.array(
    [
        [0, 0, 0],
        [1, 0, 0],
        [0, 1, 0],
        [0, 0, 1],
        [1, 1, 0],
        [1, 0, 1],
        [0, 1, 1],
        [1, 1, 1],
        [1, 1, -1],
        [1, -1, 1],
        [-1, 1, 1],
        [1, -1, 0],
        [1, 0, -1],
        [0, 1, -1],
    ],
    dtype=np.int32,
)


def padded(value, sides, width):
    for axis, dim in sides:
        size, length = (lax.axis_size(axis), value.shape[dim])
        up = [(i, (i + 1) % size) for i in range(size)]
        down = [(j, i) for i, j in up]
        last = lax.slice_in_dim(value, length - width, length, axis=dim)
        initial = lax.slice_in_dim(value, 0, width, axis=dim)
        before = lax.ppermute(last, axis, up)
        after = lax.ppermute(initial, axis, down)
        value = jnp.concatenate([before, value, after], axis=dim)
    return value


def block_energy(
    coords_a,
    coords_b,
    latent_a,
    latent_b,
    shifts,
    offset_code,
    weights,
    radial_weight,
    latent_bias,
    energy_weight,
):
    separation = coords_b[:, :, None, :] + shifts[:, :, None, None] - coords_a[:, :, :, None]
    scaled_dist = jnp.sqrt(jnp.sum(separation * separation, axis=1) + SOFTEN) / CUTOFF
    envelope = jnp.where(scaled_dist < 1.0, jnp.square(1.0 - scaled_dist * scaled_dist), 0.0)
    orders = jnp.arange(1, radial_weight.shape[0] + 1).astype(jnp.float32)
    radial_basis = jnp.sin(jnp.pi * scaled_dist[..., None] * orders).astype(jnp.bfloat16)
    preact = jnp.einsum(
        "gijn,nl->gijl", radial_basis, radial_weight, preferred_element_type=jnp.float32
    )
    preact = (
        preact
        + latent_a.astype(jnp.float32)[:, :, None, :]
        + latent_b.astype(jnp.float32)[:, None, :, :]
        + latent_bias
    )
    hidden = jax.nn.silu(preact).astype(jnp.bfloat16)
    pair_energy = (
        jnp.einsum("gijl,l->gij", hidden, energy_weight, preferred_element_type=jnp.float32)
        * envelope
    )
    slot_count = coords_a.shape[2]
    upper_mask = (jnp.arange(slot_count)[:, None] < jnp.arange(slot_count)[None, :]).astype(
        jnp.float32
    )
    keep_mask = (
        jnp.where((offset_code == 0)[:, None, None], upper_mask, 1.0) * weights[:, None, None]
    )
    return jnp.sum(pair_energy * keep_mask)


def project_rows(embed, embed_proj):
    shape_in = embed.shape
    product = jnp.dot(
        embed.reshape(-1, shape_in[-1]), embed_proj, preferred_element_type=jnp.float32
    )
    return product.astype(jnp.bfloat16).reshape(shape_in)


def fold_rim(gathered, axis_dim, span):
    core_part = lax.slice_in_dim(gathered, 2, span + 2, axis=axis_dim)
    lower_rim = lax.slice_in_dim(gathered, 0, 1, axis=axis_dim)
    upper_rim = lax.slice_in_dim(gathered, span + 3, span + 4, axis=axis_dim)
    low_pad = [(0, 0)] * gathered.ndim
    high_pad = [(0, 0)] * gathered.ndim
    low_pad[axis_dim] = (0, span - 1)
    high_pad[axis_dim] = (span - 1, 0)
    return core_part + jnp.pad(lower_rim, low_pad) + jnp.pad(upper_rim, high_pad)


def per_device(
    positions,
    velocity,
    atom_embed,
    embed_proj,
    radial_weight,
    latent_bias,
    energy_weight,
    block_list,
    block_count,
    move_slot,
    move_dest,
):
    span_x, span_y, span_z = (positions.shape[0], positions.shape[1], positions.shape[2])
    cell_atoms = positions.shape[4]
    latent_width = atom_embed.shape[4]
    padded_coords = padded(positions, (("gx", 0), ("gy", 1), ("gz", 2)), 1)
    arriving = padded(atom_embed, (("gx", 0), ("gy", 1), ("gz", 2)), 1)
    latent = project_rows(arriving, embed_proj)
    extent_y = span_y + 2
    extent_z = span_z + 2
    padded_cells = (span_x + 2) * extent_y * extent_z
    flat_coords = padded_coords.reshape(padded_cells, 3, cell_atoms)
    flat_latent = latent.reshape(padded_cells, cell_atoms, latent_width)
    owned_cell = block_list[0, 0]
    offset_code = block_list[0, 1]
    one_hot = (offset_code[:, None] == jnp.arange(14)[None, :]).astype(jnp.int32)
    offsets = jnp.sum(one_hot[:, :, None] * jnp.asarray(OFFSET_TABLE)[None, :, :], axis=1)
    local_x = owned_cell // (span_y * span_z) + 1
    local_y = owned_cell // span_z % span_y + 1
    local_z = owned_cell % span_z + 1
    first_cell = (local_x * extent_y + local_y) * extent_z + local_z
    second_cell = (
        ((local_x + offsets[:, 0]) * extent_y + local_y + offsets[:, 1]) * extent_z
        + local_z
        + offsets[:, 2]
    )
    shifts = offsets.astype(jnp.float32) * CELL_EDGE
    live_blocks = block_count[0]
    per_turn = 4
    group_count = (live_blocks + per_turn - 1) // per_turn

    def visit_group(turn_index, force_sum):
        first_block = turn_index * per_turn
        pick_first = lax.dynamic_slice_in_dim(first_cell, first_block, per_turn)
        pick_second = lax.dynamic_slice_in_dim(second_cell, first_block, per_turn)
        pick_code = lax.dynamic_slice_in_dim(offset_code, first_block, per_turn)
        pick_shift = lax.dynamic_slice_in_dim(shifts, first_block, per_turn)
        pick_weight = (first_block + jnp.arange(per_turn) < live_blocks).astype(jnp.float32)
        grad_a, grad_b = jax.grad(block_energy, argnums=(0, 1))(
            flat_coords[pick_first],
            flat_coords[pick_second],
            flat_latent[pick_first],
            flat_latent[pick_second],
            pick_shift,
            pick_code,
            pick_weight,
            radial_weight,
            latent_bias,
            energy_weight,
        )
        return force_sum.at[pick_first].add(-grad_a).at[pick_second].add(-grad_b)

    force_sum = lax.fori_loop(
        0, group_count, visit_group, jnp.zeros((padded_cells, 3, cell_atoms), jnp.float32)
    )
    padded_force = force_sum.reshape(span_x + 2, extent_y, extent_z, 3, cell_atoms)
    gathered = padded(
        padded_force.astype(jnp.bfloat16), (("gx", 0), ("gy", 1), ("gz", 2)), 1
    ).astype(padded_force.dtype)
    forces = fold_rim(fold_rim(fold_rim(gathered, 0, span_x), 1, span_y), 2, span_z)
    new_velocity = velocity + STEP * forces
    new_position = positions + STEP * new_velocity
    motion = jnp.concatenate([new_position, new_velocity], axis=3).reshape(-1, 6, cell_atoms)
    slot_list = move_slot[0]
    moving_motion = motion[slot_list // cell_atoms, :, slot_list % cell_atoms]
    moving_embed = atom_embed.reshape(-1, latent_width)[slot_list].astype(jnp.float32)
    target = move_dest[:, 0]
    device_total = lax.axis_size(("gx", "gy", "gz"))
    row_index = jnp.arange(target.shape[0])
    earlier = (target[:, None] == target[None, :]) & (row_index[None, :] < row_index[:, None])
    ranking = jnp.sum(earlier.astype(jnp.int32), axis=1)
    place_index = target * MOVE_CAP + ranking
    send_motion = (
        jnp.zeros((device_total * MOVE_CAP, 6), jnp.float32)
        .at[place_index]
        .set(moving_motion)
        .reshape(device_total, MOVE_CAP, 6)
    )
    send_embed = (
        jnp.zeros((device_total * MOVE_CAP, latent_width), jnp.float32)
        .at[place_index]
        .set(moving_embed)
        .reshape(device_total, MOVE_CAP, latent_width)
    )
    got_embed, got_motion = (
        lax.all_to_all(
            send_embed.astype(jnp.bfloat16),
            ("gx", "gy", "gz"),
            split_axis=0,
            concat_axis=0,
            tiled=True,
        ).astype(send_embed.dtype),
        lax.all_to_all(
            send_motion.astype(jnp.bfloat16),
            ("gx", "gy", "gz"),
            split_axis=0,
            concat_axis=0,
            tiled=True,
        ).astype(send_motion.dtype),
    )
    return (forces, got_motion, got_embed.astype(jnp.bfloat16))


def solution(mesh):
    placed = (
        P("gx", "gy", "gz", None, None),
        P("gx", "gy", "gz", None, None),
        P("gx", "gy", "gz", None, None),
        P(),
        P(),
        P(),
        P(),
        P(("gx", "gy", "gz"), None, None),
        P(("gx", "gy", "gz")),
        P(("gx", "gy", "gz"), None),
        P(("gx", "gy", "gz"), None),
    )
    return jax.shard_map(
        per_device,
        mesh=mesh,
        in_specs=placed,
        out_specs=(
            P("gx", "gy", "gz", None, None),
            P(("gx", "gy", "gz"), None, None),
            P(("gx", "gy", "gz"), None, None),
        ),
        check_vma=False,
    )
```

profile of v0, /device:TPU:1, one launch (start us, length us, event | category | flops | bytes accessed | tf_op | source)
XLA Modules:
  0.0 387.7 jit_solution(10378720803981110543)
XLA Ops:
  1.7 2.2 collective-permute-start.6
  3.9 4.8 %collective-permute-start.7 = (bf16[1,2,2,64,256]{4,3,2,1,0:T(8,128)(2,1)S(1)}, bf16[1,2,2,64,256]{4,3,2,1,0:T(8,128)(2,1)S(1)}, u32[]{:S(2)}, u32[]{:S(2)}) collective-permute-start(bf16[1,2,2,64,256]{4,3,2,1,0:T(8,128)(2,1)S(1)} %get-tuple-element.232), channel_id=1, source_target_pairs={{16,0},{32,16},{48,32},{64,48},{80,64},{96,80},{112,96},{0,112},{1... | collective-permute-start | bytes 393224 | tf_op jit(solution)/shard_map/ppermute | solution.py:43
  9.5 5.1 %collective-permute-start.1 = (f32[1,2,2,3,64]{4,2,3,1,0:T(2,128)S(1)}, f32[1,2,2,3,64]{4,2,3,1,0:T(2,128)S(1)}, u32[]{:S(2)}, u32[]{:S(2)}) collective-permute-start(f32[1,2,2,3,64]{4,2,3,1,0:T(2,128)S(1)} %get-tuple-element.244), channel_id=1, source_target_pairs={{16,0},{32,16},{48,32},{64,48},{80,64},{96,80},{112,96},{0,112},{1... | collective-permute-start | bytes 9224 | tf_op jit(solution)/shard_map/ppermute | solution.py:43
  17.5 2.3 collective-permute-start.2
  20.9 1.8 collective-permute-start.8
  23.0 4.7 %collective-permute-done.8 = bf16[4,1,2,64,256]{4,3,2,1,0:T(8,128)(2,1)S(1)} collective-permute-done((bf16[4,1,2,64,256]{4,3,2,1,0:T(8,128)(2,1)S(1)}, bf16[4,1,2,64,256]{4,3,2,1,0:T(8,128)(2,1)S(1)}, u32[]{:S(2)}, u32[]{:S(2)}) %collective-permute-start.8) | collective-permute-done | bytes 262176 | tf_op jit(solution)/shard_map/ppermute | solution.py:42
  27.6 2.2 collective-permute-done.9
  32.9 2.7 collective-permute-start.5
  36.3 9.2 %collective-permute-done.4 = f32[4,4,1,3,64]{4,2,3,1,0:T(1,128)S(1)} collective-permute-done((f32[4,4,1,3,64]{4,2,3,1,0:T(1,128)S(1)}, f32[4,4,1,3,64]{4,2,3,1,0:T(1,128)S(1)}, u32[]{:S(2)}, u32[]{:S(2)}) %collective-permute-start.4) | collective-permute-done | bytes 12320 | tf_op jit(solution)/shard_map/ppermute | solution.py:42
  47.6 145.0 %while.12 = (s32[]{:T(128)}, f32[64,3,64]{2,1,0:T(4,128)S(1)}, s32[]{:T(128)}, s32[32]{0:T(128)S(1)}, s32[32]{0:T(128)S(1)}, /*index=5*/f32[64,3,64]{2,1,0:T(4,1...) while((s32[]{:T(128)}, f32[64,3,64]{2,1,0:T(4,128)S(1)}, ...), condition=%wide.region_8.9_spmd, body=%wide.region_1.8_spmd.sunk | while | flops 241119040 | bytes 120851280 | solution.py:171
  47.9 1.5 gather_fusion.1
  52.2 8.6 %fusion.108 = f32[4,64,64,256]{3,2,1,0:T(8,128)} fusion(f32[8]{0:T(128)S(1)} %add_convert_fusion.2, f32[4,64,64]{2,1,0:T(8,128)S(1)} %get-tuple-element.341, bf16[8,256]{1,0:T(8,128)(2,1)S(1)} %get-tuple-element.389), kind=kOutput, calls=%fused_computation.37.clone.1 | convolution fusion | flops 67371008 | bytes 16846880 | tf_op jit(solution)/shard_map/while/body/jvp(gijn,nl->gijl)/dot_general | solution.py:65
  62.0 15.0 %fusion.110 = f32[4,64,64]{2,1,0:T(8,128)S(1)} fusion(f32[4,64,64,256]{3,2,1,0:T(8,128)} %fusion.108, f32[256]{0:T(256)S(1)} %get-tuple-element.391, f32[4,64,256]{2,1,0:T(8,128)S(1)} %convert_element_type.249, f32[4,64,256]{2,1,0:T(8,128)S(1)} %convert_element_type.250, f32[256]{0:T(256)S(1)} %convert.21, f32[4,64,64]{2,1,0:T(8,128)S(1)} %get-tuple-element.342, ...), kind=kOutput, calls=%fused_computation.33.clone.1 | convolution fusion | flops 130793472 | bytes 17504288 | tf_op jit(solution)/shard_map/while/body/transpose(jvp(gijn,nl->gijl))/dot_general | solution.py:65
  77.0 5.2 %fusion.109 = f32[1,4,64,64]{3,0,2,1:T(1,128)S(1)} fusion(f32[4,64,64,256]{3,2,1,0:T(8,128)S(1)} %copy-done.1, f32[256]{0:T(256)S(1)} %get-tuple-element.391, f32[4,64,256]{2,1,0:T(8,128)S(1)} %convert_element_type.249, f32[4,64,256]{2,1,0:T(8,128)S(1)} %convert_element_type.250, bf16[256,1,1,1]{0,1,2,3:T(2,128)(2,1)S(1)} %reshape.375), kind=kOutput, calls=%fused_computation.26.clone.1 | convolution fusion | flops 41943040 | bytes 17368576 | tf_op jit(solution)/shard_map/while/body/jvp(gijl,l->gij)/dot_general | solution.py:76
  88.4 8.6 %fusion.108 = f32[4,64,64,256]{3,2,1,0:T(8,128)} fusion(f32[8]{0:T(128)S(1)} %add_convert_fusion.2, f32[4,64,64]{2,1,0:T(8,128)S(1)} %get-tuple-element.341, bf16[8,256]{1,0:T(8,128)(2,1)S(1)} %get-tuple-element.389), kind=kOutput, calls=%fused_computation.37.clone.1 | convolution fusion | flops 67371008 | bytes 16846880 | tf_op jit(solution)/shard_map/while/body/jvp(gijn,nl->gijl)/dot_general | solution.py:65
  98.2 15.0 %fusion.110 = f32[4,64,64]{2,1,0:T(8,128)S(1)} fusion(f32[4,64,64,256]{3,2,1,0:T(8,128)} %fusion.108, f32[256]{0:T(256)S(1)} %get-tuple-element.391, f32[4,64,256]{2,1,0:T(8,128)S(1)} %convert_element_type.249, f32[4,64,256]{2,1,0:T(8,128)S(1)} %convert_element_type.250, f32[256]{0:T(256)S(1)} %convert.21, f32[4,64,64]{2,1,0:T(8,128)S(1)} %get-tuple-element.342, ...), kind=kOutput, calls=%fused_computation.33.clone.1 | convolution fusion | flops 130793472 | bytes 17504288 | tf_op jit(solution)/shard_map/while/body/transpose(jvp(gijn,nl->gijl))/dot_general | solution.py:65
  113.2 5.2 %fusion.109 = f32[1,4,64,64]{3,0,2,1:T(1,128)S(1)} fusion(f32[4,64,64,256]{3,2,1,0:T(8,128)S(1)} %copy-done.1, f32[256]{0:T(256)S(1)} %get-tuple-element.391, f32[4,64,256]{2,1,0:T(8,128)S(1)} %convert_element_type.249, f32[4,64,256]{2,1,0:T(8,128)S(1)} %convert_element_type.250, bf16[256,1,1,1]{0,1,2,3:T(2,128)(2,1)S(1)} %reshape.375), kind=kOutput, calls=%fused_computation.26.clone.1 | convolution fusion | flops 41943040 | bytes 17368576 | tf_op jit(solution)/shard_map/while/body/jvp(gijl,l->gij)/dot_general | solution.py:76
  124.5 8.6 %fusion.108 = f32[4,64,64,256]{3,2,1,0:T(8,128)} fusion(f32[8]{0:T(128)S(1)} %add_convert_fusion.2, f32[4,64,64]{2,1,0:T(8,128)S(1)} %get-tuple-element.341, bf16[8,256]{1,0:T(8,128)(2,1)S(1)} %get-tuple-element.389), kind=kOutput, calls=%fused_computation.37.clone.1 | convolution fusion | flops 67371008 | bytes 16846880 | tf_op jit(solution)/shard_map/while/body/jvp(gijn,nl->gijl)/dot_general | solution.py:65
  134.4 15.0 %fusion.110 = f32[4,64,64]{2,1,0:T(8,128)S(1)} fusion(f32[4,64,64,256]{3,2,1,0:T(8,128)} %fusion.108, f32[256]{0:T(256)S(1)} %get-tuple-element.391, f32[4,64,256]{2,1,0:T(8,128)S(1)} %convert_element_type.249, f32[4,64,256]{2,1,0:T(8,128)S(1)} %convert_element_type.250, f32[256]{0:T(256)S(1)} %convert.21, f32[4,64,64]{2,1,0:T(8,128)S(1)} %get-tuple-element.342, ...), kind=kOutput, calls=%fused_computation.33.clone.1 | convolution fusion | flops 130793472 | bytes 17504288 | tf_op jit(solution)/shard_map/while/body/transpose(jvp(gijn,nl->gijl))/dot_general | solution.py:65
  149.4 5.2 %fusion.109 = f32[1,4,64,64]{3,0,2,1:T(1,128)S(1)} fusion(f32[4,64,64,256]{3,2,1,0:T(8,128)S(1)} %copy-done.1, f32[256]{0:T(256)S(1)} %get-tuple-element.391, f32[4,64,256]{2,1,0:T(8,128)S(1)} %convert_element_type.249, f32[4,64,256]{2,1,0:T(8,128)S(1)} %convert_element_type.250, bf16[256,1,1,1]{0,1,2,3:T(2,128)(2,1)S(1)} %reshape.375), kind=kOutput, calls=%fused_computation.26.clone.1 | convolution fusion | flops 41943040 | bytes 17368576 | tf_op jit(solution)/shard_map/while/body/jvp(gijl,l->gij)/dot_general | solution.py:76
  160.7 8.6 %fusion.108 = f32[4,64,64,256]{3,2,1,0:T(8,128)} fusion(f32[8]{0:T(128)S(1)} %add_convert_fusion.2, f32[4,64,64]{2,1,0:T(8,128)S(1)} %get-tuple-element.341, bf16[8,256]{1,0:T(8,128)(2,1)S(1)} %get-tuple-element.389), kind=kOutput, calls=%fused_computation.37.clone.1 | convolution fusion | flops 67371008 | bytes 16846880 | tf_op jit(solution)/shard_map/while/body/jvp(gijn,nl->gijl)/dot_general | solution.py:65
  170.5 15.0 %fusion.110 = f32[4,64,64]{2,1,0:T(8,128)S(1)} fusion(f32[4,64,64,256]{3,2,1,0:T(8,128)} %fusion.108, f32[256]{0:T(256)S(1)} %get-tuple-element.391, f32[4,64,256]{2,1,0:T(8,128)S(1)} %convert_element_type.249, f32[4,64,256]{2,1,0:T(8,128)S(1)} %convert_element_type.250, f32[256]{0:T(256)S(1)} %convert.21, f32[4,64,64]{2,1,0:T(8,128)S(1)} %get-tuple-element.342, ...), kind=kOutput, calls=%fused_computation.33.clone.1 | convolution fusion | flops 130793472 | bytes 17504288 | tf_op jit(solution)/shard_map/while/body/transpose(jvp(gijn,nl->gijl))/dot_general | solution.py:65
  185.6 5.2 %fusion.109 = f32[1,4,64,64]{3,0,2,1:T(1,128)S(1)} fusion(f32[4,64,64,256]{3,2,1,0:T(8,128)S(1)} %copy-done.1, f32[256]{0:T(256)S(1)} %get-tuple-element.391, f32[4,64,256]{2,1,0:T(8,128)S(1)} %convert_element_type.249, f32[4,64,256]{2,1,0:T(8,128)S(1)} %convert_element_type.250, bf16[256,1,1,1]{0,1,2,3:T(2,128)(2,1)S(1)} %reshape.375), kind=kOutput, calls=%fused_computation.26.clone.1 | convolution fusion | flops 41943040 | bytes 17368576 | tf_op jit(solution)/shard_map/while/body/jvp(gijl,l->gij)/dot_general | solution.py:76
  192.7 148.6 %collective-permute-start.13 = (bf16[1,4,4,3,64]{4,2,1,0,3:T(4,128)(2,1)S(1)}, bf16[1,4,4,3,64]{4,2,1,0,3:T(4,128)(2,1)S(1)}, u32[]{:S(2)}, u32[]{:S(2)}) collective-permute-start(bf16[1,4,4,3,64]{4,2,1,0,3:T(4,128)(2,1)S(1)} %bitcast.119), channel_id=1, source_target_pairs={{16,0},{32,16},{48,32},{64,48},{80,64},{96,80},{112,96},{0,112},{1... | collective-permute-start | bytes 18440 | tf_op jit(solution)/shard_map/ppermute | solution.py:43
  343.6 2.1 collective-permute-done.15
  345.9 2.6 collective-permute-start.16
  348.5 2.6 collective-permute-start.17
  353.3 9.2 %all-to-all-start.1 = ((bf16[128,2,256]{2,1,0:T(2,128)(2,1)}), bf16[128,2,256]{2,1,0:T(2,128)(2,1)S(1)}, u32[]{:S(2)}, u32[]{:S(2)}) async-start(bf16[128,2,256]{2,1,0:T(2,128)(2,1)} %convert_element_type.153), calls=%async_computation.1 | async-start | bytes 262144 | tf_op jit(solution)/shard_map/all_to_all | solution.py:204
  363.3 1.6 scatter_custom_fusion.2
  365.5 7.0 %all-to-all-done.1 = bf16[128,2,256]{2,1,0:T(2,128)(2,1)S(1)} async-done(((bf16[128,2,256]{2,1,0:T(2,128)(2,1)}), bf16[128,2,256]{2,1,0:T(2,128)(2,1)S(1)}, u32[]{:S(2)}, u32[]{:S(2)}) %all-to-all-start.1) | async-done | bytes 131104 | tf_op jit(solution)/shard_map/all_to_all | solution.py:204
  372.5 4.2 %all-to-all-start = ((bf16[128,2,6]{2,1,0:T(2,128)(2,1)}), bf16[128,2,6]{2,1,0:T(2,128)(2,1)S(1)}, u32[]{:S(2)}, u32[]{:S(2)}) async-start(bf16[128,2,6]{2,1,0:T(2,128)(2,1)} %bitcast.25), calls=%async_computation | async-start | bytes 131072 | tf_op jit(solution)/shard_map/all_to_all | solution.py:211
  377.3 9.0 %all-to-all-done = bf16[128,2,6]{2,1,0:T(2,128)(2,1)S(1)} async-done(((bf16[128,2,6]{2,1,0:T(2,128)(2,1)}), bf16[128,2,6]{2,1,0:T(2,128)(2,1)S(1)}, u32[]{:S(2)}, u32[]{:S(2)}) %all-to-all-start) | async-done | bytes 3104 | tf_op jit(solution)/shard_map/all_to_all | solution.py:211
  (195 shorter events, 46.6 us)
Async XLA Ops:
  0.6 46.2 %copy-start = (bf16[256,256]{1,0:T(8,128)(2,1)S(1)}, bf16[256,256]{1,0:T(8,128)(2,1)}, u32[]{:S(2)}) copy-start(bf16[256,256]{1,0:T(8,128)(2,1)} %param.17) | copy-start | bytes 393220
  0.6 46.9 %copy-start.4 = (bf16[8,256]{1,0:T(8,128)(2,1)S(1)}, bf16[8,256]{1,0:T(8,128)(2,1)}, u32[]{:S(2)}) copy-start(bf16[8,256]{1,0:T(8,128)(2,1)} %param.18) | copy-start | bytes 12292
  0.7 46.9 %copy-start.9 = (f32[256]{0:T(256)S(1)}, f32[256]{0:T(256)}, u32[]{:S(2)}) copy-start(f32[256]{0:T(256)} %param.19) | copy-start | bytes 3076
  0.7 46.9 %copy-start.10 = (bf16[256]{0:T(256)(128)(2,1)S(1)}, bf16[256]{0:T(256)(128)(2,1)}, u32[]{:S(2)}) copy-start(bf16[256]{0:T(256)(128)(2,1)} %param.20) | copy-start | bytes 1540
  1.7 18.1 %collective-permute-start.6 = (bf16[1,2,2,64,256]{4,3,2,1,0:T(8,128)(2,1)S(1)}, bf16[1,2,2,64,256]{4,3,2,1,0:T(8,128)(2,1)S(1)}, u32[]{:S(2)}, u32[]{:S(2)}) collective-permute-start(bf16[1,2,2,64,256]{4,3,2,1,0:T(8,128)(2,1)S(1)} %get-tuple-element.233), channel_id=1, source_target_pairs={{0,16},{16,32},{32,48},{48,64},{64,80},{80,96},{96,112},{112,0},{1... | collective-permute-start | bytes 393224 | tf_op jit(solution)/shard_map/ppermute | solution.py:42
  3.9 16.9 %collective-permute-start.7 = (bf16[1,2,2,64,256]{4,3,2,1,0:T(8,128)(2,1)S(1)}, bf16[1,2,2,64,256]{4,3,2,1,0:T(8,128)(2,1)S(1)}, u32[]{:S(2)}, u32[]{:S(2)}) collective-permute-start(bf16[1,2,2,64,256]{4,3,2,1,0:T(8,128)(2,1)S(1)} %get-tuple-element.232), channel_id=1, source_target_pairs={{16,0},{32,16},{48,32},{64,48},{80,64},{96,80},{112,96},{0,112},{1... | collective-permute-start | bytes 393224 | tf_op jit(solution)/shard_map/ppermute | solution.py:43
  9.5 7.2 %collective-permute-start = (f32[1,2,2,3,64]{4,2,3,1,0:T(2,128)S(1)}, f32[1,2,2,3,64]{4,2,3,1,0:T(2,128)S(1)}, u32[]{:S(2)}, u32[]{:S(2)}) collective-permute-start(f32[1,2,2,3,64]{4,2,3,1,0:T(2,128)S(1)} %get-tuple-element.245), channel_id=1, source_target_pairs={{0,16},{16,32},{32,48},{48,64},{64,80},{80,96},{96,112},{112,0},{1... | collective-permute-start | bytes 9224 | tf_op jit(solution)/shard_map/ppermute | solution.py:42
  9.5 8.0 %collective-permute-start.1 = (f32[1,2,2,3,64]{4,2,3,1,0:T(2,128)S(1)}, f32[1,2,2,3,64]{4,2,3,1,0:T(2,128)S(1)}, u32[]{:S(2)}, u32[]{:S(2)}) collective-permute-start(f32[1,2,2,3,64]{4,2,3,1,0:T(2,128)S(1)} %get-tuple-element.244), channel_id=1, source_target_pairs={{16,0},{32,16},{48,32},{64,48},{80,64},{96,80},{112,96},{0,112},{1... | collective-permute-start | bytes 9224 | tf_op jit(solution)/shard_map/ppermute | solution.py:43
  17.5 5.2 %collective-permute-start.2 = (f32[4,1,2,3,64]{4,2,3,1,0:T(2,128)S(1)}, f32[4,1,2,3,64]{4,2,3,1,0:T(2,128)S(1)}, u32[]{:S(2)}, u32[]{:S(2)}) collective-permute-start(f32[4,1,2,3,64]{4,2,3,1,0:T(2,128)S(1)} %get-tuple-element.242), channel_id=1, source_target_pairs={{0,4},{4,8},{8,12},{12,0},{1,5},{5,9},{9,13},{13,1},{2,6},{6,10},{... | collective-permute-start | bytes 18440 | tf_op jit(solution)/shard_map/ppermute | solution.py:42
  19.8 3.1 collective-permute-start.3
  20.9 6.7 %collective-permute-start.8 = (bf16[4,1,2,64,256]{4,3,2,1,0:T(8,128)(2,1)S(1)}, bf16[4,1,2,64,256]{4,3,2,1,0:T(8,128)(2,1)S(1)}, u32[]{:S(2)}, u32[]{:S(2)}) collective-permute-start(bf16[4,1,2,64,256]{4,3,2,1,0:T(8,128)(2,1)S(1)} %get-tuple-element.230), channel_id=1, source_target_pairs={{0,4},{4,8},{8,12},{12,0},{1,5},{5,9},{9,13},{13,1},{2,6},{6,10},{... | collective-permute-start | bytes 786440 | tf_op jit(solution)/shard_map/ppermute | solution.py:42
  22.7 7.2 %collective-permute-start.9 = (bf16[4,1,2,64,256]{4,3,2,1,0:T(8,128)(2,1)S(1)}, bf16[4,1,2,64,256]{4,3,2,1,0:T(8,128)(2,1)S(1)}, u32[]{:S(2)}, u32[]{:S(2)}) collective-permute-start(bf16[4,1,2,64,256]{4,3,2,1,0:T(8,128)(2,1)S(1)} %get-tuple-element.231), channel_id=1, source_target_pairs={{4,0},{8,4},{12,8},{0,12},{5,1},{9,5},{13,9},{1,13},{6,2},{10,6},{... | collective-permute-start | bytes 786440 | tf_op jit(solution)/shard_map/ppermute | solution.py:43
  30.1 16.4 %collective-permute-start.10 = (bf16[4,4,1,64,256]{4,3,2,1,0:T(8,128)(2,1)S(1)}, bf16[4,4,1,64,256]{4,3,2,1,0:T(8,128)(2,1)S(1)}, u32[]{:S(2)}, u32[]{:S(2)}) collective-permute-start(bf16[4,4,1,64,256]{4,3,2,1,0:T(8,128)(2,1)S(1)} %get-tuple-element.228), channel_id=1, source_target_pairs={{0,1},{1,2},{2,3},{3,0},{4,5},{5,6},{6,7},{7,4},{8,9},{9,10},{10,1... | collective-permute-start | bytes 1572872 | tf_op jit(solution)/shard_map/ppermute | solution.py:42
  31.3 15.2 %collective-permute-start.11 = (bf16[4,4,1,64,256]{4,3,2,1,0:T(8,128)(2,1)S(1)}, bf16[4,4,1,64,256]{4,3,2,1,0:T(8,128)(2,1)S(1)}, u32[]{:S(2)}, u32[]{:S(2)}) collective-permute-start(bf16[4,4,1,64,256]{4,3,2,1,0:T(8,128)(2,1)S(1)} %get-tuple-element.229), channel_id=1, source_target_pairs={{1,0},{2,1},{3,2},{0,3},{5,4},{6,5},{7,6},{4,7},{9,8},{10,9},{11,1... | collective-permute-start | bytes 1572872 | tf_op jit(solution)/shard_map/ppermute | solution.py:43
  32.9 12.6 %collective-permute-start.4 = (f32[4,4,1,3,64]{4,2,3,1,0:T(1,128)S(1)}, f32[4,4,1,3,64]{4,2,3,1,0:T(1,128)S(1)}, u32[]{:S(2)}, u32[]{:S(2)}) collective-permute-start(f32[4,4,1,3,64]{4,2,3,1,0:T(1,128)S(1)} %get-tuple-element.240), channel_id=1, source_target_pairs={{0,1},{1,2},{2,3},{3,0},{4,5},{5,6},{6,7},{7,4},{8,9},{9,10},{10,1... | collective-permute-start | bytes 36872 | tf_op jit(solution)/shard_map/ppermute | solution.py:42
  32.9 12.8 %collective-permute-start.5 = (f32[4,4,1,3,64]{4,2,3,1,0:T(1,128)S(1)}, f32[4,4,1,3,64]{4,2,3,1,0:T(1,128)S(1)}, u32[]{:S(2)}, u32[]{:S(2)}) collective-permute-start(f32[4,4,1,3,64]{4,2,3,1,0:T(1,128)S(1)} %get-tuple-element.241), channel_id=1, source_target_pairs={{1,0},{2,1},{3,2},{0,3},{5,4},{6,5},{7,6},{4,7},{9,8},{10,9},{11,1... | collective-permute-start | bytes 36872 | tf_op jit(solution)/shard_map/ppermute | solution.py:43
  47.6 293.7 %copy-start.8 = (s32[128,1]{0,1:T(1,128)S(1)}, s32[128,1]{0,1:T(1,128)}, u32[]{:S(2)}) copy-start(s32[128,1]{0,1:T(1,128)} %param.24) | copy-start | bytes 1540
  47.6 295.3 %copy-start.7 = (s32[1,128]{1,0:T(1,128)S(1)}, s32[1,128]{1,0:T(1,128)}, u32[]{:S(2)}) copy-start(s32[1,128]{1,0:T(1,128)} %param.23) | copy-start | bytes 1540
  47.6 303.5 %copy-start.2 = (bf16[2,2,2,64,256]{4,3,2,1,0:T(8,128)(2,1)S(1)}, bf16[2,2,2,64,256]{4,3,2,1,0:T(8,128)(2,1)}, u32[]{:S(2)}) copy-start(bf16[2,2,2,64,256]{4,3,2,1,0:T(8,128)(2,1)} %param.16) | copy-start | bytes 786436
  47.6 315.2 %copy-start.6 = (pred[2]{0:T(512)(128)(4,1)S(1)}, pred[2]{0:T(512)(128)(4,1)}, u32[]{:S(2)}) copy-start(pred[2]{0:T(512)(128)(4,1)} %constant.175.clone.1) | copy-start | bytes 10
  47.6 315.4 %copy-start.3 = (f32[2,2,2,3,64]{4,2,3,1,0:T(2,128)S(1)}, f32[2,2,2,3,64]{4,2,3,1,0:T(2,128)}, u32[]{:S(2)}) copy-start(f32[2,2,2,3,64]{4,2,3,1,0:T(2,128)} %param.14) | copy-start | bytes 18436
  47.6 315.4 %copy-start.5 = (f32[2,2,2,3,64]{4,2,3,1,0:T(2,128)S(1)}, f32[2,2,2,3,64]{4,2,3,1,0:T(2,128)}, u32[]{:S(2)}) copy-start(f32[2,2,2,3,64]{4,2,3,1,0:T(2,128)} %param.15) | copy-start | bytes 18436
  62.0 15.0 %copy-start.1 = (f32[4,64,64,256]{3,2,1,0:T(8,128)S(1)}, f32[4,64,64,256]{3,2,1,0:T(8,128)}, u32[]{:S(2)}) copy-start(f32[4,64,64,256]{3,2,1,0:T(8,128)} %fusion.108) | copy-start | bytes 50331652 | tf_op jit(solution)/shard_map/while
  98.1 15.0 %copy-start.1 = (f32[4,64,64,256]{3,2,1,0:T(8,128)S(1)}, f32[4,64,64,256]{3,2,1,0:T(8,128)}, u32[]{:S(2)}) copy-start(f32[4,64,64,256]{3,2,1,0:T(8,128)} %fusion.108) | copy-start | bytes 50331652 | tf_op jit(solution)/shard_map/while
  192.6 149.7 %collective-permute-start.12 = (bf16[1,4,4,3,64]{4,2,1,3,0:T(4,128)(2,1)S(1)}, bf16[1,4,4,3,64]{4,2,1,3,0:T(4,128)(2,1)S(1)}, u32[]{:S(2)}, u32[]{:S(2)}) collective-permute-start(bf16[1,4,4,3,64]{4,2,1,3,0:T(4,128)(2,1)S(1)} %bitcast.120), channel_id=1, source_target_pairs={{0,16},{16,32},{32,48},{48,64},{64,80},{80,96},{96,112},{112,0},{1... | collective-permute-start | bytes 18440 | tf_op jit(solution)/shard_map/ppermute | solution.py:42
  192.7 149.6 %collective-permute-start.13 = (bf16[1,4,4,3,64]{4,2,1,0,3:T(4,128)(2,1)S(1)}, bf16[1,4,4,3,64]{4,2,1,0,3:T(4,128)(2,1)S(1)}, u32[]{:S(2)}, u32[]{:S(2)}) collective-permute-start(bf16[1,4,4,3,64]{4,2,1,0,3:T(4,128)(2,1)S(1)} %bitcast.119), channel_id=1, source_target_pairs={{16,0},{32,16},{48,32},{64,48},{80,64},{96,80},{112,96},{0,112},{1... | collective-permute-start | bytes 18440 | tf_op jit(solution)/shard_map/ppermute | solution.py:43
  342.3 1.3 collective-permute-start.14
  342.4 3.3 collective-permute-start.15
  345.9 16.7 %collective-permute-start.16 = (bf16[6,6,1,3,64]{4,2,1,0,3:T(2,128)(2,1)S(1)}, bf16[6,6,1,3,64]{4,2,1,0,3:T(2,128)(2,1)S(1)}, u32[]{:S(2)}, u32[]{:S(2)}) collective-permute-start(bf16[6,6,1,3,64]{4,2,1,0,3:T(2,128)(2,1)S(1)} %get-tuple-element.234), channel_id=1, source_target_pairs={{0,1},{1,2},{2,3},{3,0},{4,5},{5,6},{6,7},{7,4},{8,9},{9,10},{10,1... | collective-permute-start | bytes 41480 | tf_op jit(solution)/shard_map/ppermute | solution.py:42
  348.5 14.1 %collective-permute-start.17 = (bf16[6,6,1,3,64]{4,2,1,0,3:T(2,128)(2,1)S(1)}, bf16[6,6,1,3,64]{4,2,1,0,3:T(2,128)(2,1)S(1)}, u32[]{:S(2)}, u32[]{:S(2)}) collective-permute-start(bf16[6,6,1,3,64]{4,2,1,0,3:T(2,128)(2,1)S(1)} %get-tuple-element.235), channel_id=1, source_target_pairs={{1,0},{2,1},{3,2},{0,3},{5,4},{6,5},{7,6},{4,7},{9,8},{10,9},{11,1... | collective-permute-start | bytes 41480 | tf_op jit(solution)/shard_map/ppermute | solution.py:43
  353.3 19.2 %all-to-all-start.1 = ((bf16[128,2,256]{2,1,0:T(2,128)(2,1)}), bf16[128,2,256]{2,1,0:T(2,128)(2,1)S(1)}, u32[]{:S(2)}, u32[]{:S(2)}) async-start(bf16[128,2,256]{2,1,0:T(2,128)(2,1)} %convert_element_type.153), calls=%async_computation.1 | async-start | bytes 262144 | tf_op jit(solution)/shard_map/all_to_all | solution.py:204
  372.5 13.8 %all-to-all-start = ((bf16[128,2,6]{2,1,0:T(2,128)(2,1)}), bf16[128,2,6]{2,1,0:T(2,128)(2,1)S(1)}, u32[]{:S(2)}, u32[]{:S(2)}) async-start(bf16[128,2,6]{2,1,0:T(2,128)(2,1)} %bitcast.25), calls=%async_computation | async-start | bytes 131072 | tf_op jit(solution)/shard_map/all_to_all | solution.py:211
  (2 other events, 30.0 us)
where the time goes:
time: 389 us; the launch traced here: 388 us
  starting transfers between devices  190 us (49%)
  matrix products  116 us (30%)
  waiting for transfers between devices  36.2 us (9%)
  local copies, waits for them, and re-layouts  26.5 us (7%)
  other arithmetic  16.9 us (4%)
    ppermute x9, starting transfers between devices, padded(): after = lax.ppermute(initial, axis, down)  166 us
    dot_general x8, matrix products, block_energy(): jnp.einsum('gijn,nl->gijl', radial_basis, radial_weight, preferred_elemen...  94.4 us
    dot_general x4, matrix products, block_energy(): jnp.einsum('gijl,l->gij', hidden, energy_weight, preferred_element_type=j...  20.8 us
    ppermute x9, waiting for transfers between devices, padded(): before = lax.ppermute(last, axis, up)  15.3 us
    ppermute x9, starting transfers between devices, padded(): before = lax.ppermute(last, axis, up)  10.5 us
    all_to_all x1, starting transfers between devices, per_device(): lax.all_to_all(send_embed.astype(jnp.bfloat16), ('gx', 'gy', 'gz'), split...  9.25 us
    all_to_all x1, waiting for transfers between devices, per_device(): lax.all_to_all(send_motion.astype(jnp.bfloat16), ('gx', 'gy', 'gz'), spli...  9.03 us
  transfers between devices with their start and end apart: 20, of which 10 were waited for; matrix products, arithmetic and copies ran while one was open for 3% of the time, Pallas kernels for 0%

commit v1 on v0

v1 whole, which is shorter than its diff:
```python
import functools
import jax
import jax.numpy as jnp
import numpy as np
from jax import lax
from jax.sharding import PartitionSpec as P
from jax.experimental import pallas as pl
from jax.experimental.pallas import tpu as pltpu

F32, BF16 = jnp.float32, jnp.bfloat16
OFFSETS = np.array([[0,0,0],[1,0,0],[0,1,0],[0,0,1],[1,1,0],[1,0,1],[0,1,1],[1,1,1],[1,1,-1],[1,-1,1],[-1,1,1],[1,-1,0],[1,0,-1],[0,1,-1]], np.int32)
LANES = 128
GROUP = 4
MAXCH = 32 * 32

def dot(a, b):
    return jnp.dot(a, b, preferred_element_type=F32)

def dot_nt(a, b):
    return lax.dot_general(a, b, (((1,), (1,)), ((), ())), preferred_element_type=F32)

def iota(shape, dim):
    return lax.broadcasted_iota(jnp.int32, shape, dim)

def sinpi_cospi(theta):
    m = jnp.round(theta)
    f = theta - m
    z = f * f
    sn = f * (3.14159265 + z * (-5.16771278 + z * (2.55016404 + z * (-0.599264529 + z * (0.0821458866 + z * -0.00737043094)))))
    cs = 1.0 + z * (-4.93480220 + z * (4.05871213 + z * (-1.33526277 + z * (0.235330630 + z * (-0.0258068913 + z * 0.00192957431)))))
    sign = 1.0 - 2.0 * (m - 2.0 * jnp.floor(0.5 * m))
    return sn * sign, cs * sign

def pair_kernel(blk, cnt, delta, pos, emb, projt, rb, w2, shift, out, g1, g2, rc, re, wt, acc, tab_b, tab_k, tot):
    live = cnt[0]
    def cells(b):
        a, code = blk[0, b], blk[1, b]
        first = ((a // 4 + 1) * 4 + (a // 2) % 2 + 1) * 4 + a % 2 + 1
        return first, first + delta[code], code
    jl = iota((64, 64), 1)
    il = iota((64, 64), 0)
    upper = jnp.where(il < jl, 1.0, 0.0)
    upper_b = upper.astype(BF16)
    lower_b = jnp.where(jl < il, 1.0, 0.0).astype(BF16)
    ones_b = jnp.ones((64, LANES), BF16)
    lane = iota((64, LANES), 1)

    def prepare(b):
        ca, cb, code = cells(b)
        pa, pb = pos[ca], pos[cb]
        sh = shift[code]
        pbs = pb + sh[:, :64]
        pat = jnp.transpose(pa)
        d2 = None
        for c in range(3):
            df = pbs[c:c + 1, :] - pat[:, c:c + 1]
            d2 = df * df if d2 is None else d2 + df * df
        keep = jnp.logical_and(d2 + 0.25 < 36.001, jnp.logical_or(code != 0, il < jl))
        keep = jnp.where(jnp.logical_and(keep, b < live), 1.0, 0.0)
        keep_b = keep.astype(BF16)
        counts = dot(keep_b, ones_b)
        prefix = dot(keep_b, upper_b)
        start = dot(lower_b, counts.astype(BF16))
        end = start + counts
        rc[b] = start
        re[b] = end
        local = jnp.where(keep > 0.5, prefix, 255.0)
        hi = jnp.floor(start * (1.0 / 64.0)) * 64.0
        side = jnp.where(lane == 64, hi, jnp.where(lane == 65, start - hi, 0.0))
        z = jnp.concatenate([local, side[:, 64:]], axis=1)
        zt = jnp.transpose(z)[:72]
        ah = pa.astype(BF16).astype(F32)
        bh = pb.astype(BF16).astype(F32)
        g1[b] = jnp.concatenate([zt, ah, pa - ah, jnp.zeros((8, 64), F32)], axis=0).astype(BF16)
        g2[b] = jnp.concatenate([bh, pb - bh], axis=0).astype(BF16)
        wt[b] = (dot_nt(projt[...], jnp.concatenate([emb[ca], emb[cb]], axis=0)).astype(BF16) * 0.5).astype(BF16)
        tot[b] = jnp.sum(keep).astype(jnp.int32)

    UNR = 4
    def prep_group(g, c):
        for u in range(UNR):
            prepare(g * UNR + u)
        return c
    lax.fori_loop(0, (live + UNR - 1) // UNR, prep_group, 0)

    def fill_block(b, n):
        chunks = (tot[b] + LANES - 1) // LANES
        def put(t, n):
            tab_b[n] = b
            tab_k[n] = t * LANES
            return n + 1
        return lax.fori_loop(0, chunks, put, n)
    n = lax.fori_loop(0, live, fill_block, 0)
    for u in range(GROUP):
        tab_b[n + u] = 0
        tab_k[n + u] = 1 << 20

    acc[...] = jnp.zeros_like(acc)
    kl = iota((1, LANES), 1)
    sub = iota((8, LANES), 0)
    order = (sub + 1).astype(F32)
    ones_rows = jnp.where(sub < 3, 1.0, 0.0)
    halves = iota((8, LANES), 1) < 64

    def chunk_group(g, c):
        R = range(GROUP)
        ids = [g * GROUP + u for u in R]
        bs = [tab_b[x] for x in ids]
        ks = [(kl + tab_k[x]).astype(F32) for x in ids]
        oh_i = []
        for u in R:
            hit = jnp.logical_and(ks[u] >= rc[bs[u]], ks[u] < re[bs[u]])
            oh_i.append(jnp.where(hit, 1.0, 0.0).astype(BF16))
        got = [dot(g1[bs[u]], oh_i[u]) for u in R]
        oh_j = []
        for u in R:
            want = ks[u] - got[u][64:65] - got[u][65:66]
            oh_j.append(jnp.where(got[u][:64] == want, 1.0, 0.0).astype(BF16))
        gotb = [dot(g2[bs[u]], oh_j[u]) for u in R]
        info = []
        xs = []
        for u in R:
            ca, cb, code = cells(bs[u])
            sep = (gotb[u][:8] + gotb[u][8:] + shift[code]) - (got[u][72:80] + got[u][80:88])
            sq = sep * sep
            d2 = sq[0:1] + sq[1:2] + sq[2:3]
            s = jnp.sqrt(jnp.broadcast_to(d2, (8, LANES)) + 0.25) * (1.0 / 6.0)
            sn, cs = sinpi_cospi(order * s)
            e = jnp.where(s < 1.0, 1.0 - s * s, 0.0)
            info.append((ca, cb, sep, s, e, cs * order))
            x2 = jnp.concatenate([sn, ones_rows], axis=0).astype(BF16)
            xs.append(jnp.concatenate([oh_i[u], oh_j[u], x2, jnp.zeros((112, LANES), BF16)], axis=0))
        qs = [dot(jnp.concatenate([wt[bs[u]], rb[...]], axis=1), xs[u]) for u in R]
        hd = []
        for u in R:
            q = qs[u]
            t = jnp.tanh(q)
            h = q + q * t
            d = (1.0 + t) + h * (1.0 - t)
            hd.append(jnp.concatenate([h.astype(BF16), d.astype(BF16)], axis=0))
        rs = []
        for u in range(0, GROUP, 2):
            both = dot(w2[...], jnp.concatenate([hd[u], hd[u + 1]], axis=1))
            rs += [both[:, :LANES], both[:, LANES:]]
        fs = []
        for u in R:
            ca, cb, sep, s, e, cn = info[u]
            r = rs[u]
            terms = r[:8] * cn * (np.pi * e * e) + r[8:] * (-4.0 * s * e)
            ct = jnp.sum(terms, axis=0, keepdims=True)
            f = sep * (ct / (36.0 * s))
            fh = f.astype(BF16).astype(F32)
            fs.append(jnp.concatenate([fh, f - fh], axis=0).astype(BF16))
        for u in R:
            ca, cb = info[u][:2]
            both = dot_nt(fs[u], xs[u][:128])
            part = both[:8] + both[8:]
            acc[ca] += jnp.where(halves, part, 0.0)
            acc[cb] += jnp.where(halves, 0.0, part)
        return c
    lax.fori_loop(0, (n + GROUP - 1) // GROUP, chunk_group, 0)
    out[...] = acc[:, :, :64] - acc[:, :, 64:]

def pair_forces(block_list, block_count, pos8, emb, embed_proj, radial_weight, latent_bias, energy_weight):
    n_cells = pos8.shape[0]
    rw = radial_weight.astype(F32)
    half = 0.5 * latent_bias
    b1 = half.astype(BF16)
    b2 = (half - b1.astype(F32)).astype(BF16)
    b3 = (half - b1.astype(F32) - b2.astype(F32)).astype(BF16)
    rb = jnp.concatenate([(0.5 * rw).astype(BF16), jnp.stack([b1, b2, b3]), jnp.zeros((117, 256), BF16)], axis=0).T
    ew = energy_weight.astype(F32)
    z8 = jnp.zeros((8, 256), F32)
    w2 = jnp.concatenate([
        jnp.concatenate([z8, ew[None], z8[:7]], axis=0),
        jnp.concatenate([0.5 * rw * ew[None], z8], axis=0)], axis=1).astype(BF16)
    delta = jnp.asarray((OFFSETS[:, 0] * 4 + OFFSETS[:, 1]) * 4 + OFFSETS[:, 2])
    shift = jnp.asarray(np.broadcast_to(np.pad(8.0 * OFFSETS, ((0, 0), (0, 5)))[:, :, None], (14, 8, 128)).astype(np.float32))
    smem = pl.BlockSpec(memory_space=pltpu.SMEM)
    vmem = pl.BlockSpec(memory_space=pltpu.VMEM)
    return pl.pallas_call(
        pair_kernel,
        out_shape=jax.ShapeDtypeStruct((n_cells, 8, 64), F32),
        in_specs=[smem] * 3 + [vmem] * 6,
        out_specs=vmem,
        scratch_shapes=[
            pltpu.VMEM((32, 96, 64), BF16),
            pltpu.VMEM((32, 16, 64), BF16),
            pltpu.VMEM((32, 64, LANES), F32),
            pltpu.VMEM((32, 64, LANES), F32),
            pltpu.VMEM((32, 256, 128), BF16),
            pltpu.VMEM((n_cells, 8, LANES), F32),
            pltpu.SMEM((MAXCH + GROUP,), jnp.int32),
            pltpu.SMEM((MAXCH + GROUP,), jnp.int32),
            pltpu.SMEM((32,), jnp.int32),
        ],
        compiler_params=pltpu.CompilerParams(vmem_limit_bytes=48 * 1024 * 1024),
    )(block_list, block_count, delta, pos8, emb, embed_proj.T, rb, w2, shift)

MOVE_CAP = 2
STEP = 0.5


def padded(value, sides, width):
    for axis, dim in sides:
        size, length = (lax.axis_size(axis), value.shape[dim])
        up = [(i, (i + 1) % size) for i in range(size)]
        down = [(j, i) for i, j in up]
        last = lax.slice_in_dim(value, length - width, length, axis=dim)
        initial = lax.slice_in_dim(value, 0, width, axis=dim)
        before = lax.ppermute(last, axis, up)
        after = lax.ppermute(initial, axis, down)
        value = jnp.concatenate([before, value, after], axis=dim)
    return value


def fold_rim(gathered, axis_dim, span):
    core_part = lax.slice_in_dim(gathered, 2, span + 2, axis=axis_dim)
    lower_rim = lax.slice_in_dim(gathered, 0, 1, axis=axis_dim)
    upper_rim = lax.slice_in_dim(gathered, span + 3, span + 4, axis=axis_dim)
    low_pad = [(0, 0)] * gathered.ndim
    high_pad = [(0, 0)] * gathered.ndim
    low_pad[axis_dim] = (0, span - 1)
    high_pad[axis_dim] = (span - 1, 0)
    return core_part + jnp.pad(lower_rim, low_pad) + jnp.pad(upper_rim, high_pad)


def per_device(
    positions,
    velocity,
    atom_embed,
    embed_proj,
    radial_weight,
    latent_bias,
    energy_weight,
    block_list,
    block_count,
    move_slot,
    move_dest,
):
    span_x, span_y, span_z = (positions.shape[0], positions.shape[1], positions.shape[2])
    cell_atoms = positions.shape[4]
    latent_width = atom_embed.shape[4]
    padded_coords = padded(positions, (("gx", 0), ("gy", 1), ("gz", 2)), 1)
    arriving = padded(atom_embed, (("gx", 0), ("gy", 1), ("gz", 2)), 1)
    cells = 4 * 4 * 4
    pos8 = jnp.pad(padded_coords.reshape(cells, 3, cell_atoms), ((0, 0), (0, 5), (0, 0)))
    force_sum = pair_forces(block_list[0], block_count, pos8, arriving.reshape(cells, cell_atoms, latent_width), embed_proj, radial_weight, latent_bias, energy_weight)
    padded_force = force_sum[:, :3].reshape(span_x + 2, span_y + 2, span_z + 2, 3, cell_atoms)
    gathered = padded(
        padded_force.astype(jnp.bfloat16), (("gx", 0), ("gy", 1), ("gz", 2)), 1
    ).astype(padded_force.dtype)
    forces = fold_rim(fold_rim(fold_rim(gathered, 0, span_x), 1, span_y), 2, span_z)
    new_velocity = velocity + STEP * forces
    new_position = positions + STEP * new_velocity
    motion = jnp.concatenate([new_position, new_velocity], axis=3).reshape(-1, 6, cell_atoms)
    slot_list = move_slot[0]
    moving_motion = motion[slot_list // cell_atoms, :, slot_list % cell_atoms]
    moving_embed = atom_embed.reshape(-1, latent_width)[slot_list].astype(jnp.float32)
    target = move_dest[:, 0]
    device_total = lax.axis_size(("gx", "gy", "gz"))
    row_index = jnp.arange(target.shape[0])
    earlier = (target[:, None] == target[None, :]) & (row_index[None, :] < row_index[:, None])
    ranking = jnp.sum(earlier.astype(jnp.int32), axis=1)
    place_index = target * MOVE_CAP + ranking
    send_motion = (
        jnp.zeros((device_total * MOVE_CAP, 6), jnp.float32)
        .at[place_index]
        .set(moving_motion)
        .reshape(device_total, MOVE_CAP, 6)
    )
    send_embed = (
        jnp.zeros((device_total * MOVE_CAP, latent_width), jnp.float32)
        .at[place_index]
        .set(moving_embed)
        .reshape(device_total, MOVE_CAP, latent_width)
    )
    got_embed, got_motion = (
        lax.all_to_all(
            send_embed.astype(jnp.bfloat16),
            ("gx", "gy", "gz"),
            split_axis=0,
            concat_axis=0,
            tiled=True,
        ).astype(send_embed.dtype),
        lax.all_to_all(
            send_motion.astype(jnp.bfloat16),
            ("gx", "gy", "gz"),
            split_axis=0,
            concat_axis=0,
            tiled=True,
        ).astype(send_motion.dtype),
    )
    return (forces, got_motion, got_embed.astype(jnp.bfloat16))


def solution(mesh):
    placed = (
        P("gx", "gy", "gz", None, None),
        P("gx", "gy", "gz", None, None),
        P("gx", "gy", "gz", None, None),
        P(),
        P(),
        P(),
        P(),
        P(("gx", "gy", "gz"), None, None),
        P(("gx", "gy", "gz")),
        P(("gx", "gy", "gz"), None),
        P(("gx", "gy", "gz"), None),
    )
    return jax.shard_map(
        per_device,
        mesh=mesh,
        in_specs=placed,
        out_specs=(
            P("gx", "gy", "gz", None, None),
            P(("gx", "gy", "gz"), None, None),
            P(("gx", "gy", "gz"), None, None),
        ),
        check_vma=False,
    )
```

time: 389 us -> 122 us (0.31)
  starting transfers between devices: 190 us -> 50.2 us
  matrix products: 116 us -> 0 us
  Pallas kernels: 0 us -> 15.5 us
  waiting for transfers between devices: 36.2 us -> 21.2 us
  blocking collectives: 0 us -> 13.6 us
  local copies, waits for them, and re-layouts: 26.5 us -> 13.2 us
  other arithmetic: 16.9 us -> 6.26 us
    ppermute x9, starting transfers between devices: 166 us -> 30.9 us  [padded(): after = lax.ppermute(initial, axis, down)]
    dot_general x13 -> x0, matrix products: 116 us -> none  [the longest x8 94.4 us: block_energy(): jnp.einsum('gijn,nl->gijl', radial_basis, radial_weight, preferred_elemen...]
    gather x16 -> x0, local copies, waits for them, and re-layouts: 16.2 us -> none  [the longest x4 5.9 us: visit_group(): flat_coords[pick_second]]
    pallas_call x0 -> x1, Pallas kernels: none -> 15.5 us  [pair_forces(): pl.pallas_call(pair_kernel, out_shape=jax.ShapeDtypeStruct((n_cells, 8, 6...]
    all_to_all x0 -> x1, blocking collectives: none -> 13.6 us  [per_device(): lax.all_to_all(send_motion.astype(jnp.bfloat16), ('gx', 'gy', 'gz'), spli...]
    all_to_all x1 -> x0, waiting for transfers between devices: 9.03 us -> none  [per_device(): lax.all_to_all(send_motion.astype(jnp.bfloat16), ('gx', 'gy', 'gz'), spli...]
    ppermute x9, waiting for transfers between devices: 15.3 us -> 9.44 us  [padded(): before = lax.ppermute(last, axis, up)]
    scatter-add x8 -> x0, other arithmetic: 5.18 us -> none  [visit_group(): return force_sum.at[pick_first].add(-grad_a).at[pick_second].add(-grad_b)]
  transfers between devices with their start and end apart: 20 -> 19, of which waited for: 10 -> 8; matrix products, arithmetic and copies ran while one was open for 3% -> 13% of each run, Pallas kernels for 0% -> 0%
where the time goes in v1:
time: 122 us
  starting transfers between devices  50.2 us (41%)
  waiting for transfers between devices  21.2 us (17%)
  Pallas kernels  15.5 us (13%)
  blocking collectives  13.6 us (11%)
  local copies, waits for them, and re-layouts  13.2 us (11%)
  other arithmetic  6.26 us (5%)
  between operations  1.77 us (1%)
    ppermute x9, starting transfers between devices, padded(): after = lax.ppermute(initial, axis, down)  30.9 us
    pallas_call x1, Pallas kernels, pair_forces(): pl.pallas_call(pair_kernel, out_shape=jax.ShapeDtypeStruct((n_cells, 8, 6...  15.5 us
    all_to_all x1, blocking collectives, per_device(): lax.all_to_all(send_motion.astype(jnp.bfloat16), ('gx', 'gy', 'gz'), spli...  13.6 us
    ppermute x9, starting transfers between devices, padded(): before = lax.ppermute(last, axis, up)  10.4 us
    ppermute x9, waiting for transfers between devices, padded(): before = lax.ppermute(last, axis, up)  9.44 us
    all_to_all x1, starting transfers between devices, per_device(): lax.all_to_all(send_embed.astype(jnp.bfloat16), ('gx', 'gy', 'gz'), split...  8.89 us
    all_to_all x1, waiting for transfers between devices, per_device(): lax.all_to_all(send_embed.astype(jnp.bfloat16), ('gx', 'gy', 'gz'), split...  6.98 us
    ppermute x9, waiting for transfers between devices, padded(): after = lax.ppermute(initial, axis, down)  4.76 us
  transfers between devices with their start and end apart: 19, of which 8 were waited for; matrix products, arithmetic and copies ran while one was open for 13% of the time, Pallas kernels for 0%

profile of v1, /device:TPU:1, one launch (start us, length us, event | category | flops | bytes accessed | tf_op | source)
XLA Modules:
  0.0 121.6 jit_solution(2942962506135771860)
XLA Ops:
  0.6 1.0 fusion.30
  1.6 2.2 %collective-permute-start.6 = (bf16[1,2,2,64,256]{4,3,2,1,0:T(8,128)(2,1)S(1)}, bf16[1,2,2,64,256]{4,3,2,1,0:T(8,128)(2,1)S(1)}, u32[]{:S(2)}, u32[]{:S(2)}) collective-permute-start(bf16[1,2,2,64,256]{4,3,2,1,0:T(8,128)(2,1)S(1)} %get-tuple-element.17), channel_id=1, source_target_pairs={{0,16},{16,32},{32,48},{48,64},{64,80},{80,96},{96,112},{112,0},{1... | collective-permute-start | bytes 393224 | tf_op jit(solution)/shard_map/ppermute | solution.py:211
  3.8 4.8 %collective-permute-start.7 = (bf16[1,2,2,64,256]{4,3,2,1,0:T(8,128)(2,1)S(1)}, bf16[1,2,2,64,256]{4,3,2,1,0:T(8,128)(2,1)S(1)}, u32[]{:S(2)}, u32[]{:S(2)}) collective-permute-start(bf16[1,2,2,64,256]{4,3,2,1,0:T(8,128)(2,1)S(1)} %get-tuple-element.16), channel_id=1, source_target_pairs={{16,0},{32,16},{48,32},{64,48},{80,64},{96,80},{112,96},{0,112},{1... | collective-permute-start | bytes 393224 | tf_op jit(solution)/shard_map/ppermute | solution.py:212
  8.6 0.7 fusion.36
  9.4 5.1 %collective-permute-start.1 = (f32[1,2,2,3,64]{4,2,3,1,0:T(2,128)S(1)}, f32[1,2,2,3,64]{4,2,3,1,0:T(2,128)S(1)}, u32[]{:S(2)}, u32[]{:S(2)}) collective-permute-start(f32[1,2,2,3,64]{4,2,3,1,0:T(2,128)S(1)} %get-tuple-element.28), channel_id=1, source_target_pairs={{16,0},{32,16},{48,32},{64,48},{80,64},{96,80},{112,96},{0,112},{1... | collective-permute-start | bytes 9224 | tf_op jit(solution)/shard_map/ppermute | solution.py:212
  15.1 0.7 fusion.16
  17.1 0.7 constant_dynamic-update-slice_fusion.1
  17.9 1.0 constant_dynamic-update-slice_fusion.4
  18.9 2.3 %collective-permute-start.8 = (bf16[4,1,2,64,256]{4,3,2,1,0:T(8,128)(2,1)S(1)}, bf16[4,1,2,64,256]{4,3,2,1,0:T(8,128)(2,1)S(1)}, u32[]{:S(2)}, u32[]{:S(2)}) collective-permute-start(bf16[4,1,2,64,256]{4,3,2,1,0:T(8,128)(2,1)S(1)} %get-tuple-element.14), channel_id=1, source_target_pairs={{0,4},{4,8},{8,12},{12,0},{1,5},{5,9},{9,13},{13,1},{2,6},{6,10},{... | collective-permute-start | bytes 786440 | tf_op jit(solution)/shard_map/ppermute | solution.py:211
  21.3 1.8 %collective-permute-start.2 = (f32[4,1,2,3,64]{4,2,3,1,0:T(2,128)S(1)}, f32[4,1,2,3,64]{4,2,3,1,0:T(2,128)S(1)}, u32[]{:S(2)}, u32[]{:S(2)}) collective-permute-start(f32[4,1,2,3,64]{4,2,3,1,0:T(2,128)S(1)} %get-tuple-element.26), channel_id=1, source_target_pairs={{0,4},{4,8},{8,12},{12,0},{1,5},{5,9},{9,13},{13,1},{2,6},{6,10},{... | collective-permute-start | bytes 18440 | tf_op jit(solution)/shard_map/ppermute | solution.py:211
  23.1 3.1 %collective-permute-done.8 = bf16[4,1,2,64,256]{4,3,2,1,0:T(8,128)(2,1)S(1)} collective-permute-done((bf16[4,1,2,64,256]{4,3,2,1,0:T(8,128)(2,1)S(1)}, bf16[4,1,2,64,256]{4,3,2,1,0:T(8,128)(2,1)S(1)}, u32[]{:S(2)}, u32[]{:S(2)}) %collective-permute-start.8) | collective-permute-done | bytes 262176 | tf_op jit(solution)/shard_map/ppermute | solution.py:211
  26.2 2.4 %collective-permute-done.9 = bf16[4,1,2,64,256]{4,3,2,1,0:T(8,128)(2,1)S(1)} collective-permute-done((bf16[4,1,2,64,256]{4,3,2,1,0:T(8,128)(2,1)S(1)}, bf16[4,1,2,64,256]{4,3,2,1,0:T(8,128)(2,1)S(1)}, u32[]{:S(2)}, u32[]{:S(2)}) %collective-permute-start.9) | collective-permute-done | bytes 262176 | tf_op jit(solution)/shard_map/ppermute | solution.py:212
  28.8 1.3 %collective-permute-start.10 = (bf16[4,4,1,64,256]{4,3,2,1,0:T(8,128)(2,1)S(1)}, bf16[4,4,1,64,256]{4,3,2,1,0:T(8,128)(2,1)S(1)}, u32[]{:S(2)}, u32[]{:S(2)}) collective-permute-start(bf16[4,4,1,64,256]{4,3,2,1,0:T(8,128)(2,1)S(1)} %get-tuple-element.12), channel_id=1, source_target_pairs={{0,1},{1,2},{2,3},{3,0},{4,5},{5,6},{6,7},{7,4},{8,9},{9,10},{10,1... | collective-permute-start | bytes 1572872 | tf_op jit(solution)/shard_map/ppermute | solution.py:211
  30.1 1.5 %collective-permute-start.11 = (bf16[4,4,1,64,256]{4,3,2,1,0:T(8,128)(2,1)S(1)}, bf16[4,4,1,64,256]{4,3,2,1,0:T(8,128)(2,1)S(1)}, u32[]{:S(2)}, u32[]{:S(2)}) collective-permute-start(bf16[4,4,1,64,256]{4,3,2,1,0:T(8,128)(2,1)S(1)} %get-tuple-element.13), channel_id=1, source_target_pairs={{1,0},{2,1},{3,2},{0,3},{5,4},{6,5},{7,6},{4,7},{9,8},{10,9},{11,1... | collective-permute-start | bytes 1572872 | tf_op jit(solution)/shard_map/ppermute | solution.py:212
  32.3 2.7 %collective-permute-start.5 = (f32[4,4,1,3,64]{4,2,3,1,0:T(1,128)}, f32[4,4,1,3,64]{4,2,3,1,0:T(1,128)}, u32[]{:S(2)}, u32[]{:S(2)}) collective-permute-start(f32[4,4,1,3,64]{4,2,3,1,0:T(1,128)} %get-tuple-element.25), channel_id=1, source_target_pairs={{1,0},{2,1},{3,2},{0,3},{5,4},{6,5},{7,6},{4,7},{9,8},{10,9},{11,1... | collective-permute-start | bytes 36872 | tf_op jit(solution)/shard_map/ppermute | solution.py:212
  35.3 0.7 copy.36
  36.0 1.0 copy.35
  38.3 1.0 concatenate.53
  39.4 4.9 %collective-permute-done.4 = f32[4,4,1,3,64]{4,2,3,1,0:T(1,128)} collective-permute-done((f32[4,4,1,3,64]{4,2,3,1,0:T(1,128)}, f32[4,4,1,3,64]{4,2,3,1,0:T(1,128)}, u32[]{:S(2)}, u32[]{:S(2)}) %collective-permute-start.4) | collective-permute-done | bytes 12320 | tf_op jit(solution)/shard_map/ppermute | solution.py:211
  44.5 0.9 pad_maximum_fusion.3
  46.4 15.5 %shard_map.148 = f32[64,8,64]{2,1,0:T(8,128)S(1)} custom-call(s32[2,32]{1,0:T(2,128)S(1)} %bitcast.41, s32[1]{0:T(128)S(6)} %copy.53.cnt, s32[14]{0:T(128)S(1)} %copy-done.2, f32[64,8,64]{2,1,0:T(8,128)S(1)} %pad.30.pos, bf16[64,64,256]{2,1,0:T(8,128)(2,1)S(1)} %bitcast.38, bf16[256,256]{1,0:T(8,128)(2,1)S(1)} %bitcast.39, bf16[256,128]{1,0:T(8,128)(2,1)S(1)} %bitcast.40, ...), custom_call_target="tpu_custom_call" | custom-call | tf_op jit(solution)/shard_map/pallas_call | solution.py:181
  62.3 16.2 %collective-permute-start.13 = (bf16[1,4,4,3,64]{4,2,3,1,0:T(4,128)(2,1)S(1)}, bf16[1,4,4,3,64]{4,2,3,1,0:T(4,128)(2,1)S(1)}, u32[]{:S(2)}, u32[]{:S(2)}) collective-permute-start(bf16[1,4,4,3,64]{4,2,3,1,0:T(4,128)(2,1)S(1)} %copy.41), channel_id=1, source_target_pairs={{16,0},{32,16},{48,32},{64,48},{80,64},{96,80},{112,96},{0,112},{1... | collective-permute-start | bytes 18440 | tf_op jit(solution)/shard_map/ppermute | solution.py:212
  78.5 0.8 collective-permute-done.12
  80.6 2.1 %collective-permute-done.15 = bf16[6,1,4,3,64]{4,2,3,1,0:T(4,128)(2,1)S(1)} collective-permute-done((bf16[6,1,4,3,64]{4,2,3,1,0:T(4,128)(2,1)S(1)}, bf16[6,1,4,3,64]{4,2,3,1,0:T(4,128)(2,1)S(1)}, u32[]{:S(2)}, u32[]{:S(2)}) %collective-permute-start.15) | collective-permute-done | bytes 9248 | tf_op jit(solution)/shard_map/ppermute | solution.py:212
  82.9 2.6 %collective-permute-start.16 = (bf16[6,6,1,3,64]{4,2,3,1,0:T(2,128)(2,1)S(1)}, bf16[6,6,1,3,64]{4,2,3,1,0:T(2,128)(2,1)S(1)}, u32[]{:S(2)}, u32[]{:S(2)}) collective-permute-start(bf16[6,6,1,3,64]{4,2,3,1,0:T(2,128)(2,1)S(1)} %get-tuple-element.20), channel_id=1, source_target_pairs={{0,1},{1,2},{2,3},{3,0},{4,5},{5,6},{6,7},{7,4},{8,9},{9,10},{10,1... | collective-permute-start | bytes 41480 | tf_op jit(solution)/shard_map/ppermute | solution.py:211
  85.6 1.4 %scatter_custom_fusion.1 = f32[256,256]{1,0:T(8,128)S(1)} fusion(s32[128]{0:T(128)S(1)} %get-tuple-element.37, f32[]{:T(128)} %constant.46.clone.1, bf16[512,256]{1,0:T(8,128)(2,1)S(1)} %bitcast.42, s32[1024]{0:T(1024)S(1)} %pad_clamp_fusion), kind=kCustom, calls=%fused_computation.10 | custom fusion | flops 32768 | bytes 528388 | tf_op jit(solution)/shard_map/scatter | solution.py:275
  87.1 0.7 convert_element_type.86
  87.8 8.9 %all-to-all-start.1 = ((bf16[128,2,256]{2,1,0:T(2,128)(2,1)}), bf16[128,2,256]{2,1,0:T(2,128)(2,1)S(1)}, u32[]{:S(2)}, u32[]{:S(2)}) async-start(bf16[128,2,256]{2,1,0:T(2,128)(2,1)} %convert_element_type.86), calls=%async_computation.1 | async-start | bytes 262144 | tf_op jit(solution)/shard_map/all_to_all | solution.py:279
  98.1 1.6 %scatter_custom_fusion = f32[256,6]{1,0:T(8,128)S(1)} fusion(s32[128]{0:T(128)S(1)} %get-tuple-element.37, f32[8,6,64]{1,2,0:T(8,128)S(1)} %bitcast.46, s32[128]{0:T(128)S(1)} %get-tuple-element.36, f32[]{:T(128)} %constant.46.clone.1), kind=kCustom, calls=%fused_computation.15 | custom fusion | bytes 6148 | tf_op jit(solution)/shard_map/scatter | solution.py:269
  99.7 7.0 %all-to-all-done.1 = bf16[128,2,256]{2,1,0:T(2,128)(2,1)S(1)} async-done(((bf16[128,2,256]{2,1,0:T(2,128)(2,1)}), bf16[128,2,256]{2,1,0:T(2,128)(2,1)S(1)}, u32[]{:S(2)}, u32[]{:S(2)}) %all-to-all-start.1) | async-done | bytes 131104 | tf_op jit(solution)/shard_map/all_to_all | solution.py:279
  106.7 13.6 %all_to_all.10 = bf16[128,2,6]{2,1,0:T(2,128)(2,1)S(1)} all-to-all(bf16[128,2,6]{2,1,0:T(2,128)(2,1)S(1)} %bitcast.44), channel_id=1, replica_groups=mesh['gx'=8,'gy'=4,'gz'=4] {'gx','gy','gz'}, dimensions={0} | all-to-all | bytes 6144 | tf_op jit(solution)/shard_map/all_to_all | solution.py:286
  120.3 0.7 copy.44
  (94 shorter events, 9.0 us)
Async XLA Ops:
  1.6 16.2 %collective-permute-start.6 = (bf16[1,2,2,64,256]{4,3,2,1,0:T(8,128)(2,1)S(1)}, bf16[1,2,2,64,256]{4,3,2,1,0:T(8,128)(2,1)S(1)}, u32[]{:S(2)}, u32[]{:S(2)}) collective-permute-start(bf16[1,2,2,64,256]{4,3,2,1,0:T(8,128)(2,1)S(1)} %get-tuple-element.17), channel_id=1, source_target_pairs={{0,16},{16,32},{32,48},{48,64},{64,80},{80,96},{96,112},{112,0},{1... | collective-permute-start | bytes 393224 | tf_op jit(solution)/shard_map/ppermute | solution.py:211
  3.8 15.0 %collective-permute-start.7 = (bf16[1,2,2,64,256]{4,3,2,1,0:T(8,128)(2,1)S(1)}, bf16[1,2,2,64,256]{4,3,2,1,0:T(8,128)(2,1)S(1)}, u32[]{:S(2)}, u32[]{:S(2)}) collective-permute-start(bf16[1,2,2,64,256]{4,3,2,1,0:T(8,128)(2,1)S(1)} %get-tuple-element.16), channel_id=1, source_target_pairs={{16,0},{32,16},{48,32},{64,48},{80,64},{96,80},{112,96},{0,112},{1... | collective-permute-start | bytes 393224 | tf_op jit(solution)/shard_map/ppermute | solution.py:212
  9.4 7.8 %collective-permute-start = (f32[1,2,2,3,64]{4,2,3,1,0:T(2,128)S(1)}, f32[1,2,2,3,64]{4,2,3,1,0:T(2,128)S(1)}, u32[]{:S(2)}, u32[]{:S(2)}) collective-permute-start(f32[1,2,2,3,64]{4,2,3,1,0:T(2,128)S(1)} %get-tuple-element.29), channel_id=1, source_target_pairs={{0,16},{16,32},{32,48},{48,64},{64,80},{80,96},{96,112},{112,0},{1... | collective-permute-start | bytes 9224 | tf_op jit(solution)/shard_map/ppermute | solution.py:211
  9.4 11.9 %collective-permute-start.1 = (f32[1,2,2,3,64]{4,2,3,1,0:T(2,128)S(1)}, f32[1,2,2,3,64]{4,2,3,1,0:T(2,128)S(1)}, u32[]{:S(2)}, u32[]{:S(2)}) collective-permute-start(f32[1,2,2,3,64]{4,2,3,1,0:T(2,128)S(1)} %get-tuple-element.28), channel_id=1, source_target_pairs={{16,0},{32,16},{48,32},{64,48},{80,64},{96,80},{112,96},{0,112},{1... | collective-permute-start | bytes 9224 | tf_op jit(solution)/shard_map/ppermute | solution.py:212
  18.9 7.3 %collective-permute-start.8 = (bf16[4,1,2,64,256]{4,3,2,1,0:T(8,128)(2,1)S(1)}, bf16[4,1,2,64,256]{4,3,2,1,0:T(8,128)(2,1)S(1)}, u32[]{:S(2)}, u32[]{:S(2)}) collective-permute-start(bf16[4,1,2,64,256]{4,3,2,1,0:T(8,128)(2,1)S(1)} %get-tuple-element.14), channel_id=1, source_target_pairs={{0,4},{4,8},{8,12},{12,0},{1,5},{5,9},{9,13},{13,1},{2,6},{6,10},{... | collective-permute-start | bytes 786440 | tf_op jit(solution)/shard_map/ppermute | solution.py:211
  21.3 7.3 %collective-permute-start.9 = (bf16[4,1,2,64,256]{4,3,2,1,0:T(8,128)(2,1)S(1)}, bf16[4,1,2,64,256]{4,3,2,1,0:T(8,128)(2,1)S(1)}, u32[]{:S(2)}, u32[]{:S(2)}) collective-permute-start(bf16[4,1,2,64,256]{4,3,2,1,0:T(8,128)(2,1)S(1)} %get-tuple-element.15), channel_id=1, source_target_pairs={{4,0},{8,4},{12,8},{0,12},{5,1},{9,5},{13,9},{1,13},{6,2},{10,6},{... | collective-permute-start | bytes 786440 | tf_op jit(solution)/shard_map/ppermute | solution.py:212
  21.3 10.3 %copy-start.4 = (f32[4,2,2,3,64]{4,2,3,1,0:T(2,128)}, f32[4,2,2,3,64]{4,2,3,1,0:T(2,128)S(1)}, u32[]{:S(2)}) copy-start(f32[4,2,2,3,64]{4,2,3,1,0:T(2,128)S(1)} %constant_dynamic-update-slice_fusion) | copy-start | bytes 36868
  21.3 10.2 %collective-permute-start.2 = (f32[4,1,2,3,64]{4,2,3,1,0:T(2,128)S(1)}, f32[4,1,2,3,64]{4,2,3,1,0:T(2,128)S(1)}, u32[]{:S(2)}, u32[]{:S(2)}) collective-permute-start(f32[4,1,2,3,64]{4,2,3,1,0:T(2,128)S(1)} %get-tuple-element.26), channel_id=1, source_target_pairs={{0,4},{4,8},{8,12},{12,0},{1,5},{5,9},{9,13},{13,1},{2,6},{6,10},{... | collective-permute-start | bytes 18440 | tf_op jit(solution)/shard_map/ppermute | solution.py:211
  23.1 8.4 %collective-permute-start.3 = (f32[4,1,2,3,64]{4,2,3,1,0:T(2,128)S(1)}, f32[4,1,2,3,64]{4,2,3,1,0:T(2,128)S(1)}, u32[]{:S(2)}, u32[]{:S(2)}) collective-permute-start(f32[4,1,2,3,64]{4,2,3,1,0:T(2,128)S(1)} %get-tuple-element.27), channel_id=1, source_target_pairs={{4,0},{8,4},{12,8},{0,12},{5,1},{9,5},{13,9},{1,13},{6,2},{10,6},{... | collective-permute-start | bytes 18440 | tf_op jit(solution)/shard_map/ppermute | solution.py:212
  28.8 16.8 %collective-permute-start.10 = (bf16[4,4,1,64,256]{4,3,2,1,0:T(8,128)(2,1)S(1)}, bf16[4,4,1,64,256]{4,3,2,1,0:T(8,128)(2,1)S(1)}, u32[]{:S(2)}, u32[]{:S(2)}) collective-permute-start(bf16[4,4,1,64,256]{4,3,2,1,0:T(8,128)(2,1)S(1)} %get-tuple-element.12), channel_id=1, source_target_pairs={{0,1},{1,2},{2,3},{3,0},{4,5},{5,6},{6,7},{7,4},{8,9},{9,10},{10,1... | collective-permute-start | bytes 1572872 | tf_op jit(solution)/shard_map/ppermute | solution.py:211
  30.1 15.5 %collective-permute-start.11 = (bf16[4,4,1,64,256]{4,3,2,1,0:T(8,128)(2,1)S(1)}, bf16[4,4,1,64,256]{4,3,2,1,0:T(8,128)(2,1)S(1)}, u32[]{:S(2)}, u32[]{:S(2)}) collective-permute-start(bf16[4,4,1,64,256]{4,3,2,1,0:T(8,128)(2,1)S(1)} %get-tuple-element.13), channel_id=1, source_target_pairs={{1,0},{2,1},{3,2},{0,3},{5,4},{6,5},{7,6},{4,7},{9,8},{10,9},{11,1... | collective-permute-start | bytes 1572872 | tf_op jit(solution)/shard_map/ppermute | solution.py:212
  31.5 3.6 %copy-start.6 = (f32[4,1,2,3,64]{4,2,3,1,0:T(2,128)}, f32[4,1,2,3,64]{4,2,3,1,0:T(2,128)S(1)}, u32[]{:S(2)}) copy-start(f32[4,1,2,3,64]{4,2,3,1,0:T(2,128)S(1)} %collective-permute-done.2) | copy-start | bytes 18436
  31.6 3.6 %copy-start.7 = (f32[4,1,2,3,64]{4,2,3,1,0:T(2,128)}, f32[4,1,2,3,64]{4,2,3,1,0:T(2,128)S(1)}, u32[]{:S(2)}) copy-start(f32[4,1,2,3,64]{4,2,3,1,0:T(2,128)S(1)} %collective-permute-done.3) | copy-start | bytes 18436
  32.3 12.0 %collective-permute-start.4 = (f32[4,4,1,3,64]{4,2,3,1,0:T(1,128)}, f32[4,4,1,3,64]{4,2,3,1,0:T(1,128)}, u32[]{:S(2)}, u32[]{:S(2)}) collective-permute-start(f32[4,4,1,3,64]{4,2,3,1,0:T(1,128)} %get-tuple-element.24), channel_id=1, source_target_pairs={{0,1},{1,2},{2,3},{3,0},{4,5},{5,6},{6,7},{7,4},{8,9},{9,10},{10,1... | collective-permute-start | bytes 36872 | tf_op jit(solution)/shard_map/ppermute | solution.py:211
  32.3 12.3 %collective-permute-start.5 = (f32[4,4,1,3,64]{4,2,3,1,0:T(1,128)}, f32[4,4,1,3,64]{4,2,3,1,0:T(1,128)}, u32[]{:S(2)}, u32[]{:S(2)}) collective-permute-start(f32[4,4,1,3,64]{4,2,3,1,0:T(1,128)} %get-tuple-element.25), channel_id=1, source_target_pairs={{1,0},{2,1},{3,2},{0,3},{5,4},{6,5},{7,6},{4,7},{9,8},{10,9},{11,1... | collective-permute-start | bytes 36872 | tf_op jit(solution)/shard_map/ppermute | solution.py:212
  45.5 0.8 copy-start
  45.5 0.8 copy-start.1
  45.5 0.8 copy-start.2
  45.9 16.2 %copy-start.11 = (s32[128,1]{0,1:T(1,128)S(1)}, s32[128,1]{0,1:T(1,128)}, u32[]{:S(2)}) copy-start(s32[128,1]{0,1:T(1,128)} %param.23) | copy-start | bytes 1540
  45.9 34.0 %copy-start.10 = (s32[1,128]{1,0:T(1,128)S(1)}, s32[1,128]{1,0:T(1,128)}, u32[]{:S(2)}) copy-start(s32[1,128]{1,0:T(1,128)} %param.22) | copy-start | bytes 1540
  46.4 39.3 %copy-start.3 = (bf16[2,2,2,64,256]{4,3,2,1,0:T(8,128)(2,1)S(1)}, bf16[2,2,2,64,256]{4,3,2,1,0:T(8,128)(2,1)}, u32[]{:S(2)}) copy-start(bf16[2,2,2,64,256]{4,3,2,1,0:T(8,128)(2,1)} %param.15) | copy-start | bytes 786436
  61.8 35.1 %copy-start.9 = (pred[2]{0:T(512)(128)(4,1)S(1)}, pred[2]{0:T(512)(128)(4,1)}, u32[]{:S(2)}) copy-start(pred[2]{0:T(512)(128)(4,1)} %constant.49.clone.1) | copy-start | bytes 10
  61.9 35.3 %copy-start.5 = (f32[2,2,2,3,64]{4,2,3,1,0:T(2,128)S(1)}, f32[2,2,2,3,64]{4,2,3,1,0:T(2,128)}, u32[]{:S(2)}) copy-start(f32[2,2,2,3,64]{4,2,3,1,0:T(2,128)} %param.13) | copy-start | bytes 18436
  61.9 35.3 %copy-start.8 = (f32[2,2,2,3,64]{4,2,3,1,0:T(2,128)S(1)}, f32[2,2,2,3,64]{4,2,3,1,0:T(2,128)}, u32[]{:S(2)}) copy-start(f32[2,2,2,3,64]{4,2,3,1,0:T(2,128)} %param.14) | copy-start | bytes 18436
  61.9 17.3 %collective-permute-start.12 = (bf16[1,4,4,3,64]{4,2,3,1,0:T(4,128)(2,1)S(1)}, bf16[1,4,4,3,64]{4,2,3,1,0:T(4,128)(2,1)S(1)}, u32[]{:S(2)}, u32[]{:S(2)}) collective-permute-start(bf16[1,4,4,3,64]{4,2,3,1,0:T(4,128)(2,1)S(1)} %copy.40), channel_id=1, source_target_pairs={{0,16},{16,32},{32,48},{48,64},{64,80},{80,96},{96,112},{112,0},{1... | collective-permute-start | bytes 18440 | tf_op jit(solution)/shard_map/ppermute | solution.py:211
  62.3 17.0 %collective-permute-start.13 = (bf16[1,4,4,3,64]{4,2,3,1,0:T(4,128)(2,1)S(1)}, bf16[1,4,4,3,64]{4,2,3,1,0:T(4,128)(2,1)S(1)}, u32[]{:S(2)}, u32[]{:S(2)}) collective-permute-start(bf16[1,4,4,3,64]{4,2,3,1,0:T(4,128)(2,1)S(1)} %copy.41), channel_id=1, source_target_pairs={{16,0},{32,16},{48,32},{64,48},{80,64},{96,80},{112,96},{0,112},{1... | collective-permute-start | bytes 18440 | tf_op jit(solution)/shard_map/ppermute | solution.py:212
  79.3 1.3 %collective-permute-start.14 = (bf16[6,1,4,3,64]{4,2,3,1,0:T(4,128)(2,1)S(1)}, bf16[6,1,4,3,64]{4,2,3,1,0:T(4,128)(2,1)S(1)}, u32[]{:S(2)}, u32[]{:S(2)}) collective-permute-start(bf16[6,1,4,3,64]{4,2,3,1,0:T(4,128)(2,1)S(1)} %get-tuple-element.22), channel_id=1, source_target_pairs={{0,4},{4,8},{8,12},{12,0},{1,5},{5,9},{9,13},{13,1},{2,6},{6,10},{... | collective-permute-start | bytes 27656 | tf_op jit(solution)/shard_map/ppermute | solution.py:211
  79.4 3.3 %collective-permute-start.15 = (bf16[6,1,4,3,64]{4,2,3,1,0:T(4,128)(2,1)S(1)}, bf16[6,1,4,3,64]{4,2,3,1,0:T(4,128)(2,1)S(1)}, u32[]{:S(2)}, u32[]{:S(2)}) collective-permute-start(bf16[6,1,4,3,64]{4,2,3,1,0:T(4,128)(2,1)S(1)} %get-tuple-element.23), channel_id=1, source_target_pairs={{4,0},{8,4},{12,8},{0,12},{5,1},{9,5},{13,9},{1,13},{6,2},{10,6},{... | collective-permute-start | bytes 27656 | tf_op jit(solution)/shard_map/ppermute | solution.py:212
  82.9 13.8 %collective-permute-start.16 = (bf16[6,6,1,3,64]{4,2,3,1,0:T(2,128)(2,1)S(1)}, bf16[6,6,1,3,64]{4,2,3,1,0:T(2,128)(2,1)S(1)}, u32[]{:S(2)}, u32[]{:S(2)}) collective-permute-start(bf16[6,6,1,3,64]{4,2,3,1,0:T(2,128)(2,1)S(1)} %get-tuple-element.20), channel_id=1, source_target_pairs={{0,1},{1,2},{2,3},{3,0},{4,5},{5,6},{6,7},{7,4},{8,9},{9,10},{10,1... | collective-permute-start | bytes 41480 | tf_op jit(solution)/shard_map/ppermute | solution.py:211
  85.5 11.2 %collective-permute-start.17 = (bf16[6,6,1,3,64]{4,2,3,1,0:T(2,128)(2,1)S(1)}, bf16[6,6,1,3,64]{4,2,3,1,0:T(2,128)(2,1)S(1)}, u32[]{:S(2)}, u32[]{:S(2)}) collective-permute-start(bf16[6,6,1,3,64]{4,2,3,1,0:T(2,128)(2,1)S(1)} %get-tuple-element.21), channel_id=1, source_target_pairs={{1,0},{2,1},{3,2},{0,3},{5,4},{6,5},{7,6},{4,7},{9,8},{10,9},{11,1... | collective-permute-start | bytes 41480 | tf_op jit(solution)/shard_map/ppermute | solution.py:212
  87.8 18.9 %all-to-all-start.1 = ((bf16[128,2,256]{2,1,0:T(2,128)(2,1)}), bf16[128,2,256]{2,1,0:T(2,128)(2,1)S(1)}, u32[]{:S(2)}, u32[]{:S(2)}) async-start(bf16[128,2,256]{2,1,0:T(2,128)(2,1)} %convert_element_type.86), calls=%async_computation.1 | async-start | bytes 262144 | tf_op jit(solution)/shard_map/all_to_all | solution.py:279

commit v2 on v1

v2 whole, which is shorter than its diff:
```python
import functools

import jax
import jax.numpy as jnp
import numpy as np
from jax import lax
from jax.experimental import pallas as pl
from jax.experimental.pallas import tpu as pltpu
from jax.sharding import PartitionSpec as P

F32, BF16 = jnp.float32, jnp.bfloat16
MESH = pl.DeviceIdType.MESH
OFFSETS = np.array([[0, 0, 0], [1, 0, 0], [0, 1, 0], [0, 0, 1], [1, 1, 0], [1, 0, 1], [0, 1, 1], [1, 1, 1], [1, 1, -1], [1, -1, 1], [-1, 1, 1], [1, -1, 0], [1, 0, -1], [0, 1, -1]], np.int32)
LANES = 128
GROUP = 4
MAXCH = 32 * 32
SIZES = (8, 4, 4)


def ghost_boxes():
    need = {}
    for a in np.ndindex(2, 2, 2):
        for o in OFFSETS:
            b = [int(x) for x in np.array(a) + o]
            s = tuple(-1 if x < 0 else (1 if x > 1 else 0) for x in b)
            if any(s):
                need.setdefault(s, []).append([x - 2 * y for x, y in zip(b, s)])
    boxes = []
    for s in sorted(need, key=lambda s: (-len(set(map(tuple, need[s]))), s)):
        own = [(min(c[d] for c in need[s]), max(c[d] for c in need[s]) + 1) for d in range(3)]
        boxes.append((s, own, [(lo + 2 * s[d] + 1, hi + 2 * s[d] + 1) for d, (lo, hi) in enumerate(own)]))
    return boxes


BOXES = ghost_boxes()
N_BOX = len(BOXES)


def box(ref, ranges):
    return ref.at[tuple(pl.ds(lo, hi - lo) for lo, hi in ranges)]


def dot(a, b):
    return jnp.dot(a, b, preferred_element_type=F32)


def dot_nt(a, b):
    return lax.dot_general(a, b, (((1,), (1,)), ((), ())), preferred_element_type=F32)


def iota(shape, dim):
    return lax.broadcasted_iota(jnp.int32, shape, dim)


def position():
    return tuple(lax.axis_index(a) for a in ("gx", "gy", "gz"))


def shifted(me, s, sign):
    return tuple(lax.rem(m + sign * d + n, n) if d else m for m, d, n in zip(me, s, SIZES))


def enter(me, toward):
    barrier = pltpu.get_barrier_semaphore()
    for s, _, _ in BOXES:
        pl.semaphore_signal(barrier, inc=1, device_id=shifted(me, s, toward), device_id_type=MESH)
    for k in range(1, 16):
        pl.semaphore_signal(barrier, inc=1, device_id=plane_partner(me, k)[0], device_id_type=MESH)
    for k in range(1, 8):
        pl.semaphore_signal(barrier, inc=1, device_id=line_partner(me, k)[0], device_id_type=MESH)
    pl.semaphore_wait(barrier, N_BOX + 15 + 7)


def plane_partner(me, k):
    at = lax.rem(me[1] * 4 + me[2] + k, 16)
    return (me[0], at // 4, lax.rem(at, 4)), at


def line_partner(me, k):
    at = lax.rem(me[0] + k, 8)
    return (at, me[1], me[2]), at


def exchange(me, partner, count, rows, src, dst, send_sem, recv_sem):
    copies = []
    mine = me[0] if count == 8 else me[1] * 4 + me[2]
    here = pl.ds(pl.multiple_of(mine * rows, rows), rows)
    for k in range(1, count):
        device, at = partner(me, k)
        copy = pltpu.make_async_remote_copy(
            src_ref=src.at[pl.ds(pl.multiple_of(at * rows, rows), rows)],
            dst_ref=dst.at[here],
            send_sem=send_sem.at[k],
            recv_sem=recv_sem.at[k],
            device_id=device,
            device_id_type=MESH,
        )
        copy.start()
        copies.append(copy)
    dst[here] = src[here]
    return copies


def wait_all(copies):
    for copy in copies:
        copy.wait()


def placement(dest, ranks_apart):
    dest_f = dest.astype(F32)
    col = jnp.broadcast_to(dest_f, (128, LANES))
    row = jnp.transpose(col)
    earlier = jnp.logical_and(col == row, iota((128, 128), 1) < iota((128, 128), 0))
    rank = jnp.sum(jnp.where(earlier, 1.0, 0.0), axis=1, keepdims=True)
    gx = jnp.floor(dest_f * (1.0 / 16.0))
    order = (dest_f - 16.0 * gx) * 8.0 + gx
    place = order + 128.0 * rank if ranks_apart else 2.0 * order + rank
    lanes = iota((128, 256), 1).astype(F32)
    return jnp.where(lanes == place, 1.0, 0.0).astype(BF16)


def halo_kernel(pos, emb, slot, dest, gpos, gemb, arrived, emb_v, send1, recv1, send2, recv2, es, er, ps, pr, loc, s1, r1, s2, r2):
    me = position()
    own = [(1, 3)] * 3
    local = [
        pltpu.make_async_copy(emb, emb_v, loc.at[0]),
        pltpu.make_async_copy(emb, box(gemb, own), loc.at[1]),
        pltpu.make_async_copy(pos, box(gpos, own), loc.at[2]),
    ]
    for copy in local:
        copy.start()
    enter(me, 1)
    halo = []
    for i, (s, src, dst) in enumerate(BOXES):
        device = shifted(me, s, -1)
        for a, b, x, y in ((pos, gpos, ps, pr), (emb, gemb, es, er)):
            copy = pltpu.make_async_remote_copy(src_ref=box(a, src), dst_ref=box(b, dst), send_sem=x.at[i], recv_sem=y.at[i], device_id=device, device_id_type=MESH)
            copy.start()
            halo.append(copy)
    where = placement(dest[...], False)
    slots = slot[...]
    pick = jnp.where(iota((512, 128), 0) == slots, 1.0, 0.0).astype(BF16)
    place = lax.dot_general(where, pick, (((0,), (1,)), ((), ())), preferred_element_type=F32).astype(BF16)
    local[0].wait()
    rows = emb_v[...].reshape(512, 256)
    send1[...] = dot(place, rows).astype(BF16)
    wait_all(exchange(me, plane_partner, 16, 16, send1, recv1, s1, r1))
    out = iota((256, 256), 0)
    want = ((out // 2) % 16) * 16 + (out // 32) * 2 + out % 2
    perm = jnp.where(iota((256, 256), 1) == want, 1.0, 0.0).astype(BF16)
    send2[...] = dot(perm, recv1[...]).astype(BF16)
    wait_all(exchange(me, line_partner, 8, 32, send2, recv2, s2, r2))
    arrived[...] = recv2[...]
    local[1].wait()
    local[2].wait()
    wait_all(halo)


def return_kernel(fsum, pos, vel, slot, dest, forces, arrived, landed, mot, send1, recv1, send2, recv2, fs, fr, s1, r1, s2, r2):
    me = position()
    enter(me, -1)
    back = []
    for i, (s, own, ghost) in enumerate(BOXES):
        copy = pltpu.make_async_remote_copy(src_ref=box(fsum, ghost), dst_ref=box(landed.at[i], own), send_sem=fs.at[i], recv_sem=fr.at[i], device_id=shifted(me, s, 1), device_id_type=MESH)
        copy.start()
        back.append(copy)
    where = placement(dest[...], True)
    pick = jnp.where(iota((512, 128), 0) == slot[...], 1.0, 0.0).astype(BF16)
    place = dot(pick, where).astype(BF16)
    out = iota((128, 128), 0)
    perm = jnp.where(iota((128, 128), 1) == (out % 16) * 8 + out // 16, 1.0, 0.0).astype(BF16)
    mot[...] = jnp.zeros_like(mot)
    wait_all(back)
    for c in np.ndindex(2, 2, 2):
        total = fsum[c[0] + 1, c[1] + 1, c[2] + 1]
        for i, (s, own, ghost) in enumerate(BOXES):
            if all(lo <= x < hi for x, (lo, hi) in zip(c, own)):
                total = total + landed[i, c[0], c[1], c[2]]
        forces[c[0], c[1], c[2]] = total
        new_velocity = vel[c[0], c[1], c[2]] + 0.5 * total[:3]
        new_position = pos[c[0], c[1], c[2]] + 0.5 * new_velocity
        at = (c[0] * 4 + c[1] * 2 + c[2]) * 64
        mot[0:3, at:at + 64] = new_position
        mot[8:11, at:at + 64] = new_velocity
    rows = dot(mot[...].astype(BF16), place)
    tall = jnp.concatenate([rows[:, :128], rows[:, 128:], jnp.zeros((96, 128), F32)], axis=0)
    send1[...] = jnp.transpose(tall)
    wait_all(exchange(me, plane_partner, 16, 8, send1, recv1, s1, r1))
    send2[...] = dot(perm, recv1[...].astype(BF16))
    wait_all(exchange(me, line_partner, 8, 16, send2, recv2, s2, r2))
    arrived[...] = recv2[...]


def sinpi_cospi(theta):
    m = jnp.round(theta)
    f = theta - m
    z = f * f
    sn = f * (3.14159265 + z * (-5.16771278 + z * (2.55016404 + z * (-0.599264529 + z * (0.0821458866 + z * -0.00737043094)))))
    cs = 1.0 + z * (-4.93480220 + z * (4.05871213 + z * (-1.33526277 + z * (0.235330630 + z * (-0.0258068913 + z * 0.00192957431)))))
    sign = 1.0 - 2.0 * (m - 2.0 * jnp.floor(0.5 * m))
    return sn * sign, cs * sign


def pair_kernel(blk, cnt, delta, gpos, gemb, proj, rw, bias, ew, shift, out, pos, g1, g2, rc, re, wt, projt, rb, w2, acc, tab_b, tab_k, tot):
    live = cnt[0]

    def cells(b):
        a, code = blk[0, 0, b], blk[0, 1, b]
        first = ((a // 4 + 1) * 4 + (a // 2) % 2 + 1) * 4 + a % 2 + 1
        return first, first + delta[code], code

    jl = iota((64, 64), 1)
    il = iota((64, 64), 0)
    upper_b = jnp.where(il < jl, 1.0, 0.0).astype(BF16)
    lower_b = jnp.where(jl < il, 1.0, 0.0).astype(BF16)
    ones_b = jnp.ones((64, LANES), BF16)
    lane = iota((64, LANES), 1)

    pos[...] = jnp.zeros_like(pos)
    pos[:, 0:3, :] = gpos[...].reshape(64, 3, 64)
    projt[...] = jnp.transpose(proj[...])
    half = 0.5 * bias[...]
    b1 = half.astype(BF16).astype(F32)
    b2 = (half - b1).astype(BF16).astype(F32)
    row8 = iota((8, 256), 0)
    biases = jnp.where(row8 == 0, b1, jnp.where(row8 == 1, b2, jnp.where(row8 == 2, half - b1 - b2, 0.0)))
    rwf = rw[...].astype(F32)
    ewf = ew[...].astype(F32)
    rb[...] = jnp.transpose(jnp.concatenate([0.5 * rwf, biases, jnp.zeros((112, 256), F32)], axis=0)).astype(BF16)
    z8 = jnp.zeros((8, 256), F32)
    w2[:, :256] = jnp.concatenate([z8, jnp.where(row8 == 0, ewf, 0.0)], axis=0).astype(BF16)
    w2[:, 256:] = jnp.concatenate([0.5 * rwf * ewf, z8], axis=0).astype(BF16)

    def prepare(b):
        ca, cb, code = cells(b)
        pa, pb = pos[ca], pos[cb]
        pbs = pb + shift[code][:, :64]
        pat = jnp.transpose(pa)
        d2 = None
        for c in range(3):
            df = pbs[c:c + 1, :] - pat[:, c:c + 1]
            d2 = df * df if d2 is None else d2 + df * df
        keep = jnp.logical_and(d2 + 0.25 < 36.001, jnp.logical_or(code != 0, il < jl))
        keep = jnp.where(jnp.logical_and(keep, b < live), 1.0, 0.0)
        keep_b = keep.astype(BF16)
        counts = dot(keep_b, ones_b)
        prefix = dot(keep_b, upper_b)
        start = dot(lower_b, counts.astype(BF16))
        rc[b] = start
        re[b] = start + counts
        local = jnp.where(keep > 0.5, prefix, 255.0)
        hi = jnp.floor(start * (1.0 / 64.0)) * 64.0
        side = jnp.where(lane == 64, hi, jnp.where(lane == 65, start - hi, 0.0))
        zt = jnp.transpose(jnp.concatenate([local, side[:, 64:]], axis=1))[:72]
        ah = pa.astype(BF16).astype(F32)
        bh = pb.astype(BF16).astype(F32)
        g1[b] = jnp.concatenate([zt, ah, pa - ah, jnp.zeros((8, 64), F32)], axis=0).astype(BF16)
        g2[b] = jnp.concatenate([bh, pb - bh], axis=0).astype(BF16)
        both = jnp.concatenate([gemb[ca], gemb[cb]], axis=0)
        wt[b] = (dot_nt(projt[...], both).astype(BF16) * 0.5).astype(BF16)
        tot[b] = jnp.sum(keep).astype(jnp.int32)

    unroll = 4

    def prep_group(g, c):
        for u in range(unroll):
            prepare(g * unroll + u)
        return c

    lax.fori_loop(0, (live + unroll - 1) // unroll, prep_group, 0)

    def fill_block(b, n):
        def put(t, n):
            tab_b[n] = b
            tab_k[n] = t * LANES
            return n + 1

        return lax.fori_loop(0, (tot[b] + LANES - 1) // LANES, put, n)

    n = lax.fori_loop(0, live, fill_block, 0)
    for u in range(GROUP):
        tab_b[n + u] = 0
        tab_k[n + u] = 1 << 20

    acc[...] = jnp.zeros_like(acc)
    kl = iota((1, LANES), 1)
    sub = iota((8, LANES), 0)
    order = (sub + 1).astype(F32)
    ones_rows = jnp.where(sub < 3, 1.0, 0.0)
    halves = iota((8, LANES), 1) < 64

    def chunk_group(g, c):
        R = range(GROUP)
        ids = [g * GROUP + u for u in R]
        bs = [tab_b[x] for x in ids]
        ks = [(kl + tab_k[x]).astype(F32) for x in ids]
        oh_i = []
        for u in R:
            hit = jnp.logical_and(ks[u] >= rc[bs[u]], ks[u] < re[bs[u]])
            oh_i.append(jnp.where(hit, 1.0, 0.0).astype(BF16))
        got = [dot(g1[bs[u]], oh_i[u]) for u in R]
        oh_j = []
        for u in R:
            want = ks[u] - got[u][64:65] - got[u][65:66]
            oh_j.append(jnp.where(got[u][:64] == want, 1.0, 0.0).astype(BF16))
        gotb = [dot(g2[bs[u]], oh_j[u]) for u in R]
        info = []
        xs = []
        for u in R:
            ca, cb, code = cells(bs[u])
            sep = (gotb[u][:8] + gotb[u][8:] + shift[code]) - (got[u][72:80] + got[u][80:88])
            sq = sep * sep
            d2 = sq[0:1] + sq[1:2] + sq[2:3]
            s = jnp.sqrt(jnp.broadcast_to(d2, (8, LANES)) + 0.25) * (1.0 / 6.0)
            sn, cs = sinpi_cospi(order * s)
            e = jnp.where(s < 1.0, 1.0 - s * s, 0.0)
            info.append((ca, cb, sep, s, e, cs * order))
            x2 = jnp.concatenate([sn, ones_rows], axis=0).astype(BF16)
            xs.append(jnp.concatenate([oh_i[u], oh_j[u], x2, jnp.zeros((112, LANES), BF16)], axis=0))
        qs = [dot(jnp.concatenate([wt[bs[u]], rb[...]], axis=1), xs[u]) for u in R]
        hd = []
        for u in R:
            q = qs[u]
            t = jnp.tanh(q)
            h = q + q * t
            d = (1.0 + t) + h * (1.0 - t)
            hd.append(jnp.concatenate([h.astype(BF16), d.astype(BF16)], axis=0))
        rs = []
        for u in range(0, GROUP, 2):
            both = dot(w2[...], jnp.concatenate([hd[u], hd[u + 1]], axis=1))
            rs += [both[:, :LANES], both[:, LANES:]]
        fs = []
        for u in R:
            ca, cb, sep, s, e, cn = info[u]
            r = rs[u]
            terms = r[:8] * cn * (np.pi * e * e) + r[8:] * (-4.0 * s * e)
            ct = jnp.sum(terms, axis=0, keepdims=True)
            f = sep * (ct / (36.0 * s))
            fh = f.astype(BF16).astype(F32)
            fs.append(jnp.concatenate([fh, f - fh], axis=0).astype(BF16))
        for u in R:
            ca, cb = info[u][:2]
            both = dot_nt(fs[u], xs[u][:128])
            part = both[:8] + both[8:]
            acc[ca] += jnp.where(halves, part, 0.0)
            acc[cb] += jnp.where(halves, 0.0, part)
        return c

    lax.fori_loop(0, (n + GROUP - 1) // GROUP, chunk_group, 0)
    out[...] = (acc[:, :, :64] - acc[:, :, 64:]).reshape(4, 4, 4, 8, 64)


def pair_forces(block_list, block_count, gpos, gemb, embed_proj, radial_weight, latent_bias, energy_weight):
    delta = jnp.asarray((OFFSETS[:, 0] * 4 + OFFSETS[:, 1]) * 4 + OFFSETS[:, 2])
    shift = jnp.asarray(np.broadcast_to(np.pad(8.0 * OFFSETS, ((0, 0), (0, 5)))[:, :, None], (14, 8, 128)).astype(np.float32))
    smem = pl.BlockSpec(memory_space=pltpu.SMEM)
    vmem = pl.BlockSpec(memory_space=pltpu.VMEM)
    return pl.pallas_call(
        pair_kernel,
        out_shape=jax.ShapeDtypeStruct((4, 4, 4, 8, 64), F32),
        in_specs=[smem] * 3 + [vmem] * 7,
        out_specs=vmem,
        scratch_shapes=[
            pltpu.VMEM((64, 8, 64), F32),
            pltpu.VMEM((32, 96, 64), BF16),
            pltpu.VMEM((32, 16, 64), BF16),
            pltpu.VMEM((32, 64, LANES), F32),
            pltpu.VMEM((32, 64, LANES), F32),
            pltpu.VMEM((32, 256, 128), BF16),
            pltpu.VMEM((256, 256), BF16),
            pltpu.VMEM((256, 128), BF16),
            pltpu.VMEM((16, 512), BF16),
            pltpu.VMEM((64, 8, LANES), F32),
            pltpu.SMEM((MAXCH + GROUP,), jnp.int32),
            pltpu.SMEM((MAXCH + GROUP,), jnp.int32),
            pltpu.SMEM((32,), jnp.int32),
        ],
        compiler_params=pltpu.CompilerParams(vmem_limit_bytes=48 * 1024 * 1024),
        name="pairs",
    )(block_list, block_count, delta, gpos, gemb.reshape(64, 64, 256), embed_proj, radial_weight, latent_bias.reshape(1, 256), energy_weight.reshape(1, 256), shift)


def per_device(positions, velocity, atom_embed, embed_proj, radial_weight, latent_bias, energy_weight, block_list, block_count, move_slot, move_dest):
    any_, vmem, smem = (pl.BlockSpec(memory_space=m) for m in (pl.ANY, pltpu.VMEM, pltpu.SMEM))
    dma = pltpu.SemaphoreType.DMA
    gpos, gemb, got_embed = pl.pallas_call(
        halo_kernel,
        out_shape=(jax.ShapeDtypeStruct((4, 4, 4, 3, 64), F32), jax.ShapeDtypeStruct((4, 4, 4, 64, 256), BF16), jax.ShapeDtypeStruct((256, 256), BF16)),
        in_specs=[any_, any_, vmem, vmem],
        out_specs=(any_, any_, vmem),
        scratch_shapes=[pltpu.VMEM((2, 2, 2, 64, 256), BF16)] + [pltpu.VMEM((256, 256), BF16)] * 4
        + [dma((N_BOX,))] * 4 + [dma((3,))] + [dma((16,))] * 2 + [dma((8,))] * 2,
        compiler_params=pltpu.CompilerParams(collective_id=0, has_side_effects=True, vmem_limit_bytes=32 * 1024 * 1024),
        name="halo",
    )(positions, atom_embed, move_slot, move_dest)
    fsum = pair_forces(block_list, block_count, gpos, gemb, embed_proj, radial_weight, latent_bias, energy_weight)
    forces, moved = pl.pallas_call(
        return_kernel,
        out_shape=(jax.ShapeDtypeStruct((2, 2, 2, 8, 64), F32), jax.ShapeDtypeStruct((128, LANES), F32)),
        in_specs=[vmem] * 5,
        out_specs=(vmem, vmem),
        scratch_shapes=[pltpu.VMEM((N_BOX, 2, 2, 2, 8, 64), F32), pltpu.VMEM((16, 512), F32)] + [pltpu.VMEM((128, LANES), F32)] * 4
        + [dma((N_BOX,))] * 2 + [dma((16,))] * 2 + [dma((8,))] * 2,
        compiler_params=pltpu.CompilerParams(collective_id=1, has_side_effects=True, vmem_limit_bytes=32 * 1024 * 1024),
        name="give_back",
    )(fsum, positions, velocity, move_slot, move_dest)
    motion = moved[:, :32].reshape(128, 2, 2, 8)[..., :3].reshape(128, 2, 6)
    return forces[..., :3, :], motion, got_embed.reshape(128, 2, 256)


def solution(mesh):
    placed = (
        P("gx", "gy", "gz", None, None),
        P("gx", "gy", "gz", None, None),
        P("gx", "gy", "gz", None, None),
        P(),
        P(),
        P(),
        P(),
        P(("gx", "gy", "gz"), None, None),
        P(("gx", "gy", "gz")),
        P(("gx", "gy", "gz"), None),
        P(("gx", "gy", "gz"), None),
    )
    return jax.shard_map(
        per_device,
        mesh=mesh,
        in_specs=placed,
        out_specs=(
            P("gx", "gy", "gz", None, None),
            P(("gx", "gy", "gz"), None, None),
            P(("gx", "gy", "gz"), None, None),
        ),
        check_vma=False,
    )
```

time: 122 us -> 89.7 us (0.74)
  Pallas kernels: 15.5 us -> 77.8 us
  starting transfers between devices: 50.2 us -> 0 us
  waiting for transfers between devices: 21.2 us -> 0 us
  blocking collectives: 13.6 us -> 0 us
  other arithmetic: 6.26 us -> 0 us
  local copies, waits for them, and re-layouts: 13.2 us -> 10.2 us
    pallas_call x1 -> x3, Pallas kernels: 15.5 us -> 77.8 us  [the longest x1 39.2 us: per_device(): pl.pallas_call(return_kernel, out_shape=(jax.ShapeDtypeStruct((2, 2, 2, 8...]
    ppermute x18 -> x0, starting transfers between devices: 41.3 us -> none  [the longest x9 30.9 us: padded(): after = lax.ppermute(initial, axis, down)]
    ppermute x18 -> x0, waiting for transfers between devices: 14.2 us -> none  [the longest x9 9.44 us: padded(): before = lax.ppermute(last, axis, up)]
    all_to_all x1 -> x0, blocking collectives: 13.6 us -> none  [per_device(): lax.all_to_all(send_motion.astype(jnp.bfloat16), ('gx', 'gy', 'gz'), spli...]
    all_to_all x1 -> x0, starting transfers between devices: 8.89 us -> none  [per_device(): lax.all_to_all(send_embed.astype(jnp.bfloat16), ('gx', 'gy', 'gz'), split...]
    all_to_all x1 -> x0, waiting for transfers between devices: 6.98 us -> none  [per_device(): lax.all_to_all(send_embed.astype(jnp.bfloat16), ('gx', 'gy', 'gz'), split...]
    unnamed x33 -> x24, local copies, waits for them, and re-layouts: 4.59 us -> 8.13 us
    slice x15 -> x4, local copies, waits for them, and re-layouts: 2.67 us -> 0.68 us  [the longest x3 0.68 us: per_device(): motion = moved[:, :32].reshape(128, 2, 2, 8)[..., :3].reshape(128, 2, 6)]
  transfers between devices with their start and end apart: 19 -> 0, of which waited for: 8 -> 0; matrix products, arithmetic and copies ran while one was open for 13% -> 0% of each run, Pallas kernels for 0% -> 0%
where the time goes in v2:
time: 89.7 us; the launch traced here: 89.3 us
  Pallas kernels  77.8 us (87%)
  local copies, waits for them, and re-layouts  10.2 us (11%)
  between operations  1.36 us (2%)
    pallas_call x1, Pallas kernels, per_device(): pl.pallas_call(return_kernel, out_shape=(jax.ShapeDtypeStruct((2, 2, 2, 8...  39.2 us
    pallas_call x1, Pallas kernels, per_device(): pl.pallas_call(halo_kernel, out_shape=(jax.ShapeDtypeStruct((4, 4, 4, 3,...  31.2 us
    unnamed x24, local copies, waits for them, and re-layouts  8.13 us
    pallas_call x1, Pallas kernels, pair_forces(): pl.pallas_call(pair_kernel, out_shape=jax.ShapeDtypeStruct((4, 4, 4, 8, 6...  7.36 us

profile of v2, /device:TPU:1, one launch (start us, length us, event | category | flops | bytes accessed | tf_op | source)
XLA Modules:
  0.0 89.3 jit_solution(16390712203944106681)
XLA Ops:
  0.6 0.0 copy-start.5
  0.6 0.0 copy-start.9
  0.7 0.8 copy.32.dest
  1.4 0.7 copy.31.pos
  2.1 0.0 copy-start
  2.1 0.9 %copy-done = bf16[2,2,2,64,256]{4,3,2,1,0:T(8,128)(2,1)S(1)} copy-done((bf16[2,2,2,64,256]{4,3,2,1,0:T(8,128)(2,1)S(1)}, bf16[2,2,2,64,256]{4,3,2,1,0:T(8,128)(2,1)}, u32[]{:S(2)}) %copy-start) | copy-done | bytes 262168
  3.1 0.0 copy-start.4
  3.1 0.7 copy-done.4
  3.7 31.2 %halo.1 = (f32[4,4,4,3,64]{4,3,2,1,0:T(4,128)S(1)}, bf16[4,4,4,64,256]{4,3,2,1,0:T(8,128)(2,1)S(1)}, bf16[256,256]{1,0:T(8,128)(2,1)S(1)}) custom-call(f32[2,2,2,3,64]{4,3,2,1,0:T(4,128)S(1)} %copy.31.pos, bf16[2,2,2,64,256]{4,3,2,1,0:T(8,128)(2,1)S(1)} %copy-done, s32[1,128]{1,0:T(1,128)S(1)} %copy-done.4, s32[128,1]{1,0:T(8,128)S(1)} %copy.32.dest), custom_call_target="tpu_custom_call" | custom-call | tf_op jit(solution)/shard_map/halo/pallas_call | solution.py:386
  34.9 0.7 reshape.26.ew
  36.3 0.0 copy-start.1
  36.3 0.9 %copy-done.1 = bf16[256,256]{1,0:T(8,128)(2,1)S(1)} copy-done((bf16[256,256]{1,0:T(8,128)(2,1)S(1)}, bf16[256,256]{1,0:T(8,128)(2,1)}, u32[]{:S(2)}) %copy-start.1) | copy-done | bytes 131096
  37.2 0.0 copy-start.2
  37.2 0.8 copy-done.2
  38.0 0.0 copy-start.3
  38.0 0.7 copy-done.3
  38.7 0.0 copy-start.6
  38.7 0.7 copy-done.6
  39.4 0.0 copy-start.7
  39.4 0.7 copy-done.7
  40.0 0.0 copy-start.8
  40.0 0.7 copy-done.8
  40.7 7.4 %pairs.1.fsum = f32[4,4,4,8,64]{4,3,2,1,0:T(8,128)S(1)} custom-call(s32[1,2,32]{2,1,0:T(2,128)S(1)} %copy-done.6, s32[1]{0:T(128)S(6)} %copy.39.cnt, s32[14]{0:T(128)S(1)} %copy-done.8, f32[4,4,4,3,64]{4,3,2,1,0:T(4,128)S(1)} %get-tuple-element.8.gpos, bf16[64,64,256]{2,1,0:T(8,128)(2,1)S(1)} %bitcast.5, bf16[256,256]{1,0:T(8,128)(2,1)S(1)} %copy-done.1, ...), custom_call_target="tpu_custom_call" | custom-call | tf_op jit(solution)/shard_map/pairs/pallas_call | solution.py:358
  48.1 0.0 copy-done.9
  48.1 0.0 copy-done.5
  48.1 39.2 %give_back.1 = (f32[2,2,2,8,64]{4,3,2,1,0:T(8,128)S(1)}, f32[128,128]{1,0:T(8,128)S(1)}) custom-call(f32[4,4,4,8,64]{4,3,2,1,0:T(8,128)S(1)} %pairs.1.fsum, f32[2,2,2,3,64]{4,3,2,1,0:T(4,128)S(1)} %copy.31.pos, f32[2,2,2,3,64]{4,3,2,1,0:T(4,128)S(1)} %copy.34.vel, s32[1,128]{1,0:T(1,128)S(1)} %copy-done.5, s32[128,1]{1,0:T(8,128)S(1)} %copy.32.dest), custom_call_target="tpu_custom_call" | custom-call | tf_op jit(solution)/shard_map/give_back/pallas_call | solution.py:397
  87.3 0.1 copy.36
  87.4 0.6 copy.37
  88.0 0.6 copy.38
  88.6 0.7 reshape.29
  (3 shorter events, 0.0 us)
Async XLA Ops:
  0.6 47.5 %copy-start.5 = (s32[1,128]{1,0:T(1,128)S(1)}, s32[1,128]{1,0:T(1,128)}, u32[]{:S(2)}) copy-start(s32[1,128]{1,0:T(1,128)} %slot.3) | copy-start | bytes 1540
  0.6 47.4 %copy-start.9 = (f32[2,2,2,3,64]{4,2,3,1,0:T(2,128)S(1)}, f32[2,2,2,3,64]{4,2,3,1,0:T(2,128)}, u32[]{:S(2)}) copy-start(f32[2,2,2,3,64]{4,2,3,1,0:T(2,128)} %param.14) | copy-start | bytes 18436
  2.1 0.9 %copy-start = (bf16[2,2,2,64,256]{4,3,2,1,0:T(8,128)(2,1)S(1)}, bf16[2,2,2,64,256]{4,3,2,1,0:T(8,128)(2,1)}, u32[]{:S(2)}) copy-start(bf16[2,2,2,64,256]{4,3,2,1,0:T(8,128)(2,1)} %emb.1) | copy-start | bytes 786436
  3.1 0.7 copy-start.4
  36.3 0.9 %copy-start.1 = (bf16[256,256]{1,0:T(8,128)(2,1)S(1)}, bf16[256,256]{1,0:T(8,128)(2,1)}, u32[]{:S(2)}) copy-start(bf16[256,256]{1,0:T(8,128)(2,1)} %proj.1) | copy-start | bytes 393220
  37.2 0.8 copy-start.2
  38.0 0.7 copy-start.3
  38.7 0.7 copy-start.6
  39.4 0.7 copy-start.7
  40.0 0.7 copy-start.8

commit v3 on v2

v3 whole, which is shorter than its diff:
```python
import functools

import jax
import jax.numpy as jnp
import numpy as np
from jax import lax
from jax.experimental import pallas as pl
from jax.experimental.pallas import tpu as pltpu
from jax.sharding import PartitionSpec as P

F32, BF16 = jnp.float32, jnp.bfloat16
MESH = pl.DeviceIdType.MESH
OFFSETS = np.array([[0, 0, 0], [1, 0, 0], [0, 1, 0], [0, 0, 1], [1, 1, 0], [1, 0, 1], [0, 1, 1], [1, 1, 1], [1, 1, -1], [1, -1, 1], [-1, 1, 1], [1, -1, 0], [1, 0, -1], [0, 1, -1]], np.int32)
LANES = 128
GROUP = 12
MAXCH = 32 * 32
SIZES = (8, 4, 4)


def ghost_boxes():
    need = {}
    for a in np.ndindex(2, 2, 2):
        for o in OFFSETS:
            b = [int(x) for x in np.array(a) + o]
            s = tuple(-1 if x < 0 else (1 if x > 1 else 0) for x in b)
            if any(s):
                need.setdefault(s, []).append([x - 2 * y for x, y in zip(b, s)])
    boxes = []
    for s in sorted(need, key=lambda s: (-len(set(map(tuple, need[s]))), s)):
        own = [(min(c[d] for c in need[s]), max(c[d] for c in need[s]) + 1) for d in range(3)]
        boxes.append((s, own, [(lo + 2 * s[d] + 1, hi + 2 * s[d] + 1) for d, (lo, hi) in enumerate(own)]))
    return boxes


BOXES = ghost_boxes()
N_BOX = len(BOXES)


def box(ref, ranges):
    return ref.at[tuple(pl.ds(lo, hi - lo) for lo, hi in ranges)]


def dot(a, b):
    return jnp.dot(a, b, preferred_element_type=F32)


def dot_nt(a, b):
    return lax.dot_general(a, b, (((1,), (1,)), ((), ())), preferred_element_type=F32)


def iota(shape, dim):
    return lax.broadcasted_iota(jnp.int32, shape, dim)


def position():
    return tuple(lax.axis_index(a) for a in ("gx", "gy", "gz"))


def shifted(me, s, sign):
    return tuple(lax.rem(m + sign * d + n, n) if d else m for m, d, n in zip(me, s, SIZES))


def greet(me, toward, line):
    barrier = pltpu.get_barrier_semaphore()
    for s, _, _ in BOXES:
        pl.semaphore_signal(barrier, inc=1, device_id=shifted(me, s, toward), device_id_type=MESH)
    for k in range(1, 16):
        pl.semaphore_signal(barrier, inc=1, device_id=plane_partner(me, k)[0], device_id_type=MESH)
    for k in range(1, 8 if line else 1):
        pl.semaphore_signal(barrier, inc=1, device_id=line_partner(me, k)[0], device_id_type=MESH)
    return N_BOX + 15 + (7 if line else 0)


def plane_partner(me, k):
    at = lax.rem(me[1] * 4 + me[2] + k, 16)
    return (me[0], at // 4, lax.rem(at, 4)), at


def line_partner(me, k):
    at = lax.rem(me[0] + k, 8)
    return (at, me[1], me[2]), at


def exchange(me, partner, count, rows, src, dst, send_sem, recv_sem):
    copies = []
    mine = me[0] if count == 8 else me[1] * 4 + me[2]
    here = pl.ds(pl.multiple_of(mine * rows, rows), rows)
    for k in range(1, count):
        device, at = partner(me, k)
        copy = pltpu.make_async_remote_copy(
            src_ref=src.at[pl.ds(pl.multiple_of(at * rows, rows), rows)],
            dst_ref=dst.at[here],
            send_sem=send_sem.at[k],
            recv_sem=recv_sem.at[k],
            device_id=device,
            device_id_type=MESH,
        )
        copy.start()
        copies.append(copy)
    dst[here] = src[here]
    return copies


def wait_all(copies):
    for copy in copies:
        copy.wait()


def placement(dest, ranks_apart):
    dest_f = dest.astype(F32)
    row = jnp.broadcast_to(dest_f, (128, LANES))
    col = jnp.transpose(row)
    earlier = jnp.logical_and(col == row, iota((128, 128), 1) < iota((128, 128), 0))
    rank = jnp.sum(jnp.where(earlier, 1.0, 0.0), axis=1, keepdims=True)
    dest_c = col[:, :1]
    gx = jnp.floor(dest_c * (1.0 / 16.0))
    order = (dest_c - 16.0 * gx) * 8.0 + gx
    place = order + 128.0 * rank if ranks_apart else 2.0 * order + rank
    lanes = iota((128, 256), 1).astype(F32)
    return jnp.where(lanes == place, 1.0, 0.0).astype(BF16)


def offset_of(code):
    out = []
    for d in range(3):
        v = 0
        for c, o in enumerate(OFFSETS):
            if o[d]:
                v = v + jnp.where(code == c, int(o[d]), 0)
        out.append(v)
    return out


def shift_rows(code, lanes):
    x, y, z = [(8 * v).astype(F32) for v in offset_of(code)]
    row = iota((8, lanes), 0)
    return jnp.where(row == 0, x, jnp.where(row == 1, y, jnp.where(row == 2, z, 0.0)))


def pair_cells(blk, b):
    a, code = blk[0, 0, b], blk[0, 1, b]
    x, y, z = offset_of(code)
    first = ((a // 4 + 1) * 4 + (a // 2) % 2 + 1) * 4 + a % 2 + 1
    return first, first + (x * 4 + y) * 4 + z, code


def halo_kernel(pos_in, emb, slot, dest, blk_in, proj, rw, bias, ew, cnt, gemb, held, g1, g2, rc, projt, rb, w2, blk, tot,
                pos, pos_v, emb_v, slot_v, dest_v, proj_v, rw_v, bias_v, ew_v, send1, recv1, loc, es, er, ps, pr, s1, r1):
    me = position()
    barrier = pltpu.get_barrier_semaphore()
    pos[...] = jnp.zeros_like(pos)
    partners = greet(me, 1, False)
    own = [(1, 3)] * 3
    local = []
    for i, (x, y) in enumerate(((pos_in, pos_v), (emb, emb_v), (slot, slot_v), (dest, dest_v), (blk_in, blk), (proj, proj_v), (rw, rw_v), (bias, bias_v), (ew, ew_v), (emb, box(gemb, own)))):
        local.append(pltpu.make_async_copy(x, y, loc.at[i]))
        local[-1].start()
    local[0].wait()
    for c in np.ndindex(2, 2, 2):
        pos[c[0] + 1, c[1] + 1, c[2] + 1, 0:3] = pos_v[c[0], c[1], :, c[2], :]
    pl.semaphore_wait(barrier, partners)
    halo = []
    for a, b, x, y in ((pos, pos, ps, pr), (emb, gemb, es, er)):
        copies = []
        for i, (s, src, dst) in enumerate(BOXES):
            start = box(a, [(lo + 1, hi + 1) for lo, hi in src]) if a is pos else box(a, src)
            copies.append(pltpu.make_async_remote_copy(src_ref=start, dst_ref=box(b, dst), send_sem=x.at[i], recv_sem=y.at[i], device_id=shifted(me, s, -1), device_id_type=MESH))
            copies[-1].start()
        halo.append(copies)
    for copy in local[1:]:
        copy.wait()
    where = placement(dest_v[...], False)
    pick = jnp.where(iota((512, 128), 0) == slot_v[...], 1.0, 0.0).astype(BF16)
    place = lax.dot_general(where, pick, (((0,), (1,)), ((), ())), preferred_element_type=F32).astype(BF16)
    send1[...] = dot(place, emb_v[...].reshape(512, 256)).astype(BF16)
    rows = exchange(me, plane_partner, 16, 16, send1, recv1, s1, r1)
    projt[...] = jnp.transpose(proj_v[...])
    half = 0.5 * bias_v[...]
    b1 = half.astype(BF16).astype(F32)
    b2 = (half - b1).astype(BF16).astype(F32)
    row8 = iota((8, 256), 0)
    biases = jnp.where(row8 == 0, b1, jnp.where(row8 == 1, b2, jnp.where(row8 == 2, half - b1 - b2, 0.0)))
    rwf = rw_v[...].astype(F32)
    ewf = ew_v[...].astype(F32).reshape(1, 256)
    rb[...] = jnp.transpose(jnp.concatenate([0.5 * rwf, biases, jnp.zeros((112, 256), F32)], axis=0)).astype(BF16)
    z8 = jnp.zeros((8, 256), F32)
    w2[:, :256] = jnp.concatenate([z8, jnp.where(row8 == 0, ewf, 0.0)], axis=0).astype(BF16)
    w2[:, 256:] = jnp.concatenate([0.5 * rwf * ewf, z8], axis=0).astype(BF16)

    jl = iota((64, 64), 1)
    il = iota((64, 64), 0)
    upper_b = jnp.where(il < jl, 1.0, 0.0).astype(BF16)
    lower_b = jnp.where(jl < il, 1.0, 0.0).astype(BF16)
    ones_b = jnp.ones((64, LANES), BF16)
    lane = iota((64, LANES), 1)

    def pos_at(c):
        return pos[c // 16, c // 4 % 4, c % 4]

    def prepare(b):
        ca, cb, code = pair_cells(blk, b)
        pa, pb = pos_at(ca), pos_at(cb)
        pbs = pb + shift_rows(code, 64)
        pat = jnp.transpose(pa)
        d2 = None
        for c in range(3):
            df = pbs[c:c + 1, :] - pat[:, c:c + 1]
            d2 = df * df if d2 is None else d2 + df * df
        keep = jnp.logical_and(d2 + 0.25 < 36.001, jnp.logical_or(code != 0, il < jl))
        keep = jnp.where(jnp.logical_and(keep, b < cnt[0]), 1.0, 0.0)
        keep_b = keep.astype(BF16)
        counts = dot(keep_b, ones_b)
        prefix = dot(keep_b, upper_b)
        start = dot(lower_b, counts.astype(BF16))
        rc[b, 0:64] = start
        rc[b, 64:72] = jnp.broadcast_to(start[63:64] + counts[63:64], (8, LANES))
        local = jnp.where(keep > 0.5, prefix, 255.0)
        hi = jnp.floor(start * (1.0 / 64.0)) * 64.0
        side = jnp.where(lane == 64, hi, jnp.where(lane == 65, start - hi, 0.0))
        zt = jnp.transpose(jnp.concatenate([local, side[:, 64:]], axis=1))[:72]
        ah = pa.astype(BF16).astype(F32)
        bh = pb.astype(BF16).astype(F32)
        g1[b] = jnp.concatenate([zt, ah, pa - ah, jnp.zeros((8, 64), F32)], axis=0).astype(BF16)
        g2[b] = jnp.concatenate([bh, pb - bh], axis=0).astype(BF16)
        tot[b] = jnp.sum(keep).astype(jnp.int32)
    wait_all(halo[0])

    def prep_group(g, c):
        for u in range(4):
            prepare(g * 4 + u)
        return c

    lax.fori_loop(0, 8, prep_group, 0)
    wait_all(rows)
    held[...] = recv1[...]
    wait_all(halo[1])


def sinpi_cospi(theta):
    m = jnp.round(theta)
    f = theta - m
    z = f * f
    sn = f * (3.14159265 + z * (-5.16771278 + z * (2.55016404 + z * (-0.599264529 + z * (0.0821458866 + z * -0.00737043094)))))
    cs = 1.0 + z * (-4.93480220 + z * (4.05871213 + z * (-1.33526277 + z * (0.235330630 + z * (-0.0258068913 + z * 0.00192957431)))))
    sign = 1.0 - 2.0 * (m - 2.0 * jnp.floor(0.5 * m))
    return sn * sign, cs * sign


def pair_kernel(blk, cnt, tot, gemb, g1, g2, rc, projt, rb, w2, out, wt, acc, tab_b, tab_k):
    def project(g, c):
        for u in range(4):
            ca, cb, _ = pair_cells(blk, g * 4 + u)
            both = jnp.concatenate([gemb[ca], gemb[cb]], axis=0)
            wt[g * 4 + u] = (dot_nt(projt[...], both).astype(BF16) * 0.5).astype(BF16)
        return c

    lax.fori_loop(0, (cnt[0] + 3) // 4, project, 0)

    def fill_block(b, n):
        def put(t, n):
            tab_b[n] = b
            tab_k[n] = t * LANES
            return n + 1

        return lax.fori_loop(0, (tot[b] + LANES - 1) // LANES, put, n)

    n = lax.fori_loop(0, cnt[0], fill_block, 0)
    for u in range(GROUP):
        tab_b[n + u] = 0
        tab_k[n + u] = 1 << 20

    acc[...] = jnp.zeros_like(acc)
    kl = iota((1, LANES), 1)
    sub = iota((8, LANES), 0)
    order = (sub + 1).astype(F32)
    ones_rows = jnp.where(sub < 3, 1.0, 0.0)
    halves = iota((8, LANES), 1) < 64

    def chunk_group(g, c):
        R = range(GROUP)
        ids = [g * GROUP + u for u in R]
        bs = [tab_b[x] for x in ids]
        ks = [(kl + tab_k[x]).astype(F32) for x in ids]
        oh_i = []
        for u in R:
            hit = jnp.logical_and(ks[u] >= rc[bs[u], 0:64], ks[u] < rc[bs[u], 1:65])
            oh_i.append(jnp.where(hit, 1.0, 0.0).astype(BF16))
        got = [dot(g1[bs[u]], oh_i[u]) for u in R]
        oh_j = []
        for u in R:
            want = ks[u] - got[u][64:65] - got[u][65:66]
            oh_j.append(jnp.where(got[u][:64] == want, 1.0, 0.0).astype(BF16))
        gotb = [dot(g2[bs[u]], oh_j[u]) for u in R]
        info = []
        xs = []
        for u in R:
            ca, cb, code = pair_cells(blk, bs[u])
            sep = (gotb[u][:8] + gotb[u][8:] + shift_rows(code, LANES)) - (got[u][72:80] + got[u][80:88])
            sq = sep * sep
            d2 = sq[0:1] + sq[1:2] + sq[2:3]
            s = jnp.sqrt(jnp.broadcast_to(d2, (8, LANES)) + 0.25) * (1.0 / 6.0)
            sn, cs = sinpi_cospi(order * s)
            e = jnp.where(s < 1.0, 1.0 - s * s, 0.0)
            info.append((ca, cb, sep, s, e, cs * order))
            x2 = jnp.concatenate([sn, ones_rows], axis=0).astype(BF16)
            xs.append(jnp.concatenate([oh_i[u], oh_j[u], x2, jnp.zeros((112, LANES), BF16)], axis=0))
        qs = [dot(jnp.concatenate([wt[bs[u]], rb[...]], axis=1), xs[u]) for u in R]
        hd = []
        for u in R:
            q = qs[u]
            t = jnp.tanh(q)
            h = q + q * t
            d = (1.0 + t) + h * (1.0 - t)
            hd.append(jnp.concatenate([h.astype(BF16), d.astype(BF16)], axis=0))
        rs = []
        for u in range(0, GROUP, 2):
            both = dot(w2[...], jnp.concatenate([hd[u], hd[u + 1]], axis=1))
            rs += [both[:, :LANES], both[:, LANES:]]
        fs = []
        for u in R:
            ca, cb, sep, s, e, cn = info[u]
            r = rs[u]
            terms = r[:8] * cn * (np.pi * e * e) + r[8:] * (-4.0 * s * e)
            ct = jnp.sum(terms, axis=0, keepdims=True)
            f = sep * (ct / (36.0 * s))
            fh = f.astype(BF16).astype(F32)
            fs.append(jnp.concatenate([fh, f - fh], axis=0).astype(BF16))
        for u in R:
            ca, cb = info[u][:2]
            both = dot_nt(fs[u], xs[u][:128])
            part = both[:8] + both[8:]
            acc[ca] += jnp.where(halves, part, 0.0)
            acc[cb] += jnp.where(halves, 0.0, part)
        return c

    lax.fori_loop(0, (n + GROUP - 1) // GROUP, chunk_group, 0)
    out[...] = (acc[:, :, :64] - acc[:, :, 64:]).reshape(4, 4, 4, 8, 64)


def return_kernel(fsum, pos_in, vel_in, slot, dest, held, forces, moved, embeds, pos_v, vel_v, slot_v, dest_v, landed, mot, send1, recv1, send2, recv2, esend, erecv, loc, fs, fr, s1, r1, s2, r2, s3, r3):
    me = position()
    barrier = pltpu.get_barrier_semaphore()
    partners = greet(me, -1, True)
    local = []
    for i, (x, y) in enumerate(((pos_in, pos_v), (vel_in, vel_v), (slot, slot_v), (dest, dest_v))):
        local.append(pltpu.make_async_copy(x, y, loc.at[i]))
        local[-1].start()
    mot[...] = jnp.zeros_like(mot)
    out = iota((256, 256), 0)
    want = ((out // 2) % 16) * 16 + (out // 32) * 2 + out % 2
    perm2 = jnp.where(iota((256, 256), 1) == want, 1.0, 0.0).astype(BF16)
    esend[...] = dot(perm2, held[...]).astype(BF16)
    out = iota((128, 128), 0)
    perm = jnp.where(iota((128, 128), 1) == (out % 16) * 8 + out // 16, 1.0, 0.0).astype(BF16)
    pl.semaphore_wait(barrier, partners)
    back = []
    for i, (s, own, ghost) in enumerate(BOXES):
        copy = pltpu.make_async_remote_copy(src_ref=box(fsum, ghost), dst_ref=box(landed.at[i], own), send_sem=fs.at[i], recv_sem=fr.at[i], device_id=shifted(me, s, 1), device_id_type=MESH)
        copy.start()
        back.append(copy)
    rows_sent = exchange(me, line_partner, 8, 32, esend, erecv, s3, r3)
    wait_all(local)
    where = placement(dest_v[...], True)
    pick = jnp.where(iota((512, 128), 0) == slot_v[...], 1.0, 0.0).astype(BF16)
    place = dot(pick, where).astype(BF16)
    wait_all(back)
    for c in np.ndindex(2, 2, 2):
        total = fsum[c[0] + 1, c[1] + 1, c[2] + 1]
        for i, (s, own, ghost) in enumerate(BOXES):
            if all(lo <= x < hi for x, (lo, hi) in zip(c, own)):
                total = total + landed[i, c[0], c[1], c[2]]
        forces[c[0], c[1], c[2]] = total
        new_velocity = vel_v[c[0], c[1], :, c[2], :] + 0.5 * total[:3]
        new_position = pos_v[c[0], c[1], :, c[2], :] + 0.5 * new_velocity
        at = (c[0] * 4 + c[1] * 2 + c[2]) * 64
        mot[0:3, at:at + 64] = new_position
        mot[8:11, at:at + 64] = new_velocity
    rows = dot(mot[...].astype(BF16), place)
    tall = jnp.concatenate([rows[:, :128], rows[:, 128:], jnp.zeros((96, 128), F32)], axis=0)
    send1[...] = jnp.transpose(tall)
    wait_all(exchange(me, plane_partner, 16, 8, send1, recv1, s1, r1))
    send2[...] = dot(perm, recv1[...].astype(BF16))
    last = exchange(me, line_partner, 8, 16, send2, recv2, s2, r2)
    wait_all(rows_sent)
    embeds[...] = erecv[...]
    wait_all(last)
    moved[...] = jnp.transpose(recv2[...])[:32]


def finish_kernel(forces, moved, embeds, forces_out, motion_out, embeds_out):
    for c in np.ndindex(2, 2, 2):
        forces_out[c[0], c[1], :, c[2], :] = forces[c[0], c[1], c[2]][:3]
    for v in range(6):
        for h in range(2):
            at = 16 * h + 8 * (v // 3) + v % 3
            motion_out[v, h:h + 1, :] = moved[at:at + 1, :]
    embeds_out[...] = embeds[...].reshape(128, 2, 256)


def per_device(positions, velocity, atom_embed, embed_proj, radial_weight, latent_bias, energy_weight, block_list, block_count, move_slot, move_dest):
    any_, vmem, smem, hbm = (pl.BlockSpec(memory_space=m) for m in (pl.ANY, pltpu.VMEM, pltpu.SMEM, pltpu.HBM))
    dma = pltpu.SemaphoreType.DMA
    array = jax.ShapeDtypeStruct
    pos_rows, vel_rows = (x.transpose(0, 1, 3, 2, 4) for x in (positions, velocity))
    dest_row = move_dest.reshape(1, 128)
    spaces = pltpu.VMEM((2, 2, 3, 2, 64), F32)
    gemb, held, g1, g2, rc, projt, rb, w2, blk, tot = pl.pallas_call(
        halo_kernel,
        out_shape=(
            array((4, 4, 4, 64, 256), BF16),
            array((256, 256), BF16),
            array((32, 96, 64), BF16),
            array((32, 16, 64), BF16),
            array((32, 72, LANES), F32),
            array((256, 256), BF16),
            array((256, 128), BF16),
            array((16, 512), BF16),
            array((1, 2, 32), jnp.int32),
            array((32,), jnp.int32),
        ),
        in_specs=[hbm] * 9 + [smem],
        out_specs=(any_,) + (vmem,) * 7 + (smem,) * 2,
        scratch_shapes=[
            pltpu.VMEM((4, 4, 4, 8, 64), F32),
            spaces,
            pltpu.VMEM((2, 2, 2, 64, 256), BF16),
            pltpu.VMEM((1, 128), jnp.int32),
            pltpu.VMEM((1, 128), jnp.int32),
            pltpu.VMEM((256, 256), BF16),
            pltpu.VMEM((8, 256), BF16),
            pltpu.VMEM((1, 256), F32),
            pltpu.VMEM((256,), BF16),
            pltpu.VMEM((256, 256), BF16),
            pltpu.VMEM((256, 256), BF16),
        ]
        + [dma((10,))] + [dma((N_BOX,))] * 4 + [dma((16,))] * 2,
        compiler_params=pltpu.CompilerParams(collective_id=0, has_side_effects=True, vmem_limit_bytes=16 * 1024 * 1024),
        name="halo",
    )(*(pltpu.with_memory_space_constraint(x, pltpu.HBM) for x in (pos_rows, atom_embed, move_slot, dest_row, block_list, embed_proj, radial_weight, latent_bias.reshape(1, 256), energy_weight)), block_count)
    fsum = pl.pallas_call(
        pair_kernel,
        out_shape=array((4, 4, 4, 8, 64), F32),
        in_specs=[smem] * 3 + [vmem] * 7,
        out_specs=vmem,
        scratch_shapes=[
            pltpu.VMEM((32, 256, 128), BF16),
            pltpu.VMEM((64, 8, LANES), F32),
            pltpu.SMEM((MAXCH + GROUP,), jnp.int32),
            pltpu.SMEM((MAXCH + GROUP,), jnp.int32),
        ],
        compiler_params=pltpu.CompilerParams(vmem_limit_bytes=24 * 1024 * 1024),
        name="pairs",
    )(blk, block_count, tot, gemb.reshape(64, 64, 256), g1, g2, rc, projt, rb, w2)
    raw = pl.pallas_call(
        return_kernel,
        out_shape=(array((2, 2, 2, 8, 64), F32), array((32, LANES), F32), array((256, 256), BF16)),
        in_specs=[vmem] + [hbm] * 4 + [vmem],
        out_specs=(vmem,) * 3,
        scratch_shapes=[spaces, spaces, pltpu.VMEM((1, 128), jnp.int32), pltpu.VMEM((1, 128), jnp.int32)]
        + [pltpu.VMEM((N_BOX, 2, 2, 2, 8, 64), F32), pltpu.VMEM((16, 512), F32)]
        + [pltpu.VMEM((128, LANES), F32)] * 4
        + [pltpu.VMEM((256, 256), BF16)] * 2
        + [dma((4,))] + [dma((N_BOX,))] * 2 + [dma((16,))] * 2 + [dma((8,))] * 4,
        compiler_params=pltpu.CompilerParams(collective_id=1, has_side_effects=True, vmem_limit_bytes=16 * 1024 * 1024),
        name="give_back",
    )(fsum, *(pltpu.with_memory_space_constraint(x, pltpu.HBM) for x in (pos_rows, vel_rows, move_slot, dest_row)), held)
    forces, motion, embeds = pl.pallas_call(
        finish_kernel,
        out_shape=(array((2, 2, 3, 2, 64), F32), array((6, 2, 128), F32), array((128, 2, 256), BF16)),
        in_specs=[vmem] * 3,
        out_specs=(vmem,) * 3,
        name="finish",
    )(*raw)
    return forces.transpose(0, 1, 3, 2, 4), motion.transpose(2, 1, 0), embeds


def solution(mesh):
    placed = (
        P("gx", "gy", "gz", None, None),
        P("gx", "gy", "gz", None, None),
        P("gx", "gy", "gz", None, None),
        P(),
        P(),
        P(),
        P(),
        P(("gx", "gy", "gz"), None, None),
        P(("gx", "gy", "gz")),
        P(("gx", "gy", "gz"), None),
        P(("gx", "gy", "gz"), None),
    )
    return jax.shard_map(
        per_device,
        mesh=mesh,
        in_specs=placed,
        out_specs=(
            P("gx", "gy", "gz", None, None),
            P(("gx", "gy", "gz"), None, None),
            P(("gx", "gy", "gz"), None, None),
        ),
        check_vma=False,
    )
```

time: 89.7 us -> 68.6 us (0.76)
  Pallas kernels: 77.8 us -> 65.2 us
  local copies, waits for them, and re-layouts: 10.2 us -> 1.84 us
    pallas_call x3 -> x4, Pallas kernels: 77.8 us -> 65.2 us  [the longest x1 31 us: per_device(): pl.pallas_call(return_kernel, out_shape=(array((2, 2, 2, 8, 64), F32), ar...]
    unnamed x24 -> x6, local copies, waits for them, and re-layouts: 8.13 us -> 1.84 us
    reshape x2 -> x0, local copies, waits for them, and re-layouts: 1.37 us -> none  [the longest x1 0.71 us: per_device(): return (forces[..., :3, :], motion, got_embed.reshape(128, 2, 256))]
where the time goes in v3:
time: 68.6 us; the launch traced here: 68.3 us
  Pallas kernels  65.2 us (95%)
  local copies, waits for them, and re-layouts  1.84 us (3%)
  between operations  1.31 us (2%)
    pallas_call x1, Pallas kernels, per_device(): pl.pallas_call(return_kernel, out_shape=(array((2, 2, 2, 8, 64), F32), ar...  31 us
    pallas_call x1, Pallas kernels, per_device(): pl.pallas_call(halo_kernel, out_shape=(array((4, 4, 4, 64, 256), BF16), a...  25.9 us
    pallas_call x1, Pallas kernels, per_device(): pl.pallas_call(pair_kernel, out_shape=array((4, 4, 4, 8, 64), F32), in_sp...  6.68 us
    unnamed x6, local copies, waits for them, and re-layouts  1.84 us
    pallas_call x1, Pallas kernels, per_device(): pl.pallas_call(finish_kernel, out_shape=(array((2, 2, 3, 2, 64), F32), ar...  1.65 us

profile of v3, /device:TPU:1, one launch (start us, length us, event | category | flops | bytes accessed | tf_op | source)
XLA Modules:
  0.0 68.3 jit_solution(8058486259647685110)
XLA Ops:
  1.3 25.9 %halo.1 = (bf16[4,4,4,64,256]{4,3,2,1,0:T(8,128)(2,1)S(1)}, bf16[256,256]{1,0:T(8,128)(2,1)S(1)}, bf16[32,96,64]{2,1,0:T(8,128)(2,1)S(1)}, bf16[32,16,64]{2,1,0:...) custom-call(f32[2,2,3,2,64]{4,3,2,1,0:T(2,128)} %bitcast.8, ...), custom_call_target="tpu_custom_call" | custom-call | tf_op jit(solution)/shard_map/halo/pallas_call | solution.py:407
  27.2 6.7 %pairs.1.fsum = f32[4,4,4,8,64]{4,3,2,1,0:T(8,128)S(1)} custom-call(s32[1,2,32]{2,1,0:T(2,128)S(1)} %get-tuple-element.19.blk, s32[1]{0:T(128)S(6)} %copy.14.cnt, s32[32]{0:T(128)S(1)} %get-tuple-element.20.tot, bf16[64,64,256]{2,1,0:T(8,128)(2,1)S(1)} %bitcast.7, bf16[32,96,64]{2,1,0:T(8,128)(2,1)S(1)} %get-tuple-element.22.g1, ...), custom_call_target="tpu_custom_call" | custom-call | tf_op jit(solution)/shard_map/pairs/pallas_call | solution.py:440
  33.8 31.0 %give_back.1 = (f32[2,2,2,8,64]{4,3,2,1,0:T(8,128)S(1)}, f32[32,128]{1,0:T(8,128)S(1)}, bf16[256,256]{1,0:T(8,128)(2,1)S(1)}) custom-call(f32[4,4,4,8,64]{4,3,2,1,0:T(8,128)S(1)} %pairs.1.fsum, f32[2,2,3,2,64]{4,3,2,1,0:T(2,128)} %bitcast.9, f32[2,2,3,2,64]{4,3,2,1,0:T(2,128)} %bitcast.10, s32[1,128]{1,0:T(1,128)} %slot.3, s32[1,128]{1,0:T(1,128)} %bitcast.12, ...), custom_call_target="tpu_custom_call" | custom-call | tf_op jit(solution)/shard_map/give_back/pallas_call | solution.py:454
  64.8 0.0 copy-start
  64.9 0.6 copy-done
  65.5 0.0 copy-start.1
  65.5 0.6 copy-done.1
  66.1 0.0 copy-start.2
  66.1 0.6 copy-done.2
  66.7 1.7 %finish.1 = (f32[2,2,3,2,64]{4,3,2,1,0:T(2,128)}, f32[6,2,128]{2,1,0:T(2,128)}, bf16[128,2,256]{2,1,0:T(2,128)(2,1)}) custom-call(f32[2,2,2,8,64]{4,3,2,1,0:T(8,128)} %copy-done.1, f32[32,128]{1,0:T(8,128)} %copy-done.2, bf16[256,256]{1,0:T(8,128)(2,1)} %copy-done), custom_call_target="tpu_custom_call" | custom-call | tf_op jit(solution)/shard_map/finish/pallas_call | solution.py:467
Async XLA Ops:
  64.8 0.6 copy-start
  65.5 0.6 copy-start.1
  66.1 0.6 copy-start.2

commit v4 on v3

--- a/solution.py
+++ b/solution.py
@@ -13,6 +13,7 @@
 OFFSETS = np.array([[0, 0, 0], [1, 0, 0], [0, 1, 0], [0, 0, 1], [1, 1, 0], [1, 0, 1], [0, 1, 1], [1, 1, 1], [1, 1, -1], [1, -1, 1], [-1, 1, 1], [1, -1, 0], [1, 0, -1], [0, 1, -1]], np.int32)
 LANES = 128
 GROUP = 12
+CHUNK = 128
 MAXCH = 32 * 32
 SIZES = (8, 4, 4)
 
@@ -26,7 +27,7 @@
             if any(s):
                 need.setdefault(s, []).append([x - 2 * y for x, y in zip(b, s)])
     boxes = []
-    for s in sorted(need, key=lambda s: (-len(set(map(tuple, need[s]))), s)):
+    for s in sorted(need, key=lambda s: (-s[0], -len(set(map(tuple, need[s]))), s)):
         own = [(min(c[d] for c in need[s]), max(c[d] for c in need[s]) + 1) for d in range(3)]
         boxes.append((s, own, [(lo + 2 * s[d] + 1, hi + 2 * s[d] + 1) for d, (lo, hi) in enumerate(own)]))
     return boxes
@@ -120,35 +121,20 @@
     return jnp.where(lanes == place, 1.0, 0.0).astype(BF16)
 
 
-def offset_of(code):
-    out = []
-    for d in range(3):
-        v = 0
-        for c, o in enumerate(OFFSETS):
-            if o[d]:
-                v = v + jnp.where(code == c, int(o[d]), 0)
-        out.append(v)
-    return out
-
-
-def shift_rows(code, lanes):
-    x, y, z = [(8 * v).astype(F32) for v in offset_of(code)]
+def shift_rows(offset, lanes):
+    x, y, z = [(8 * v).astype(F32) for v in offset]
     row = iota((8, lanes), 0)
     return jnp.where(row == 0, x, jnp.where(row == 1, y, jnp.where(row == 2, z, 0.0)))
 
 
-def pair_cells(blk, b):
-    a, code = blk[0, 0, b], blk[0, 1, b]
-    x, y, z = offset_of(code)
-    first = ((a // 4 + 1) * 4 + (a // 2) % 2 + 1) * 4 + a % 2 + 1
-    return first, first + (x * 4 + y) * 4 + z, code
-
-
-def halo_kernel(pos_in, emb, slot, dest, blk_in, proj, rw, bias, ew, cnt, gemb, held, g1, g2, rc, projt, rb, w2, blk, tot,
-                pos, pos_v, emb_v, slot_v, dest_v, proj_v, rw_v, bias_v, ew_v, send1, recv1, loc, es, er, ps, pr, s1, r1):
+def halo_kernel(pos_in, emb, slot, dest, blk_in, proj, rw, bias, ew, cnt, gemb, held, g1, g2, rc, projt, rb, w2, plan, tot,
+                pos, pos_v, emb_v, slot_v, dest_v, proj_v, rw_v, bias_v, ew_v, send1, recv1, blk, offs, loc, es, er, ps, pr, s1, r1):
     me = position()
     barrier = pltpu.get_barrier_semaphore()
     pos[...] = jnp.zeros_like(pos)
+    for c, o in enumerate(OFFSETS):
+        for d in range(3):
+            offs[d, c] = int(o[d])
     partners = greet(me, 1, False)
     own = [(1, 3)] * 3
     local = []
@@ -157,7 +143,7 @@
         local[-1].start()
     local[0].wait()
     for c in np.ndindex(2, 2, 2):
-        pos[c[0] + 1, c[1] + 1, c[2] + 1, 0:3] = pos_v[c[0], c[1], :, c[2], :]
+        pos[c[0] + 1, c[1] + 1, c[2] + 1, 0:3, 0:64] = pos_v[c[0], c[1], :, c[2], :]
     pl.semaphore_wait(barrier, partners)
     halo = []
     for a, b, x, y in ((pos, pos, ps, pr), (emb, gemb, es, er)):
@@ -195,12 +181,18 @@
     lane = iota((64, LANES), 1)
 
     def pos_at(c):
-        return pos[c // 16, c // 4 % 4, c % 4]
+        return pos[c // 16, c // 4 % 4, c % 4][:, :64]
 
     def prepare(b):
-        ca, cb, code = pair_cells(blk, b)
+        a, code = blk[0, 0, b], blk[0, 1, b]
+        off = [offs[d, code] for d in range(3)]
+        ca = ((a // 4 + 1) * 4 + (a // 2) % 2 + 1) * 4 + a % 2 + 1
+        cb = ca + (off[0] * 4 + off[1]) * 4 + off[2]
+        plan[0, b] = ca
+        plan[1, b] = cb
+        sh = shift_rows(off, 64)
         pa, pb = pos_at(ca), pos_at(cb)
-        pbs = pb + shift_rows(code, 64)
+        pbs = pb + sh
         pat = jnp.transpose(pa)
         d2 = None
         for c in range(3):
@@ -213,15 +205,16 @@
         prefix = dot(keep_b, upper_b)
         start = dot(lower_b, counts.astype(BF16))
         rc[b, 0:64] = start
-        rc[b, 64:72] = jnp.broadcast_to(start[63:64] + counts[63:64], (8, LANES))
+        rc[b, 64:128] = start + counts
         local = jnp.where(keep > 0.5, prefix, 255.0)
         hi = jnp.floor(start * (1.0 / 64.0)) * 64.0
         side = jnp.where(lane == 64, hi, jnp.where(lane == 65, start - hi, 0.0))
         zt = jnp.transpose(jnp.concatenate([local, side[:, 64:]], axis=1))[:72]
         ah = pa.astype(BF16).astype(F32)
         bh = pb.astype(BF16).astype(F32)
+        far = jnp.concatenate([sh, jnp.zeros_like(sh)], axis=0)
         g1[b] = jnp.concatenate([zt, ah, pa - ah, jnp.zeros((8, 64), F32)], axis=0).astype(BF16)
-        g2[b] = jnp.concatenate([bh, pb - bh], axis=0).astype(BF16)
+        g2[b] = jnp.concatenate([bh, pb - bh, far], axis=0).astype(BF16)
         tot[b] = jnp.sum(keep).astype(jnp.int32)
     wait_all(halo[0])
 
@@ -246,12 +239,15 @@
     return sn * sign, cs * sign
 
 
-def pair_kernel(blk, cnt, tot, gemb, g1, g2, rc, projt, rb, w2, out, wt, acc, tab_b, tab_k):
+def pair_kernel(plan, cnt, tot, gemb, g1, g2, rc, projt, rb, w2, out, wt, acc, tab_b, tab_k):
     def project(g, c):
+        four = []
         for u in range(4):
-            ca, cb, _ = pair_cells(blk, g * 4 + u)
-            both = jnp.concatenate([gemb[ca], gemb[cb]], axis=0)
-            wt[g * 4 + u] = (dot_nt(projt[...], both).astype(BF16) * 0.5).astype(BF16)
+            four += [gemb[plan[0, g * 4 + u]], gemb[plan[1, g * 4 + u]]]
+        for u in (0, 2):
+            both = (dot_nt(projt[...], jnp.concatenate(four[2 * u:2 * u + 4], axis=0)).astype(BF16) * 0.5).astype(BF16)
+            wt[g * 4 + u] = both[:, :LANES]
+            wt[g * 4 + u + 1] = both[:, LANES:]
         return c
 
     lax.fori_loop(0, (cnt[0] + 3) // 4, project, 0)
@@ -259,10 +255,10 @@
     def fill_block(b, n):
         def put(t, n):
             tab_b[n] = b
-            tab_k[n] = t * LANES
+            tab_k[n] = t * CHUNK
             return n + 1
 
-        return lax.fori_loop(0, (tot[b] + LANES - 1) // LANES, put, n)
+        return lax.fori_loop(0, (tot[b] + CHUNK - 1) // CHUNK, put, n)
 
     n = lax.fori_loop(0, cnt[0], fill_block, 0)
     for u in range(GROUP):
@@ -270,20 +266,22 @@
         tab_k[n + u] = 1 << 20
 
     acc[...] = jnp.zeros_like(acc)
-    kl = iota((1, LANES), 1)
-    sub = iota((8, LANES), 0)
+    kl = iota((1, CHUNK), 1)
+    sub = iota((8, CHUNK), 0)
     order = (sub + 1).astype(F32)
     ones_rows = jnp.where(sub < 3, 1.0, 0.0)
     halves = iota((8, LANES), 1) < 64
 
+    def wide(x):
+        return jnp.concatenate([x] * (CHUNK // LANES), axis=1)
+
     def chunk_group(g, c):
         R = range(GROUP)
-        ids = [g * GROUP + u for u in R]
-        bs = [tab_b[x] for x in ids]
-        ks = [(kl + tab_k[x]).astype(F32) for x in ids]
+        bs = [tab_b[g * GROUP + u] for u in R]
+        ks = [(kl + tab_k[g * GROUP + u]).astype(F32) for u in R]
         oh_i = []
         for u in R:
-            hit = jnp.logical_and(ks[u] >= rc[bs[u], 0:64], ks[u] < rc[bs[u], 1:65])
+            hit = jnp.logical_and(ks[u] >= wide(rc[bs[u], 0:64]), ks[u] < wide(rc[bs[u], 64:128]))
             oh_i.append(jnp.where(hit, 1.0, 0.0).astype(BF16))
         got = [dot(g1[bs[u]], oh_i[u]) for u in R]
         oh_j = []
@@ -294,16 +292,15 @@
         info = []
         xs = []
         for u in R:
-            ca, cb, code = pair_cells(blk, bs[u])
-            sep = (gotb[u][:8] + gotb[u][8:] + shift_rows(code, LANES)) - (got[u][72:80] + got[u][80:88])
+            sep = (gotb[u][:8] + gotb[u][8:16] + gotb[u][16:24]) - (got[u][72:80] + got[u][80:88])
             sq = sep * sep
             d2 = sq[0:1] + sq[1:2] + sq[2:3]
-            s = jnp.sqrt(jnp.broadcast_to(d2, (8, LANES)) + 0.25) * (1.0 / 6.0)
+            s = jnp.sqrt(jnp.broadcast_to(d2, (8, CHUNK)) + 0.25) * (1.0 / 6.0)
             sn, cs = sinpi_cospi(order * s)
             e = jnp.where(s < 1.0, 1.0 - s * s, 0.0)
-            info.append((ca, cb, sep, s, e, cs * order))
+            info.append((sep, s, e, cs * order))
             x2 = jnp.concatenate([sn, ones_rows], axis=0).astype(BF16)
-            xs.append(jnp.concatenate([oh_i[u], oh_j[u], x2, jnp.zeros((112, LANES), BF16)], axis=0))
+            xs.append(jnp.concatenate([oh_i[u], oh_j[u], x2, jnp.zeros((112, CHUNK), BF16)], axis=0))
         qs = [dot(jnp.concatenate([wt[bs[u]], rb[...]], axis=1), xs[u]) for u in R]
         hd = []
         for u in R:
@@ -315,26 +312,24 @@
         rs = []
         for u in range(0, GROUP, 2):
             both = dot(w2[...], jnp.concatenate([hd[u], hd[u + 1]], axis=1))
-            rs += [both[:, :LANES], both[:, LANES:]]
+            rs += [both[:, :CHUNK], both[:, CHUNK:]]
         fs = []
         for u in R:
-            ca, cb, sep, s, e, cn = info[u]
-            r = rs[u]
-            terms = r[:8] * cn * (np.pi * e * e) + r[8:] * (-4.0 * s * e)
+            sep, s, e, cn = info[u]
+            terms = rs[u][:8] * cn * (np.pi * e * e) + rs[u][8:] * (-4.0 * s * e)
             ct = jnp.sum(terms, axis=0, keepdims=True)
             f = sep * (ct / (36.0 * s))
             fh = f.astype(BF16).astype(F32)
             fs.append(jnp.concatenate([fh, f - fh], axis=0).astype(BF16))
         for u in R:
-            ca, cb = info[u][:2]
             both = dot_nt(fs[u], xs[u][:128])
             part = both[:8] + both[8:]
-            acc[ca] += jnp.where(halves, part, 0.0)
-            acc[cb] += jnp.where(halves, 0.0, part)
+            acc[plan[0, bs[u]]] += jnp.where(halves, part, 0.0)
+            acc[plan[1, bs[u]]] += jnp.where(halves, 0.0, part)
         return c
 
     lax.fori_loop(0, (n + GROUP - 1) // GROUP, chunk_group, 0)
-    out[...] = (acc[:, :, :64] - acc[:, :, 64:]).reshape(4, 4, 4, 8, 64)
+    out[...] = (acc[...] - jnp.roll(acc[...], 64, axis=2)).reshape(4, 4, 4, 8, LANES)
 
 
 def return_kernel(fsum, pos_in, vel_in, slot, dest, held, forces, moved, embeds, pos_v, vel_v, slot_v, dest_v, landed, mot, send1, recv1, send2, recv2, esend, erecv, loc, fs, fr, s1, r1, s2, r2, s3, r3):
@@ -346,18 +341,18 @@
         local.append(pltpu.make_async_copy(x, y, loc.at[i]))
         local[-1].start()
     mot[...] = jnp.zeros_like(mot)
+    pl.semaphore_wait(barrier, partners)
+    back = []
+    for i, (s, own, ghost) in enumerate(BOXES):
+        copy = pltpu.make_async_remote_copy(src_ref=box(fsum, ghost), dst_ref=box(landed.at[i], own), send_sem=fs.at[i], recv_sem=fr.at[i], device_id=shifted(me, s, 1), device_id_type=MESH)
+        copy.start()
+        back.append(copy)
     out = iota((256, 256), 0)
     want = ((out // 2) % 16) * 16 + (out // 32) * 2 + out % 2
     perm2 = jnp.where(iota((256, 256), 1) == want, 1.0, 0.0).astype(BF16)
     esend[...] = dot(perm2, held[...]).astype(BF16)
     out = iota((128, 128), 0)
     perm = jnp.where(iota((128, 128), 1) == (out % 16) * 8 + out // 16, 1.0, 0.0).astype(BF16)
-    pl.semaphore_wait(barrier, partners)
-    back = []
-    for i, (s, own, ghost) in enumerate(BOXES):
-        copy = pltpu.make_async_remote_copy(src_ref=box(fsum, ghost), dst_ref=box(landed.at[i], own), send_sem=fs.at[i], recv_sem=fr.at[i], device_id=shifted(me, s, 1), device_id_type=MESH)
-        copy.start()
-        back.append(copy)
     rows_sent = exchange(me, line_partner, 8, 32, esend, erecv, s3, r3)
     wait_all(local)
     where = placement(dest_v[...], True)
@@ -370,7 +365,7 @@
             if all(lo <= x < hi for x, (lo, hi) in zip(c, own)):
                 total = total + landed[i, c[0], c[1], c[2]]
         forces[c[0], c[1], c[2]] = total
-        new_velocity = vel_v[c[0], c[1], :, c[2], :] + 0.5 * total[:3]
+        new_velocity = vel_v[c[0], c[1], :, c[2], :] + 0.5 * total[:3, :64]
         new_position = pos_v[c[0], c[1], :, c[2], :] + 0.5 * new_velocity
         at = (c[0] * 4 + c[1] * 2 + c[2]) * 64
         mot[0:3, at:at + 64] = new_position
@@ -389,7 +384,7 @@
 
 def finish_kernel(forces, moved, embeds, forces_out, motion_out, embeds_out):
     for c in np.ndindex(2, 2, 2):
-        forces_out[c[0], c[1], :, c[2], :] = forces[c[0], c[1], c[2]][:3]
+        forces_out[c[0], c[1], :, c[2], :] = forces[c[0], c[1], c[2]][:3, :64]
     for v in range(6):
         for h in range(2):
             at = 16 * h + 8 * (v // 3) + v % 3
@@ -404,24 +399,24 @@
     pos_rows, vel_rows = (x.transpose(0, 1, 3, 2, 4) for x in (positions, velocity))
     dest_row = move_dest.reshape(1, 128)
     spaces = pltpu.VMEM((2, 2, 3, 2, 64), F32)
-    gemb, held, g1, g2, rc, projt, rb, w2, blk, tot = pl.pallas_call(
+    gemb, held, g1, g2, rc, projt, rb, w2, plan, tot = pl.pallas_call(
         halo_kernel,
         out_shape=(
             array((4, 4, 4, 64, 256), BF16),
             array((256, 256), BF16),
             array((32, 96, 64), BF16),
-            array((32, 16, 64), BF16),
-            array((32, 72, LANES), F32),
+            array((32, 32, 64), BF16),
+            array((32, 128, LANES), F32),
             array((256, 256), BF16),
             array((256, 128), BF16),
             array((16, 512), BF16),
-            array((1, 2, 32), jnp.int32),
+            array((2, 32), jnp.int32),
             array((32,), jnp.int32),
         ),
         in_specs=[hbm] * 9 + [smem],
         out_specs=(any_,) + (vmem,) * 7 + (smem,) * 2,
         scratch_shapes=[
-            pltpu.VMEM((4, 4, 4, 8, 64), F32),
+            pltpu.VMEM((4, 4, 4, 8, LANES), F32),
             spaces,
             pltpu.VMEM((2, 2, 2, 64, 256), BF16),
             pltpu.VMEM((1, 128), jnp.int32),
@@ -432,6 +427,8 @@
             pltpu.VMEM((256,), BF16),
             pltpu.VMEM((256, 256), BF16),
             pltpu.VMEM((256, 256), BF16),
+            pltpu.SMEM((1, 2, 32), jnp.int32),
+            pltpu.SMEM((3, 16), jnp.int32),
         ]
         + [dma((10,))] + [dma((N_BOX,))] * 4 + [dma((16,))] * 2,
         compiler_params=pltpu.CompilerParams(collective_id=0, has_side_effects=True, vmem_limit_bytes=16 * 1024 * 1024),
@@ -439,7 +436,7 @@
     )(*(pltpu.with_memory_space_constraint(x, pltpu.HBM) for x in (pos_rows, atom_embed, move_slot, dest_row, block_list, embed_proj, radial_weight, latent_bias.reshape(1, 256), energy_weight)), block_count)
     fsum = pl.pallas_call(
         pair_kernel,
-        out_shape=array((4, 4, 4, 8, 64), F32),
+        out_shape=array((4, 4, 4, 8, LANES), F32),
         in_specs=[smem] * 3 + [vmem] * 7,
         out_specs=vmem,
         scratch_shapes=[
@@ -450,14 +447,14 @@
         ],
         compiler_params=pltpu.CompilerParams(vmem_limit_bytes=24 * 1024 * 1024),
         name="pairs",
-    )(blk, block_count, tot, gemb.reshape(64, 64, 256), g1, g2, rc, projt, rb, w2)
+    )(plan, block_count, tot, gemb.reshape(64, 64, 256), g1, g2, rc, projt, rb, w2)
     raw = pl.pallas_call(
         return_kernel,
-        out_shape=(array((2, 2, 2, 8, 64), F32), array((32, LANES), F32), array((256, 256), BF16)),
+        out_shape=(array((2, 2, 2, 8, LANES), F32), array((32, LANES), F32), array((256, 256), BF16)),
         in_specs=[vmem] + [hbm] * 4 + [vmem],
         out_specs=(vmem,) * 3,
         scratch_shapes=[spaces, spaces, pltpu.VMEM((1, 128), jnp.int32), pltpu.VMEM((1, 128), jnp.int32)]
-        + [pltpu.VMEM((N_BOX, 2, 2, 2, 8, 64), F32), pltpu.VMEM((16, 512), F32)]
+        + [pltpu.VMEM((N_BOX, 2, 2, 2, 8, LANES), F32), pltpu.VMEM((16, 512), F32)]
         + [pltpu.VMEM((128, LANES), F32)] * 4
         + [pltpu.VMEM((256, 256), BF16)] * 2
         + [dma((4,))] + [dma((N_BOX,))] * 2 + [dma((16,))] * 2 + [dma((8,))] * 4,
@@ -469,6 +466,7 @@
         out_shape=(array((2, 2, 3, 2, 64), F32), array((6, 2, 128), F32), array((128, 2, 256), BF16)),
         in_specs=[vmem] * 3,
         out_specs=(vmem,) * 3,
+        compiler_params=pltpu.CompilerParams(vmem_limit_bytes=8 * 1024 * 1024),
         name="finish",
     )(*raw)
     return forces.transpose(0, 1, 3, 2, 4), motion.transpose(2, 1, 0), embeds

time: 68.6 us -> 62.9 us (0.917)
  Pallas kernels: 65.2 us -> 61.3 us
  local copies, waits for them, and re-layouts: 1.84 us -> 0 us
    pallas_call x2, Pallas kernels: 37.7 us -> 34.2 us  [the longest x1 25.6 us: per_device(): pl.pallas_call(return_kernel, out_shape=(array((2, 2, 2, 8, LANES), F32),...]
    unnamed x6 -> x0, local copies, waits for them, and re-layouts: 1.84 us -> none
    pallas_call x1, Pallas kernels: 1.65 us -> 0.71 us  [per_device(): pl.pallas_call(finish_kernel, out_shape=(array((2, 2, 3, 2, 64), F32), ar...]
where the time goes in v4:
time: 62.9 us; the launch traced here: 62.6 us
  Pallas kernels  61.3 us (97%)
  between operations  1.3 us (2%)
    pallas_call x1, Pallas kernels, per_device(): pl.pallas_call(halo_kernel, out_shape=(array((4, 4, 4, 64, 256), BF16), a...  26.4 us
    pallas_call x1, Pallas kernels, per_device(): pl.pallas_call(return_kernel, out_shape=(array((2, 2, 2, 8, LANES), F32),...  25.6 us
    pallas_call x1, Pallas kernels, per_device(): pl.pallas_call(pair_kernel, out_shape=array((4, 4, 4, 8, LANES), F32), in...  8.59 us

profile of v4, /device:TPU:1, one launch (start us, length us, event | category | flops | bytes accessed | tf_op | source)
XLA Modules:
  0.0 62.6 jit_solution(11508871025103525714)
XLA Ops:
  1.3 26.4 %halo.1 = (bf16[4,4,4,64,256]{4,3,2,1,0:T(8,128)(2,1)S(1)}, bf16[256,256]{1,0:T(8,128)(2,1)S(1)}, bf16[32,96,64]{2,1,0:T(8,128)(2,1)S(1)}, bf16[32,32,64]{2,1,0:...) custom-call(f32[2,2,3,2,64]{4,3,2,1,0:T(2,128)} %bitcast.8, ...), custom_call_target="tpu_custom_call" | custom-call | tf_op jit(solution)/shard_map/halo/pallas_call | solution.py:402
  27.7 8.6 %pairs.1.fsum = f32[4,4,4,8,128]{4,3,2,1,0:T(8,128)S(1)} custom-call(s32[2,32]{1,0:T(2,128)S(1)} %get-tuple-element.19.plan, s32[1]{0:T(128)S(6)} %copy.14.cnt, s32[32]{0:T(128)S(1)} %get-tuple-element.20.tot, bf16[64,64,256]{2,1,0:T(8,128)(2,1)S(1)} %bitcast.7, bf16[32,96,64]{2,1,0:T(8,128)(2,1)S(1)} %get-tuple-element.22.g1, ...), custom_call_target="tpu_custom_call" | custom-call | tf_op jit(solution)/shard_map/pairs/pallas_call | solution.py:437
  36.3 25.6 %give_back.1 = (f32[2,2,2,8,128]{4,3,2,1,0:T(8,128)S(1)}, f32[32,128]{1,0:T(8,128)S(1)}, bf16[256,256]{1,0:T(8,128)(2,1)S(1)}) custom-call(f32[4,4,4,8,128]{4,3,2,1,0:T(8,128)S(1)} %pairs.1.fsum, f32[2,2,3,2,64]{4,3,2,1,0:T(2,128)} %bitcast.9, f32[2,2,3,2,64]{4,3,2,1,0:T(2,128)} %bitcast.10, s32[1,128]{1,0:T(1,128)} %slot.3, s32[1,128]{1,0:T(1,128)} %bitcast.12, ...), custom_call_target="tpu_custom_call" | custom-call | tf_op jit(solution)/shard_map/give_back/pallas_call | solution.py:451
  61.9 0.7 %finish.1 = (f32[2,2,3,2,64]{4,3,2,1,0:T(2,128)}, f32[6,2,128]{2,1,0:T(2,128)}, bf16[128,2,256]{2,1,0:T(2,128)(2,1)}) custom-call(f32[2,2,2,8,128]{4,3,2,1,0:T(8,128)S(1)} %get-tuple-element.29.forces, f32[32,128]{1,0:T(8,128)S(1)} %get-tuple-element.30.moved, bf16[256,256]{1,0:T(8,128)(2,1)S(1)} %get-tuple-element.31.embeds), custom_call_target="tpu_custom_call" | custom-call | tf_op jit(solution)/shard_map/finish/pallas_call | solution.py:464

commit v5 on v4

--- a/solution.py
+++ b/solution.py
@@ -107,18 +107,44 @@
         copy.wait()
 
 
-def placement(dest, ranks_apart):
+def leaving(dest, slot):
     dest_f = dest.astype(F32)
     row = jnp.broadcast_to(dest_f, (128, LANES))
     col = jnp.transpose(row)
-    earlier = jnp.logical_and(col == row, iota((128, 128), 1) < iota((128, 128), 0))
-    rank = jnp.sum(jnp.where(earlier, 1.0, 0.0), axis=1, keepdims=True)
-    dest_c = col[:, :1]
-    gx = jnp.floor(dest_c * (1.0 / 16.0))
-    order = (dest_c - 16.0 * gx) * 8.0 + gx
-    place = order + 128.0 * rank if ranks_apart else 2.0 * order + rank
-    lanes = iota((128, 256), 1).astype(F32)
-    return jnp.where(lanes == place, 1.0, 0.0).astype(BF16)
+    earlier = jnp.logical_and(col == row, iota((128, 128), 0) < iota((128, 128), 1))
+    rank = jnp.sum(jnp.where(earlier, 1.0, 0.0), axis=0, keepdims=True)
+    gx = jnp.floor(dest_f * (1.0 / 16.0))
+    place = 2.0 * ((dest_f - 16.0 * gx) * 8.0 + gx) + rank
+    sub = iota((8, LANES), 0)
+    return jnp.where(sub == 0, slot.astype(F32), jnp.where(sub == 1, place, 0.0))
+
+
+def places_of(rows):
+    return jnp.where(iota((256, LANES), 0).astype(F32) == rows[1:2], 1.0, 0.0).astype(BF16)
+
+
+def slots_of(rows, cells):
+    at = iota((64, LANES), 0)
+    hits = [(at + (c[0] * 4 + c[1] * 2 + c[2]) * 64).astype(F32) == rows[0:1] for c in cells]
+    return jnp.where(jnp.concatenate(hits, axis=0), 1.0, 0.0).astype(BF16)
+
+
+def cells_in(own):
+    return [c for c in np.ndindex(2, 2, 2) if all(lo <= x < hi for x, (lo, hi) in zip(c, own))]
+
+
+OWNERS = [((0, 0, 0), cells_in([(0, 2)] * 3))] + [(s, cells_in(own)) for s, own, _ in BOXES]
+N_ROWS = 64 * sum(len(cells) for _, cells in OWNERS)
+
+
+def turned(x, s):
+    lane = iota(x.shape, 1)
+    if s[0]:
+        x = pltpu.roll(x, (16 * s[0]) % 128, 1)
+    for size, step, at in ((s[1], 4, lane // 4 % 4), (s[2], 1, lane % 4)):
+        if size:
+            x = jnp.where(at == (0 if size > 0 else 3), pltpu.roll(x, (-3 * step * size) % 128, 1), pltpu.roll(x, (step * size) % 128, 1))
+    return x
 
 
 def shift_rows(offset, lanes):
@@ -127,8 +153,8 @@
     return jnp.where(row == 0, x, jnp.where(row == 1, y, jnp.where(row == 2, z, 0.0)))
 
 
-def halo_kernel(pos_in, emb, slot, dest, blk_in, proj, rw, bias, ew, cnt, gemb, held, g1, g2, rc, projt, rb, w2, plan, tot,
-                pos, pos_v, emb_v, slot_v, dest_v, proj_v, rw_v, bias_v, ew_v, send1, recv1, blk, offs, loc, es, er, ps, pr, s1, r1):
+def halo_kernel(pos_in, emb, slot, dest, blk_in, proj, rw, bias, ew, cnt, gemb, held, g1, g2, rc, projt, rb, w2, places, plan, tot,
+                pos, pos_v, emb_v, slot_v, dest_v, proj_v, rw_v, bias_v, ew_v, send1, recv1, mine, lists, blk, offs, loc, es, er, ps, pr, ls, lr, s1, r1):
     me = position()
     barrier = pltpu.get_barrier_semaphore()
     pos[...] = jnp.zeros_like(pos)
@@ -155,9 +181,14 @@
         halo.append(copies)
     for copy in local[1:]:
         copy.wait()
-    where = placement(dest_v[...], False)
-    pick = jnp.where(iota((512, 128), 0) == slot_v[...], 1.0, 0.0).astype(BF16)
-    place = lax.dot_general(where, pick, (((0,), (1,)), ((), ())), preferred_element_type=F32).astype(BF16)
+    rows_out = leaving(dest_v[...], slot_v[...])
+    mine[...] = rows_out
+    copies = []
+    for i, (s, src, dst) in enumerate(BOXES):
+        copies.append(pltpu.make_async_remote_copy(src_ref=mine, dst_ref=lists.at[i], send_sem=ls.at[i], recv_sem=lr.at[i], device_id=shifted(me, s, -1), device_id_type=MESH))
+        copies[-1].start()
+    halo.append(copies)
+    place = dot_nt(places_of(rows_out), slots_of(rows_out, OWNERS[0][1])).astype(BF16)
     send1[...] = dot(place, emb_v[...].reshape(512, 256)).astype(BF16)
     rows = exchange(me, plane_partner, 16, 16, send1, recv1, s1, r1)
     projt[...] = jnp.transpose(proj_v[...])
@@ -224,6 +255,13 @@
         return c
 
     lax.fori_loop(0, 8, prep_group, 0)
+    wait_all(halo[2])
+    at = 0
+    for i, (s, owned) in enumerate(OWNERS):
+        rows_out = lists[i - 1] if i else mine[...]
+        size = 64 * len(owned)
+        places[at:at + size] = dot_nt(slots_of(rows_out, owned), places_of(rows_out)).astype(BF16)
+        at += size
     wait_all(rows)
     held[...] = recv1[...]
     wait_all(halo[1])
@@ -332,32 +370,48 @@
     out[...] = (acc[...] - jnp.roll(acc[...], 64, axis=2)).reshape(4, 4, 4, 8, LANES)
 
 
-def return_kernel(fsum, pos_in, vel_in, slot, dest, held, forces, moved, embeds, pos_v, vel_v, slot_v, dest_v, landed, mot, send1, recv1, send2, recv2, esend, erecv, loc, fs, fr, s1, r1, s2, r2, s3, r3):
+def return_kernel(fsum, pos_in, vel_in, held, places, forces, moved, embeds, pos_v, vel_v, landed, lhs, send1, recv1, send2, recv2, esend, erecv, loc, fs, fr, s1, r1, s2, r2, s3, r3):
     me = position()
     barrier = pltpu.get_barrier_semaphore()
     partners = greet(me, -1, True)
     local = []
-    for i, (x, y) in enumerate(((pos_in, pos_v), (vel_in, vel_v), (slot, slot_v), (dest, dest_v))):
+    for i, (x, y) in enumerate(((pos_in, pos_v), (vel_in, vel_v))):
         local.append(pltpu.make_async_copy(x, y, loc.at[i]))
         local[-1].start()
-    mot[...] = jnp.zeros_like(mot)
+    lhs[...] = jnp.zeros_like(lhs)
+    at = 0
+    for i, (s, owned) in enumerate(OWNERS):
+        for c in owned:
+            part = fsum[tuple(x + 2 * d + 1 for x, d in zip(c, s))]
+            if i % 2:
+                part = pltpu.roll(part, 4, 0)
+            lhs[8 * (i // 2):8 * (i // 2) + 8, at:at + 64] = part[:, :64]
+            at += 64
+    wait_all(local)
+    for j, c in enumerate(OWNERS[0][1]):
+        velocity = vel_v[c[0], c[1], :, c[2], :]
+        lhs[80:83, 64 * j:64 * j + 64] = pos_v[c[0], c[1], :, c[2], :] + 0.5 * velocity
+        lhs[84:87, 64 * j:64 * j + 64] = velocity
+    rows = dot(lhs[...].astype(BF16), places[...])
+    send1[...] = jnp.transpose(jnp.concatenate([rows, jnp.zeros((32, 256), F32)], axis=0)).astype(BF16)
     pl.semaphore_wait(barrier, partners)
+    first = exchange(me, plane_partner, 16, 16, send1, recv1, s1, r1)
     back = []
     for i, (s, own, ghost) in enumerate(BOXES):
         copy = pltpu.make_async_remote_copy(src_ref=box(fsum, ghost), dst_ref=box(landed.at[i], own), send_sem=fs.at[i], recv_sem=fr.at[i], device_id=shifted(me, s, 1), device_id_type=MESH)
         copy.start()
         back.append(copy)
     out = iota((256, 256), 0)
+    source = iota((256, 256), 1)
     want = ((out // 2) % 16) * 16 + (out // 32) * 2 + out % 2
-    perm2 = jnp.where(iota((256, 256), 1) == want, 1.0, 0.0).astype(BF16)
+    perm2 = jnp.where(source == want, 1.0, 0.0).astype(BF16)
     esend[...] = dot(perm2, held[...]).astype(BF16)
-    out = iota((128, 128), 0)
-    perm = jnp.where(iota((128, 128), 1) == (out % 16) * 8 + out // 16, 1.0, 0.0).astype(BF16)
     rows_sent = exchange(me, line_partner, 8, 32, esend, erecv, s3, r3)
-    wait_all(local)
-    where = placement(dest_v[...], True)
-    pick = jnp.where(iota((512, 128), 0) == slot_v[...], 1.0, 0.0).astype(BF16)
-    place = dot(pick, where).astype(BF16)
+    want = (out % 16) * 16 + (out // 32) * 2 + (out // 16) % 2
+    perm = jnp.where(source == want, 1.0, 0.0).astype(BF16)
+    wait_all(first)
+    send2[...] = dot(perm, recv1[...]).astype(BF16)
+    last = exchange(me, line_partner, 8, 32, send2, recv2, s2, r2)
     wait_all(back)
     for c in np.ndindex(2, 2, 2):
         total = fsum[c[0] + 1, c[1] + 1, c[2] + 1]
@@ -365,21 +419,20 @@
             if all(lo <= x < hi for x, (lo, hi) in zip(c, own)):
                 total = total + landed[i, c[0], c[1], c[2]]
         forces[c[0], c[1], c[2]] = total
-        new_velocity = vel_v[c[0], c[1], :, c[2], :] + 0.5 * total[:3, :64]
-        new_position = pos_v[c[0], c[1], :, c[2], :] + 0.5 * new_velocity
-        at = (c[0] * 4 + c[1] * 2 + c[2]) * 64
-        mot[0:3, at:at + 64] = new_position
-        mot[8:11, at:at + 64] = new_velocity
-    rows = dot(mot[...].astype(BF16), place)
-    tall = jnp.concatenate([rows[:, :128], rows[:, 128:], jnp.zeros((96, 128), F32)], axis=0)
-    send1[...] = jnp.transpose(tall)
-    wait_all(exchange(me, plane_partner, 16, 8, send1, recv1, s1, r1))
-    send2[...] = dot(perm, recv1[...].astype(BF16))
-    last = exchange(me, line_partner, 8, 16, send2, recv2, s2, r2)
     wait_all(rows_sent)
     embeds[...] = erecv[...]
     wait_all(last)
-    moved[...] = jnp.transpose(recv2[...])[:32]
+    for h in range(2):
+        by_source = jnp.concatenate([recv2[32 * g + 16 * h:32 * g + 16 * h + 16] for g in range(8)], axis=0)
+        by_source = jnp.transpose(by_source.astype(F32))
+        sums = [None, None]
+        for i, (s, _) in enumerate(OWNERS):
+            part = turned(by_source[8 * (i // 2):8 * (i // 2) + 8], s)
+            sums[i % 2] = part if sums[i % 2] is None else sums[i % 2] + part
+        total = sums[0] + pltpu.roll(sums[1], 4, 0)
+        base = by_source[80:88]
+        moved[16 * h:16 * h + 8] = base + 0.25 * total
+        moved[16 * h + 8:16 * h + 16] = pltpu.roll(base, 4, 0) + 0.5 * total
 
 
 def finish_kernel(forces, moved, embeds, forces_out, motion_out, embeds_out):
@@ -399,7 +452,7 @@
     pos_rows, vel_rows = (x.transpose(0, 1, 3, 2, 4) for x in (positions, velocity))
     dest_row = move_dest.reshape(1, 128)
     spaces = pltpu.VMEM((2, 2, 3, 2, 64), F32)
-    gemb, held, g1, g2, rc, projt, rb, w2, plan, tot = pl.pallas_call(
+    gemb, held, g1, g2, rc, projt, rb, w2, places, plan, tot = pl.pallas_call(
         halo_kernel,
         out_shape=(
             array((4, 4, 4, 64, 256), BF16),
@@ -410,11 +463,12 @@
             array((256, 256), BF16),
             array((256, 128), BF16),
             array((16, 512), BF16),
+            array((N_ROWS, 256), BF16),
             array((2, 32), jnp.int32),
             array((32,), jnp.int32),
         ),
         in_specs=[hbm] * 9 + [smem],
-        out_specs=(any_,) + (vmem,) * 7 + (smem,) * 2,
+        out_specs=(any_,) + (vmem,) * 8 + (smem,) * 2,
         scratch_shapes=[
             pltpu.VMEM((4, 4, 4, 8, LANES), F32),
             spaces,
@@ -427,10 +481,12 @@
             pltpu.VMEM((256,), BF16),
             pltpu.VMEM((256, 256), BF16),
             pltpu.VMEM((256, 256), BF16),
+            pltpu.VMEM((8, LANES), F32),
+            pltpu.VMEM((N_BOX, 8, LANES), F32),
             pltpu.SMEM((1, 2, 32), jnp.int32),
             pltpu.SMEM((3, 16), jnp.int32),
         ]
-        + [dma((10,))] + [dma((N_BOX,))] * 4 + [dma((16,))] * 2,
+        + [dma((10,))] + [dma((N_BOX,))] * 6 + [dma((16,))] * 2,
         compiler_params=pltpu.CompilerParams(collective_id=0, has_side_effects=True, vmem_limit_bytes=16 * 1024 * 1024),
         name="halo",
     )(*(pltpu.with_memory_space_constraint(x, pltpu.HBM) for x in (pos_rows, atom_embed, move_slot, dest_row, block_list, embed_proj, radial_weight, latent_bias.reshape(1, 256), energy_weight)), block_count)
@@ -451,16 +507,15 @@
     raw = pl.pallas_call(
         return_kernel,
         out_shape=(array((2, 2, 2, 8, LANES), F32), array((32, LANES), F32), array((256, 256), BF16)),
-        in_specs=[vmem] + [hbm] * 4 + [vmem],
+        in_specs=[vmem] + [hbm] * 2 + [vmem] * 2,
         out_specs=(vmem,) * 3,
-        scratch_shapes=[spaces, spaces, pltpu.VMEM((1, 128), jnp.int32), pltpu.VMEM((1, 128), jnp.int32)]
-        + [pltpu.VMEM((N_BOX, 2, 2, 2, 8, LANES), F32), pltpu.VMEM((16, 512), F32)]
-        + [pltpu.VMEM((128, LANES), F32)] * 4
+        scratch_shapes=[spaces, spaces, pltpu.VMEM((N_BOX, 2, 2, 2, 8, LANES), F32), pltpu.VMEM((96, N_ROWS), F32)]
+        + [pltpu.VMEM((256, LANES), BF16)] * 4
         + [pltpu.VMEM((256, 256), BF16)] * 2
-        + [dma((4,))] + [dma((N_BOX,))] * 2 + [dma((16,))] * 2 + [dma((8,))] * 4,
+        + [dma((2,))] + [dma((N_BOX,))] * 2 + [dma((16,))] * 2 + [dma((8,))] * 4,
         compiler_params=pltpu.CompilerParams(collective_id=1, has_side_effects=True, vmem_limit_bytes=16 * 1024 * 1024),
         name="give_back",
-    )(fsum, *(pltpu.with_memory_space_constraint(x, pltpu.HBM) for x in (pos_rows, vel_rows, move_slot, dest_row)), held)
+    )(fsum, *(pltpu.with_memory_space_constraint(x, pltpu.HBM) for x in (pos_rows, vel_rows)), held, places)
     forces, motion, embeds = pl.pallas_call(
         finish_kernel,
         out_shape=(array((2, 2, 3, 2, 64), F32), array((6, 2, 128), F32), array((128, 2, 256), BF16)),

time: 62.9 us -> 59.4 us (0.944)
  Pallas kernels: 61.3 us -> 57.8 us
    pallas_call x1, Pallas kernels: 25.6 us -> 22.7 us  [per_device(): pl.pallas_call(return_kernel, out_shape=(array((2, 2, 2, 8, LANES), F32),...]
    pallas_call x1, Pallas kernels: 8.59 us -> 6.45 us  [per_device(): pl.pallas_call(pair_kernel, out_shape=array((4, 4, 4, 8, LANES), F32), in...]
    pallas_call x1, Pallas kernels: 26.4 us -> 28 us  [per_device(): pl.pallas_call(halo_kernel, out_shape=(array((4, 4, 4, 64, 256), BF16), a...]
where the time goes in v5:
time: 59.4 us; the launch traced here: 59.1 us
  Pallas kernels  57.8 us (97%)
  between operations  1.3 us (2%)
    pallas_call x1, Pallas kernels, per_device(): pl.pallas_call(halo_kernel, out_shape=(array((4, 4, 4, 64, 256), BF16), a...  28 us
    pallas_call x1, Pallas kernels, per_device(): pl.pallas_call(return_kernel, out_shape=(array((2, 2, 2, 8, LANES), F32),...  22.7 us
    pallas_call x1, Pallas kernels, per_device(): pl.pallas_call(pair_kernel, out_shape=array((4, 4, 4, 8, LANES), F32), in...  6.45 us

profile of v5, /device:TPU:1, one launch (start us, length us, event | category | flops | bytes accessed | tf_op | source)
XLA Modules:
  0.0 59.1 jit_solution(7199050913603598742)
XLA Ops:
  1.3 28.0 %halo.1 = (bf16[4,4,4,64,256]{4,3,2,1,0:T(8,128)(2,1)S(1)}, bf16[256,256]{1,0:T(8,128)(2,1)S(1)}, bf16[32,96,64]{2,1,0:T(8,128)(2,1)S(1)}, bf16[32,32,64]{2,1,0:...) custom-call(f32[2,2,3,2,64]{4,3,2,1,0:T(2,128)} %bitcast.8, ...), custom_call_target="tpu_custom_call" | custom-call | tf_op jit(solution)/shard_map/halo/pallas_call | solution.py:455
  29.2 6.4 %pairs.1.fsum = f32[4,4,4,8,128]{4,3,2,1,0:T(8,128)S(1)} custom-call(s32[2,32]{1,0:T(2,128)S(1)} %get-tuple-element.20.plan, s32[1]{0:T(128)S(6)} %copy.14.cnt, s32[32]{0:T(128)S(1)} %get-tuple-element.21.tot, bf16[64,64,256]{2,1,0:T(8,128)(2,1)S(1)} %bitcast.7, bf16[32,96,64]{2,1,0:T(8,128)(2,1)S(1)} %get-tuple-element.23.g1, ...), custom_call_target="tpu_custom_call" | custom-call | tf_op jit(solution)/shard_map/pairs/pallas_call | solution.py:493
  35.7 22.7 %give_back.1 = (f32[2,2,2,8,128]{4,3,2,1,0:T(8,128)S(1)}, f32[32,128]{1,0:T(8,128)S(1)}, bf16[256,256]{1,0:T(8,128)(2,1)S(1)}) custom-call(f32[4,4,4,8,128]{4,3,2,1,0:T(8,128)S(1)} %pairs.1.fsum, f32[2,2,3,2,64]{4,3,2,1,0:T(2,128)} %bitcast.9, f32[2,2,3,2,64]{4,3,2,1,0:T(2,128)} %bitcast.10, bf16[256,256]{1,0:T(8,128)(2,1)S(1)} %get-tuple-element.29.held, ...), custom_call_target="tpu_custom_call" | custom-call | tf_op jit(solution)/shard_map/give_back/pallas_call | solution.py:507
  58.4 0.7 %finish.1 = (f32[2,2,3,2,64]{4,3,2,1,0:T(2,128)}, f32[6,2,128]{2,1,0:T(2,128)}, bf16[128,2,256]{2,1,0:T(2,128)(2,1)}) custom-call(f32[2,2,2,8,128]{4,3,2,1,0:T(8,128)S(1)} %get-tuple-element.31.forces, f32[32,128]{1,0:T(8,128)S(1)} %get-tuple-element.32.moved, bf16[256,256]{1,0:T(8,128)(2,1)S(1)} %get-tuple-element.33.embeds), custom_call_target="tpu_custom_call" | custom-call | tf_op jit(solution)/shard_map/finish/pallas_call | solution.py:519

commit v6 on v5

--- a/solution.py
+++ b/solution.py
@@ -116,16 +116,16 @@
     gx = jnp.floor(dest_f * (1.0 / 16.0))
     place = 2.0 * ((dest_f - 16.0 * gx) * 8.0 + gx) + rank
     sub = iota((8, LANES), 0)
-    return jnp.where(sub == 0, slot.astype(F32), jnp.where(sub == 1, place, 0.0))
+    return jnp.where(sub == 4, slot.astype(F32), jnp.where(sub == 5, place, 0.0))
 
 
 def places_of(rows):
-    return jnp.where(iota((256, LANES), 0).astype(F32) == rows[1:2], 1.0, 0.0).astype(BF16)
+    return jnp.where(iota((256, LANES), 0).astype(F32) == rows[5:6], 1.0, 0.0).astype(BF16)
 
 
 def slots_of(rows, cells):
     at = iota((64, LANES), 0)
-    hits = [(at + (c[0] * 4 + c[1] * 2 + c[2]) * 64).astype(F32) == rows[0:1] for c in cells]
+    hits = [(at + (c[0] * 4 + c[1] * 2 + c[2]) * 64).astype(F32) == rows[4:5] for c in cells]
     return jnp.where(jnp.concatenate(hits, axis=0), 1.0, 0.0).astype(BF16)
 
 
@@ -154,7 +154,7 @@
 
 
 def halo_kernel(pos_in, emb, slot, dest, blk_in, proj, rw, bias, ew, cnt, gemb, held, g1, g2, rc, projt, rb, w2, places, plan, tot,
-                pos, pos_v, emb_v, slot_v, dest_v, proj_v, rw_v, bias_v, ew_v, send1, recv1, mine, lists, blk, offs, loc, es, er, ps, pr, ls, lr, s1, r1):
+                pos, pos_v, emb_v, slot_v, dest_v, proj_v, rw_v, bias_v, ew_v, send1, recv1, blk, offs, loc, es, er, ps, pr, s1, r1):
     me = position()
     barrier = pltpu.get_barrier_semaphore()
     pos[...] = jnp.zeros_like(pos)
@@ -164,11 +164,14 @@
     partners = greet(me, 1, False)
     own = [(1, 3)] * 3
     local = []
-    for i, (x, y) in enumerate(((pos_in, pos_v), (emb, emb_v), (slot, slot_v), (dest, dest_v), (blk_in, blk), (proj, proj_v), (rw, rw_v), (bias, bias_v), (ew, ew_v), (emb, box(gemb, own)))):
+    for i, (x, y) in enumerate(((pos_in, pos_v), (slot, slot_v), (dest, dest_v), (emb, emb_v), (blk_in, blk), (proj, proj_v), (rw, rw_v), (bias, bias_v), (ew, ew_v), (emb, box(gemb, own)))):
         local.append(pltpu.make_async_copy(x, y, loc.at[i]))
         local[-1].start()
-    local[0].wait()
+    for copy in local[:3]:
+        copy.wait()
+    rows_out = leaving(dest_v[...], slot_v[...])
     for c in np.ndindex(2, 2, 2):
+        pos[c[0] + 1, c[1] + 1, c[2] + 1] = rows_out
         pos[c[0] + 1, c[1] + 1, c[2] + 1, 0:3, 0:64] = pos_v[c[0], c[1], :, c[2], :]
     pl.semaphore_wait(barrier, partners)
     halo = []
@@ -179,15 +182,8 @@
             copies.append(pltpu.make_async_remote_copy(src_ref=start, dst_ref=box(b, dst), send_sem=x.at[i], recv_sem=y.at[i], device_id=shifted(me, s, -1), device_id_type=MESH))
             copies[-1].start()
         halo.append(copies)
-    for copy in local[1:]:
+    for copy in local[3:]:
         copy.wait()
-    rows_out = leaving(dest_v[...], slot_v[...])
-    mine[...] = rows_out
-    copies = []
-    for i, (s, src, dst) in enumerate(BOXES):
-        copies.append(pltpu.make_async_remote_copy(src_ref=mine, dst_ref=lists.at[i], send_sem=ls.at[i], recv_sem=lr.at[i], device_id=shifted(me, s, -1), device_id_type=MESH))
-        copies[-1].start()
-    halo.append(copies)
     place = dot_nt(places_of(rows_out), slots_of(rows_out, OWNERS[0][1])).astype(BF16)
     send1[...] = dot(place, emb_v[...].reshape(512, 256)).astype(BF16)
     rows = exchange(me, plane_partner, 16, 16, send1, recv1, s1, r1)
@@ -212,7 +208,7 @@
     lane = iota((64, LANES), 1)
 
     def pos_at(c):
-        return pos[c // 16, c // 4 % 4, c % 4][:, :64]
+        return jnp.where(iota((8, 64), 0) < 3, pos[c // 16, c // 4 % 4, c % 4][:, :64], 0.0)
 
     def prepare(b):
         a, code = blk[0, 0, b], blk[0, 1, b]
@@ -250,15 +246,15 @@
     wait_all(halo[0])
 
     def prep_group(g, c):
-        for u in range(4):
-            prepare(g * 4 + u)
+        for u in range(8):
+            prepare(g * 8 + u)
         return c
 
-    lax.fori_loop(0, 8, prep_group, 0)
-    wait_all(halo[2])
+    lax.fori_loop(0, 4, prep_group, 0)
     at = 0
     for i, (s, owned) in enumerate(OWNERS):
-        rows_out = lists[i - 1] if i else mine[...]
+        first = tuple(x + 2 * d + 1 for x, d in zip(owned[0], s))
+        rows_out = pos[first]
         size = 64 * len(owned)
         places[at:at + size] = dot_nt(slots_of(rows_out, owned), places_of(rows_out)).astype(BF16)
         at += size
@@ -481,12 +477,10 @@
             pltpu.VMEM((256,), BF16),
             pltpu.VMEM((256, 256), BF16),
             pltpu.VMEM((256, 256), BF16),
-            pltpu.VMEM((8, LANES), F32),
-            pltpu.VMEM((N_BOX, 8, LANES), F32),
             pltpu.SMEM((1, 2, 32), jnp.int32),
             pltpu.SMEM((3, 16), jnp.int32),
         ]
-        + [dma((10,))] + [dma((N_BOX,))] * 6 + [dma((16,))] * 2,
+        + [dma((10,))] + [dma((N_BOX,))] * 4 + [dma((16,))] * 2,
         compiler_params=pltpu.CompilerParams(collective_id=0, has_side_effects=True, vmem_limit_bytes=16 * 1024 * 1024),
         name="halo",
     )(*(pltpu.with_memory_space_constraint(x, pltpu.HBM) for x in (pos_rows, atom_embed, move_slot, dest_row, block_list, embed_proj, radial_weight, latent_bias.reshape(1, 256), energy_weight)), block_count)

time: 59.4 us -> 57.5 us (0.968)
  Pallas kernels: 57.8 us -> 55.9 us
    pallas_call x1, Pallas kernels: 22.7 us -> 17.2 us  [per_device(): pl.pallas_call(return_kernel, out_shape=(array((2, 2, 2, 8, LANES), F32),...]
    pallas_call x1, Pallas kernels: 6.45 us -> 11.6 us  [per_device(): pl.pallas_call(pair_kernel, out_shape=array((4, 4, 4, 8, LANES), F32), in...]
    pallas_call x1, Pallas kernels: 28 us -> 26.4 us  [per_device(): pl.pallas_call(halo_kernel, out_shape=(array((4, 4, 4, 64, 256), BF16), a...]
where the time goes in v6:
time: 57.5 us; the launch traced here: 57.2 us
  Pallas kernels  55.9 us (97%)
  between operations  1.3 us (2%)
    pallas_call x1, Pallas kernels, per_device(): pl.pallas_call(halo_kernel, out_shape=(array((4, 4, 4, 64, 256), BF16), a...  26.4 us
    pallas_call x1, Pallas kernels, per_device(): pl.pallas_call(return_kernel, out_shape=(array((2, 2, 2, 8, LANES), F32),...  17.2 us
    pallas_call x1, Pallas kernels, per_device(): pl.pallas_call(pair_kernel, out_shape=array((4, 4, 4, 8, LANES), F32), in...  11.6 us

profile of v6, /device:TPU:1, one launch (start us, length us, event | category | flops | bytes accessed | tf_op | source)
XLA Modules:
  0.0 57.2 jit_solution(11366461364821169757)
XLA Ops:
  1.3 26.4 %halo.1 = (bf16[4,4,4,64,256]{4,3,2,1,0:T(8,128)(2,1)S(1)}, bf16[256,256]{1,0:T(8,128)(2,1)S(1)}, bf16[32,96,64]{2,1,0:T(8,128)(2,1)S(1)}, bf16[32,32,64]{2,1,0:...) custom-call(f32[2,2,3,2,64]{4,3,2,1,0:T(2,128)} %bitcast.8, ...), custom_call_target="tpu_custom_call" | custom-call | tf_op jit(solution)/shard_map/halo/pallas_call | solution.py:451
  27.7 11.6 %pairs.1.fsum = f32[4,4,4,8,128]{4,3,2,1,0:T(8,128)S(1)} custom-call(s32[2,32]{1,0:T(2,128)S(1)} %get-tuple-element.20.plan, s32[1]{0:T(128)S(6)} %copy.14.cnt, s32[32]{0:T(128)S(1)} %get-tuple-element.21.tot, bf16[64,64,256]{2,1,0:T(8,128)(2,1)S(1)} %bitcast.7, bf16[32,96,64]{2,1,0:T(8,128)(2,1)S(1)} %get-tuple-element.23.g1, ...), custom_call_target="tpu_custom_call" | custom-call | tf_op jit(solution)/shard_map/pairs/pallas_call | solution.py:487
  39.3 17.2 %give_back.1 = (f32[2,2,2,8,128]{4,3,2,1,0:T(8,128)S(1)}, f32[32,128]{1,0:T(8,128)S(1)}, bf16[256,256]{1,0:T(8,128)(2,1)S(1)}) custom-call(f32[4,4,4,8,128]{4,3,2,1,0:T(8,128)S(1)} %pairs.1.fsum, f32[2,2,3,2,64]{4,3,2,1,0:T(2,128)} %bitcast.9, f32[2,2,3,2,64]{4,3,2,1,0:T(2,128)} %bitcast.10, bf16[256,256]{1,0:T(8,128)(2,1)S(1)} %get-tuple-element.29.held, ...), custom_call_target="tpu_custom_call" | custom-call | tf_op jit(solution)/shard_map/give_back/pallas_call | solution.py:501
  56.5 0.7 %finish.1 = (f32[2,2,3,2,64]{4,3,2,1,0:T(2,128)}, f32[6,2,128]{2,1,0:T(2,128)}, bf16[128,2,256]{2,1,0:T(2,128)(2,1)}) custom-call(f32[2,2,2,8,128]{4,3,2,1,0:T(8,128)S(1)} %get-tuple-element.31.forces, f32[32,128]{1,0:T(8,128)S(1)} %get-tuple-element.32.moved, bf16[256,256]{1,0:T(8,128)(2,1)S(1)} %get-tuple-element.33.embeds), custom_call_target="tpu_custom_call" | custom-call | tf_op jit(solution)/shard_map/finish/pallas_call | solution.py:513

commit v7 on v6

--- a/solution.py
+++ b/solution.py
@@ -13,8 +13,9 @@
 OFFSETS = np.array([[0, 0, 0], [1, 0, 0], [0, 1, 0], [0, 0, 1], [1, 1, 0], [1, 0, 1], [0, 1, 1], [1, 1, 1], [1, 1, -1], [1, -1, 1], [-1, 1, 1], [1, -1, 0], [1, 0, -1], [0, 1, -1]], np.int32)
 LANES = 128
 GROUP = 12
-CHUNK = 128
-MAXCH = 32 * 32
+WIDE = 256
+WIDE_GROUP = 6
+MAXCH = 32 * 16
 SIZES = (8, 4, 4)
 
 
@@ -187,7 +188,7 @@
     place = dot_nt(places_of(rows_out), slots_of(rows_out, OWNERS[0][1])).astype(BF16)
     send1[...] = dot(place, emb_v[...].reshape(512, 256)).astype(BF16)
     rows = exchange(me, plane_partner, 16, 16, send1, recv1, s1, r1)
-    projt[...] = jnp.transpose(proj_v[...])
+    projt[...] = (0.5 * jnp.transpose(proj_v[...]).astype(F32)).astype(BF16)
     half = 0.5 * bias_v[...]
     b1 = half.astype(BF16).astype(F32)
     b2 = (half - b1).astype(BF16).astype(F32)
@@ -273,96 +274,107 @@
     return sn * sign, cs * sign
 
 
-def pair_kernel(plan, cnt, tot, gemb, g1, g2, rc, projt, rb, w2, out, wt, acc, tab_b, tab_k):
+def pair_kernel(plan, cnt, tot, gemb, g1, g2, rc, projt, rb, w2, out, wt, acc, tab_b, tab_k, rest_b, rest_k):
     def project(g, c):
-        four = []
-        for u in range(4):
-            four += [gemb[plan[0, g * 4 + u]], gemb[plan[1, g * 4 + u]]]
-        for u in (0, 2):
-            both = (dot_nt(projt[...], jnp.concatenate(four[2 * u:2 * u + 4], axis=0)).astype(BF16) * 0.5).astype(BF16)
-            wt[g * 4 + u] = both[:, :LANES]
-            wt[g * 4 + u + 1] = both[:, LANES:]
+        for u in range(0, 8, 2):
+            four = [gemb[plan[d, g * 8 + v]] for v in (u, u + 1) for d in range(2)]
+            both = dot_nt(projt[...], jnp.concatenate(four, axis=0)).astype(BF16)
+            wt[g * 8 + u] = both[:, :LANES]
+            wt[g * 8 + u + 1] = both[:, LANES:]
         return c
 
-    lax.fori_loop(0, (cnt[0] + 3) // 4, project, 0)
-
-    def fill_block(b, n):
+    lax.fori_loop(0, (cnt[0] + 7) // 8, project, 0)
+
+    def fill_block(b, c):
+        n, m = c
+        wide_chunks = (tot[b] + WIDE - LANES - 1) // WIDE
+
         def put(t, n):
             tab_b[n] = b
-            tab_k[n] = t * CHUNK
+            tab_k[n] = t * WIDE
             return n + 1
 
-        return lax.fori_loop(0, (tot[b] + CHUNK - 1) // CHUNK, put, n)
-
-    n = lax.fori_loop(0, cnt[0], fill_block, 0)
-    for u in range(GROUP):
+        rest_b[m] = b
+        rest_k[m] = wide_chunks * WIDE
+        return lax.fori_loop(0, wide_chunks, put, n), m + jnp.where(tot[b] > wide_chunks * WIDE, 1, 0)
+
+    n, m = lax.fori_loop(0, cnt[0], fill_block, (0, 0))
+    for u in range(WIDE_GROUP):
         tab_b[n + u] = 0
         tab_k[n + u] = 1 << 20
+    for u in range(GROUP):
+        rest_b[m + u] = 0
+        rest_k[m + u] = 1 << 20
 
     acc[...] = jnp.zeros_like(acc)
-    kl = iota((1, CHUNK), 1)
-    sub = iota((8, CHUNK), 0)
-    order = (sub + 1).astype(F32)
-    ones_rows = jnp.where(sub < 3, 1.0, 0.0)
     halves = iota((8, LANES), 1) < 64
 
-    def wide(x):
-        return jnp.concatenate([x] * (CHUNK // LANES), axis=1)
-
-    def chunk_group(g, c):
-        R = range(GROUP)
-        bs = [tab_b[g * GROUP + u] for u in R]
-        ks = [(kl + tab_k[g * GROUP + u]).astype(F32) for u in R]
-        oh_i = []
-        for u in R:
-            hit = jnp.logical_and(ks[u] >= wide(rc[bs[u], 0:64]), ks[u] < wide(rc[bs[u], 64:128]))
-            oh_i.append(jnp.where(hit, 1.0, 0.0).astype(BF16))
-        got = [dot(g1[bs[u]], oh_i[u]) for u in R]
-        oh_j = []
-        for u in R:
-            want = ks[u] - got[u][64:65] - got[u][65:66]
-            oh_j.append(jnp.where(got[u][:64] == want, 1.0, 0.0).astype(BF16))
-        gotb = [dot(g2[bs[u]], oh_j[u]) for u in R]
-        info = []
-        xs = []
-        for u in R:
-            sep = (gotb[u][:8] + gotb[u][8:16] + gotb[u][16:24]) - (got[u][72:80] + got[u][80:88])
-            sq = sep * sep
-            d2 = sq[0:1] + sq[1:2] + sq[2:3]
-            s = jnp.sqrt(jnp.broadcast_to(d2, (8, CHUNK)) + 0.25) * (1.0 / 6.0)
-            sn, cs = sinpi_cospi(order * s)
-            e = jnp.where(s < 1.0, 1.0 - s * s, 0.0)
-            info.append((sep, s, e, cs * order))
-            x2 = jnp.concatenate([sn, ones_rows], axis=0).astype(BF16)
-            xs.append(jnp.concatenate([oh_i[u], oh_j[u], x2, jnp.zeros((112, CHUNK), BF16)], axis=0))
-        qs = [dot(jnp.concatenate([wt[bs[u]], rb[...]], axis=1), xs[u]) for u in R]
-        hd = []
-        for u in R:
-            q = qs[u]
-            t = jnp.tanh(q)
-            h = q + q * t
-            d = (1.0 + t) + h * (1.0 - t)
-            hd.append(jnp.concatenate([h.astype(BF16), d.astype(BF16)], axis=0))
-        rs = []
-        for u in range(0, GROUP, 2):
-            both = dot(w2[...], jnp.concatenate([hd[u], hd[u + 1]], axis=1))
-            rs += [both[:, :CHUNK], both[:, CHUNK:]]
-        fs = []
-        for u in R:
-            sep, s, e, cn = info[u]
-            terms = rs[u][:8] * cn * (np.pi * e * e) + rs[u][8:] * (-4.0 * s * e)
-            ct = jnp.sum(terms, axis=0, keepdims=True)
-            f = sep * (ct / (36.0 * s))
-            fh = f.astype(BF16).astype(F32)
-            fs.append(jnp.concatenate([fh, f - fh], axis=0).astype(BF16))
-        for u in R:
-            both = dot_nt(fs[u], xs[u][:128])
-            part = both[:8] + both[8:]
-            acc[plan[0, bs[u]]] += jnp.where(halves, part, 0.0)
-            acc[plan[1, bs[u]]] += jnp.where(halves, 0.0, part)
-        return c
-
-    lax.fori_loop(0, (n + GROUP - 1) // GROUP, chunk_group, 0)
+    def run(chunk, group, tab_b, tab_k, count):
+        kl = iota((1, chunk), 1)
+        sub = iota((8, chunk), 0)
+        order = (sub + 1).astype(F32)
+        ones_rows = jnp.where(sub < 3, 1.0, 0.0)
+
+        def wide(x):
+            return jnp.concatenate([x] * (chunk // LANES), axis=1)
+
+        def chunk_group(g, c):
+            R = range(group)
+            bs = [tab_b[g * group + u] for u in R]
+            ks = [(kl + tab_k[g * group + u]).astype(F32) for u in R]
+            oh_i = []
+            for u in R:
+                hit = jnp.logical_and(ks[u] >= wide(rc[bs[u], 0:64]), ks[u] < wide(rc[bs[u], 64:128]))
+                oh_i.append(jnp.where(hit, 1.0, 0.0).astype(BF16))
+            got = [dot(g1[bs[u]], oh_i[u]) for u in R]
+            oh_j = []
+            for u in R:
+                want = ks[u] - got[u][64:65] - got[u][65:66]
+                oh_j.append(jnp.where(got[u][:64] == want, 1.0, 0.0).astype(BF16))
+            gotb = [dot(g2[bs[u]], oh_j[u]) for u in R]
+            info = []
+            xs = []
+            for u in R:
+                sep = (gotb[u][:8] + gotb[u][8:16] + gotb[u][16:24]) - (got[u][72:80] + got[u][80:88])
+                sq = sep * sep
+                d2 = sq[0:1] + sq[1:2] + sq[2:3]
+                s = jnp.sqrt(jnp.broadcast_to(d2, (8, chunk)) + 0.25) * (1.0 / 6.0)
+                sn, cs = sinpi_cospi(order * s)
+                e = jnp.where(s < 1.0, 1.0 - s * s, 0.0)
+                info.append((sep, s, e, cs * order))
+                x2 = jnp.concatenate([sn, ones_rows], axis=0).astype(BF16)
+                xs.append(jnp.concatenate([oh_i[u], oh_j[u], x2, jnp.zeros((112, chunk), BF16)], axis=0))
+            qs = [dot(jnp.concatenate([wt[bs[u]], rb[...]], axis=1), xs[u]) for u in R]
+            hd = []
+            for u in R:
+                q = qs[u]
+                t = jnp.tanh(q)
+                h = q + q * t
+                d = (1.0 + t) + h * (1.0 - t)
+                hd.append(jnp.concatenate([h.astype(BF16), d.astype(BF16)], axis=0))
+            rs = []
+            for u in range(0, group, 2 if chunk == LANES else 1):
+                both = dot(w2[...], jnp.concatenate(hd[u:u + 2], axis=1) if chunk == LANES else hd[u])
+                rs += [both[:, :LANES], both[:, LANES:]] if chunk == LANES else [both]
+            fs = []
+            for u in R:
+                sep, s, e, cn = info[u]
+                terms = rs[u][:8] * cn * (np.pi * e * e) + rs[u][8:] * (-4.0 * s * e)
+                ct = jnp.sum(terms, axis=0, keepdims=True)
+                f = sep * (ct / (36.0 * s))
+                fh = f.astype(BF16).astype(F32)
+                fs.append(jnp.concatenate([fh, f - fh], axis=0).astype(BF16))
+            for u in R:
+                both = dot_nt(fs[u], xs[u][:128])
+                part = both[:8] + both[8:]
+                acc[plan[0, bs[u]]] += jnp.where(halves, part, 0.0)
+                acc[plan[1, bs[u]]] += jnp.where(halves, 0.0, part)
+            return c
+
+        lax.fori_loop(0, (count + group - 1) // group, chunk_group, 0)
+
+    run(WIDE, WIDE_GROUP, tab_b, tab_k, n)
+    run(LANES, GROUP, rest_b, rest_k, m)
     out[...] = (acc[...] - jnp.roll(acc[...], 64, axis=2)).reshape(4, 4, 4, 8, LANES)
 
 
@@ -492,8 +504,10 @@
         scratch_shapes=[
             pltpu.VMEM((32, 256, 128), BF16),
             pltpu.VMEM((64, 8, LANES), F32),
-            pltpu.SMEM((MAXCH + GROUP,), jnp.int32),
-            pltpu.SMEM((MAXCH + GROUP,), jnp.int32),
+            pltpu.SMEM((MAXCH + WIDE_GROUP,), jnp.int32),
+            pltpu.SMEM((MAXCH + WIDE_GROUP,), jnp.int32),
+            pltpu.SMEM((40 + GROUP,), jnp.int32),
+            pltpu.SMEM((40 + GROUP,), jnp.int32),
         ],
         compiler_params=pltpu.CompilerParams(vmem_limit_bytes=24 * 1024 * 1024),
         name="pairs",

time: 57.5 us -> 55.6 us (0.967)
  Pallas kernels: 55.9 us -> 54 us
    pallas_call x1, Pallas kernels: 11.6 us -> 8.47 us  [per_device(): pl.pallas_call(pair_kernel, out_shape=array((4, 4, 4, 8, LANES), F32), in...]
    pallas_call x1, Pallas kernels: 17.2 us -> 18.5 us  [per_device(): pl.pallas_call(return_kernel, out_shape=(array((2, 2, 2, 8, LANES), F32),...]
where the time goes in v7:
time: 55.6 us; the launch traced here: 55.3 us
  Pallas kernels  54 us (97%)
  between operations  1.3 us (2%)
    pallas_call x1, Pallas kernels, per_device(): pl.pallas_call(halo_kernel, out_shape=(array((4, 4, 4, 64, 256), BF16), a...  26.4 us
    pallas_call x1, Pallas kernels, per_device(): pl.pallas_call(return_kernel, out_shape=(array((2, 2, 2, 8, LANES), F32),...  18.5 us
    pallas_call x1, Pallas kernels, per_device(): pl.pallas_call(pair_kernel, out_shape=array((4, 4, 4, 8, LANES), F32), in...  8.47 us

profile of v7, /device:TPU:1, one launch (start us, length us, event | category | flops | bytes accessed | tf_op | source)
XLA Modules:
  0.0 55.3 jit_solution(12699875056140297784)
XLA Ops:
  1.3 26.4 %halo.1 = (bf16[4,4,4,64,256]{4,3,2,1,0:T(8,128)(2,1)S(1)}, bf16[256,256]{1,0:T(8,128)(2,1)S(1)}, bf16[32,96,64]{2,1,0:T(8,128)(2,1)S(1)}, bf16[32,32,64]{2,1,0:...) custom-call(f32[2,2,3,2,64]{4,3,2,1,0:T(2,128)} %bitcast.8, ...), custom_call_target="tpu_custom_call" | custom-call | tf_op jit(solution)/shard_map/halo/pallas_call | solution.py:463
  27.7 8.5 %pairs.1.fsum = f32[4,4,4,8,128]{4,3,2,1,0:T(8,128)S(1)} custom-call(s32[2,32]{1,0:T(2,128)S(1)} %get-tuple-element.20.plan, s32[1]{0:T(128)S(6)} %copy.14.cnt, s32[32]{0:T(128)S(1)} %get-tuple-element.21.tot, bf16[64,64,256]{2,1,0:T(8,128)(2,1)S(1)} %bitcast.7, bf16[32,96,64]{2,1,0:T(8,128)(2,1)S(1)} %get-tuple-element.23.g1, ...), custom_call_target="tpu_custom_call" | custom-call | tf_op jit(solution)/shard_map/pairs/pallas_call | solution.py:499
  36.2 18.5 %give_back.1 = (f32[2,2,2,8,128]{4,3,2,1,0:T(8,128)S(1)}, f32[32,128]{1,0:T(8,128)S(1)}, bf16[256,256]{1,0:T(8,128)(2,1)S(1)}) custom-call(f32[4,4,4,8,128]{4,3,2,1,0:T(8,128)S(1)} %pairs.1.fsum, f32[2,2,3,2,64]{4,3,2,1,0:T(2,128)} %bitcast.9, f32[2,2,3,2,64]{4,3,2,1,0:T(2,128)} %bitcast.10, bf16[256,256]{1,0:T(8,128)(2,1)S(1)} %get-tuple-element.29.held, ...), custom_call_target="tpu_custom_call" | custom-call | tf_op jit(solution)/shard_map/give_back/pallas_call | solution.py:515
  54.6 0.7 %finish.1 = (f32[2,2,3,2,64]{4,3,2,1,0:T(2,128)}, f32[6,2,128]{2,1,0:T(2,128)}, bf16[128,2,256]{2,1,0:T(2,128)(2,1)}) custom-call(f32[2,2,2,8,128]{4,3,2,1,0:T(8,128)S(1)} %get-tuple-element.31.forces, f32[32,128]{1,0:T(8,128)S(1)} %get-tuple-element.32.moved, bf16[256,256]{1,0:T(8,128)(2,1)S(1)} %get-tuple-element.33.embeds), custom_call_target="tpu_custom_call" | custom-call | tf_op jit(solution)/shard_map/finish/pallas_call | solution.py:527

commit v8 on v7

--- a/solution.py
+++ b/solution.py
@@ -14,7 +14,7 @@
 LANES = 128
 GROUP = 12
 WIDE = 256
-WIDE_GROUP = 6
+WIDE_GROUP = 7
 MAXCH = 32 * 16
 SIZES = (8, 4, 4)
 
@@ -28,7 +28,7 @@
             if any(s):
                 need.setdefault(s, []).append([x - 2 * y for x, y in zip(b, s)])
     boxes = []
-    for s in sorted(need, key=lambda s: (-s[0], -len(set(map(tuple, need[s]))), s)):
+    for s in sorted(need, key=lambda s: (len(set(map(tuple, need[s]))), s)):
         own = [(min(c[d] for c in need[s]), max(c[d] for c in need[s]) + 1) for d in range(3)]
         boxes.append((s, own, [(lo + 2 * s[d] + 1, hi + 2 * s[d] + 1) for d, (lo, hi) in enumerate(own)]))
     return boxes
@@ -154,7 +154,7 @@
     return jnp.where(row == 0, x, jnp.where(row == 1, y, jnp.where(row == 2, z, 0.0)))
 
 
-def halo_kernel(pos_in, emb, slot, dest, blk_in, proj, rw, bias, ew, cnt, gemb, held, g1, g2, rc, projt, rb, w2, places, plan, tot,
+def halo_kernel(pos_in, emb, slot, dest, blk_in, proj, rw, bias, ew, cnt, gemb, held, g1, g2, rc, projt, rb, w2, ewc, places, plan, tot,
                 pos, pos_v, emb_v, slot_v, dest_v, proj_v, rw_v, bias_v, ew_v, send1, recv1, blk, offs, loc, es, er, ps, pr, s1, r1):
     me = position()
     barrier = pltpu.get_barrier_semaphore()
@@ -198,8 +198,8 @@
     ewf = ew_v[...].astype(F32).reshape(1, 256)
     rb[...] = jnp.transpose(jnp.concatenate([0.5 * rwf, biases, jnp.zeros((112, 256), F32)], axis=0)).astype(BF16)
     z8 = jnp.zeros((8, 256), F32)
-    w2[:, :256] = jnp.concatenate([z8, jnp.where(row8 == 0, ewf, 0.0)], axis=0).astype(BF16)
-    w2[:, 256:] = jnp.concatenate([0.5 * rwf * ewf, z8], axis=0).astype(BF16)
+    w2[...] = jnp.concatenate([0.5 * rwf * ewf, z8], axis=0).astype(BF16)
+    ewc[...] = jnp.transpose(jnp.broadcast_to(ewf, (LANES, 256)))
 
     jl = iota((64, 64), 1)
     il = iota((64, 64), 0)
@@ -274,7 +274,7 @@
     return sn * sign, cs * sign
 
 
-def pair_kernel(plan, cnt, tot, gemb, g1, g2, rc, projt, rb, w2, out, wt, acc, tab_b, tab_k, rest_b, rest_k):
+def pair_kernel(plan, cnt, tot, gemb, g1, g2, rc, projt, rb, w2, ewc, out, wt, acc, tab_b, tab_k, rest_b, rest_k):
     def project(g, c):
         for u in range(0, 8, 2):
             four = [gemb[plan[d, g * 8 + v]] for v in (u, u + 1) for d in range(2)]
@@ -346,12 +346,14 @@
                 xs.append(jnp.concatenate([oh_i[u], oh_j[u], x2, jnp.zeros((112, chunk), BF16)], axis=0))
             qs = [dot(jnp.concatenate([wt[bs[u]], rb[...]], axis=1), xs[u]) for u in R]
             hd = []
+            us = []
             for u in R:
                 q = qs[u]
                 t = jnp.tanh(q)
                 h = q + q * t
                 d = (1.0 + t) + h * (1.0 - t)
-                hd.append(jnp.concatenate([h.astype(BF16), d.astype(BF16)], axis=0))
+                hd.append(d.astype(BF16))
+                us.append(jnp.sum((h * wide(ewc[...])).reshape(32, 8, chunk), axis=0))
             rs = []
             for u in range(0, group, 2 if chunk == LANES else 1):
                 both = dot(w2[...], jnp.concatenate(hd[u:u + 2], axis=1) if chunk == LANES else hd[u])
@@ -359,7 +361,7 @@
             fs = []
             for u in R:
                 sep, s, e, cn = info[u]
-                terms = rs[u][:8] * cn * (np.pi * e * e) + rs[u][8:] * (-4.0 * s * e)
+                terms = rs[u][:8] * cn * (np.pi * e * e) + us[u] * (-4.0 * s * e)
                 ct = jnp.sum(terms, axis=0, keepdims=True)
                 f = sep * (ct / (36.0 * s))
                 fh = f.astype(BF16).astype(F32)
@@ -460,7 +462,7 @@
     pos_rows, vel_rows = (x.transpose(0, 1, 3, 2, 4) for x in (positions, velocity))
     dest_row = move_dest.reshape(1, 128)
     spaces = pltpu.VMEM((2, 2, 3, 2, 64), F32)
-    gemb, held, g1, g2, rc, projt, rb, w2, places, plan, tot = pl.pallas_call(
+    gemb, held, g1, g2, rc, projt, rb, w2, ewc, places, plan, tot = pl.pallas_call(
         halo_kernel,
         out_shape=(
             array((4, 4, 4, 64, 256), BF16),
@@ -470,13 +472,14 @@
             array((32, 128, LANES), F32),
             array((256, 256), BF16),
             array((256, 128), BF16),
-            array((16, 512), BF16),
+            array((16, 256), BF16),
+            array((256, LANES), F32),
             array((N_ROWS, 256), BF16),
             array((2, 32), jnp.int32),
             array((32,), jnp.int32),
         ),
         in_specs=[hbm] * 9 + [smem],
-        out_specs=(any_,) + (vmem,) * 8 + (smem,) * 2,
+        out_specs=(any_,) + (vmem,) * 9 + (smem,) * 2,
         scratch_shapes=[
             pltpu.VMEM((4, 4, 4, 8, LANES), F32),
             spaces,
@@ -499,7 +502,7 @@
     fsum = pl.pallas_call(
         pair_kernel,
         out_shape=array((4, 4, 4, 8, LANES), F32),
-        in_specs=[smem] * 3 + [vmem] * 7,
+        in_specs=[smem] * 3 + [vmem] * 8,
         out_specs=vmem,
         scratch_shapes=[
             pltpu.VMEM((32, 256, 128), BF16),
@@ -511,7 +514,7 @@
         ],
         compiler_params=pltpu.CompilerParams(vmem_limit_bytes=24 * 1024 * 1024),
         name="pairs",
-    )(plan, block_count, tot, gemb.reshape(64, 64, 256), g1, g2, rc, projt, rb, w2)
+    )(plan, block_count, tot, gemb.reshape(64, 64, 256), g1, g2, rc, projt, rb, w2, ewc)
     raw = pl.pallas_call(
         return_kernel,
         out_shape=(array((2, 2, 2, 8, LANES), F32), array((32, LANES), F32), array((256, 256), BF16)),

time: 55.6 us -> 55.3 us (level); the launches traced: 55.3 us -> 54.3 us
  Pallas kernels: 54 us -> 53 us
    pallas_call x1, Pallas kernels: 8.47 us -> 11 us  [per_device(): pl.pallas_call(pair_kernel, out_shape=array((4, 4, 4, 8, LANES), F32), in...]
    pallas_call x1, Pallas kernels: 26.4 us -> 24.5 us  [per_device(): pl.pallas_call(halo_kernel, out_shape=(array((4, 4, 4, 64, 256), BF16), a...]
    pallas_call x1, Pallas kernels: 18.5 us -> 16.8 us  [per_device(): pl.pallas_call(return_kernel, out_shape=(array((2, 2, 2, 8, LANES), F32),...]
where the time goes in v8:
time: 55.3 us; the launch traced here: 54.3 us
  Pallas kernels  53 us (96%)
  between operations  1.3 us (2%)
    pallas_call x1, Pallas kernels, per_device(): pl.pallas_call(halo_kernel, out_shape=(array((4, 4, 4, 64, 256), BF16), a...  24.5 us
    pallas_call x1, Pallas kernels, per_device(): pl.pallas_call(return_kernel, out_shape=(array((2, 2, 2, 8, LANES), F32),...  16.8 us
    pallas_call x1, Pallas kernels, per_device(): pl.pallas_call(pair_kernel, out_shape=array((4, 4, 4, 8, LANES), F32), in...  11 us

profile of v8, /device:TPU:1, one launch (start us, length us, event | category | flops | bytes accessed | tf_op | source)
XLA Modules:
  0.0 54.3 jit_solution(9255932803070182409)
XLA Ops:
  1.3 24.5 %halo.1 = (bf16[4,4,4,64,256]{4,3,2,1,0:T(8,128)(2,1)S(1)}, bf16[256,256]{1,0:T(8,128)(2,1)S(1)}, bf16[32,96,64]{2,1,0:T(8,128)(2,1)S(1)}, bf16[32,32,64]{2,1,0:...) custom-call(f32[2,2,3,2,64]{4,3,2,1,0:T(2,128)} %bitcast.8, ...), custom_call_target="tpu_custom_call" | custom-call | tf_op jit(solution)/shard_map/halo/pallas_call | solution.py:465
  25.8 11.0 %pairs.1.fsum = f32[4,4,4,8,128]{4,3,2,1,0:T(8,128)S(1)} custom-call(s32[2,32]{1,0:T(2,128)S(1)} %get-tuple-element.21.plan, s32[1]{0:T(128)S(6)} %copy.14.cnt, s32[32]{0:T(128)S(1)} %get-tuple-element.22.tot, bf16[64,64,256]{2,1,0:T(8,128)(2,1)S(1)} %bitcast.7, bf16[32,96,64]{2,1,0:T(8,128)(2,1)S(1)} %get-tuple-element.24.g1, ...), custom_call_target="tpu_custom_call" | custom-call | tf_op jit(solution)/shard_map/pairs/pallas_call | solution.py:502
  36.8 16.8 %give_back.1 = (f32[2,2,2,8,128]{4,3,2,1,0:T(8,128)S(1)}, f32[32,128]{1,0:T(8,128)S(1)}, bf16[256,256]{1,0:T(8,128)(2,1)S(1)}) custom-call(f32[4,4,4,8,128]{4,3,2,1,0:T(8,128)S(1)} %pairs.1.fsum, f32[2,2,3,2,64]{4,3,2,1,0:T(2,128)} %bitcast.9, f32[2,2,3,2,64]{4,3,2,1,0:T(2,128)} %bitcast.10, bf16[256,256]{1,0:T(8,128)(2,1)S(1)} %get-tuple-element.31.held, ...), custom_call_target="tpu_custom_call" | custom-call | tf_op jit(solution)/shard_map/give_back/pallas_call | solution.py:518
  53.6 0.7 %finish.1 = (f32[2,2,3,2,64]{4,3,2,1,0:T(2,128)}, f32[6,2,128]{2,1,0:T(2,128)}, bf16[128,2,256]{2,1,0:T(2,128)(2,1)}) custom-call(f32[2,2,2,8,128]{4,3,2,1,0:T(8,128)S(1)} %get-tuple-element.33.forces, f32[32,128]{1,0:T(8,128)S(1)} %get-tuple-element.34.moved, bf16[256,256]{1,0:T(8,128)(2,1)S(1)} %get-tuple-element.35.embeds), custom_call_target="tpu_custom_call" | custom-call | tf_op jit(solution)/shard_map/finish/pallas_call | solution.py:530

commit v9 on v8

--- a/solution.py
+++ b/solution.py
@@ -12,7 +12,7 @@
 MESH = pl.DeviceIdType.MESH
 OFFSETS = np.array([[0, 0, 0], [1, 0, 0], [0, 1, 0], [0, 0, 1], [1, 1, 0], [1, 0, 1], [0, 1, 1], [1, 1, 1], [1, 1, -1], [1, -1, 1], [-1, 1, 1], [1, -1, 0], [1, 0, -1], [0, 1, -1]], np.int32)
 LANES = 128
-GROUP = 12
+GROUP = 16
 WIDE = 256
 WIDE_GROUP = 7
 MAXCH = 32 * 16

time: 55.3 us -> 55.4 us (level)
    pallas_call x1, Pallas kernels: 16.8 us -> 18 us  [per_device(): pl.pallas_call(return_kernel, out_shape=(array((2, 2, 2, 8, LANES), F32),...]
    pallas_call x1, Pallas kernels: 11 us -> 10.1 us  [per_device(): pl.pallas_call(pair_kernel, out_shape=array((4, 4, 4, 8, LANES), F32), in...]
where the time goes in v9:
time: 55.4 us; the launch traced here: 54.6 us
  Pallas kernels  53.3 us (96%)
  between operations  1.3 us (2%)
    pallas_call x1, Pallas kernels, per_device(): pl.pallas_call(halo_kernel, out_shape=(array((4, 4, 4, 64, 256), BF16), a...  24.5 us
    pallas_call x1, Pallas kernels, per_device(): pl.pallas_call(return_kernel, out_shape=(array((2, 2, 2, 8, LANES), F32),...  18 us
    pallas_call x1, Pallas kernels, per_device(): pl.pallas_call(pair_kernel, out_shape=array((4, 4, 4, 8, LANES), F32), in...  10.1 us

profile of v9, /device:TPU:1, one launch (start us, length us, event | category | flops | bytes accessed | tf_op | source)
XLA Modules:
  0.0 54.6 jit_solution(16254419547728858271)
XLA Ops:
  1.3 24.5 %halo.1 = (bf16[4,4,4,64,256]{4,3,2,1,0:T(8,128)(2,1)S(1)}, bf16[256,256]{1,0:T(8,128)(2,1)S(1)}, bf16[32,96,64]{2,1,0:T(8,128)(2,1)S(1)}, bf16[32,32,64]{2,1,0:...) custom-call(f32[2,2,3,2,64]{4,3,2,1,0:T(2,128)} %bitcast.8, ...), custom_call_target="tpu_custom_call" | custom-call | tf_op jit(solution)/shard_map/halo/pallas_call | solution.py:465
  25.8 10.1 %pairs.1.fsum = f32[4,4,4,8,128]{4,3,2,1,0:T(8,128)S(1)} custom-call(s32[2,32]{1,0:T(2,128)S(1)} %get-tuple-element.21.plan, s32[1]{0:T(128)S(6)} %copy.14.cnt, s32[32]{0:T(128)S(1)} %get-tuple-element.22.tot, bf16[64,64,256]{2,1,0:T(8,128)(2,1)S(1)} %bitcast.7, bf16[32,96,64]{2,1,0:T(8,128)(2,1)S(1)} %get-tuple-element.24.g1, ...), custom_call_target="tpu_custom_call" | custom-call | tf_op jit(solution)/shard_map/pairs/pallas_call | solution.py:502
  35.9 18.0 %give_back.1 = (f32[2,2,2,8,128]{4,3,2,1,0:T(8,128)S(1)}, f32[32,128]{1,0:T(8,128)S(1)}, bf16[256,256]{1,0:T(8,128)(2,1)S(1)}) custom-call(f32[4,4,4,8,128]{4,3,2,1,0:T(8,128)S(1)} %pairs.1.fsum, f32[2,2,3,2,64]{4,3,2,1,0:T(2,128)} %bitcast.9, f32[2,2,3,2,64]{4,3,2,1,0:T(2,128)} %bitcast.10, bf16[256,256]{1,0:T(8,128)(2,1)S(1)} %get-tuple-element.31.held, ...), custom_call_target="tpu_custom_call" | custom-call | tf_op jit(solution)/shard_map/give_back/pallas_call | solution.py:518
  53.9 0.7 %finish.1 = (f32[2,2,3,2,64]{4,3,2,1,0:T(2,128)}, f32[6,2,128]{2,1,0:T(2,128)}, bf16[128,2,256]{2,1,0:T(2,128)(2,1)}) custom-call(f32[2,2,2,8,128]{4,3,2,1,0:T(8,128)S(1)} %get-tuple-element.33.forces, f32[32,128]{1,0:T(8,128)S(1)} %get-tuple-element.34.moved, bf16[256,256]{1,0:T(8,128)(2,1)S(1)} %get-tuple-element.35.embeds), custom_call_target="tpu_custom_call" | custom-call | tf_op jit(solution)/shard_map/finish/pallas_call | solution.py:530
